TPU v7x, 32 devices: a whole 2x2x4 slice. The times are simulated.
32 devices in a mesh: slab: 8 (over z, y), sub: 4 (over x, core).
Axes of the slice: x: 2, y: 2, z: 4, core: 2. Of those that a mesh axis runs over, the one named last changes fastest.
Arguments:
- right_sides: bfloat16 [65536, 768], P(('slab', 'sub')), may hold values from -6 to 6
- front_sides: bfloat16 [16384, 768], P(('slab', 'sub')), may hold values from -6 to 6
- pending_front: bfloat16 [16384, 256], P(('slab', 'sub')), may hold values from -6 to 6
- inner_index: int32 [512, 6], P(('slab', 'sub')), may hold values from 0 to 15, all different within a row
- inner_blocks: bfloat16 [512, 6, 128, 128], P(('slab', 'sub')), may hold values from -0.15625 to 0.15625
- inner_inverse: bfloat16 [512, 128, 128], P(('slab', 'sub')), may hold values from -1 to 2
- outer_index: int32 [128, 8], P(('slab', 'sub')), may hold values from 0 to 15, all different within a row
- outer_blocks: bfloat16 [128, 8, 128, 128], P(('slab', 'sub')), may hold values from -0.125 to 0.125
- front_inverse: bfloat16 [128, 128, 128], P(('slab', 'sub')), may hold values from -1 to 2
Outputs:
- solution: bfloat16 [65536, 768], P(('slab', 'sub'))
- front_solution: bfloat16 [16384, 768], P(('slab', 'sub'))
All inputs are finite; a program needn't handle non-finite values.
Results may differ from a plain program's by a relative error of at most 0.009.
Values may be sent and summed in bfloat16 or wider, within the bound.
No kernel may reach another device: no remote copies, remote signals or barrier semaphores. Data moves between devices by JAX's collectives and lax.ppermute only.
A program may use at most 64 MiB of HBM per device.

v0:
```python
import jax
import jax.numpy as jnp
from jax import lax
from jax.sharding import PartitionSpec as P


def passed_along(x, axis, by):
    size = lax.axis_size(axis)
    pairs = [(i, i + by) for i in range(size) if 0 <= i + by < size]
    return lax.ppermute(x, axis, pairs)


def shards(
    right_sides,
    front_sides,
    pending_front,
    inner_index,
    inner_blocks,
    inner_inverse,
    outer_index,
    outer_blocks,
    front_inverse,
):
    block_size = inner_inverse.shape[1]
    inner_rows = inner_inverse.shape[0]
    outer_rows = front_inverse.shape[0]
    columns = pending_front.shape[1]
    groups = right_sides.shape[1] // columns
    arrived = pending_front
    solved_list = []
    front_list = []
    for group in range(groups):
        gathered = lax.all_gather(arrived, "sub", axis=0, tiled=True)
        front_blocks = gathered.reshape(-1, block_size, columns)
        picked = jnp.take(front_blocks, inner_index, axis=0)
        coupled = jnp.einsum(
            "ikab,ikbc->iac", inner_blocks, picked, preferred_element_type=jnp.float32
        )
        group_sides = right_sides[:, group * columns : (group + 1) * columns].reshape(
            inner_rows, block_size, columns
        )
        inner_values = (group_sides.astype(jnp.float32) - coupled).astype(jnp.bfloat16)
        solved = jnp.einsum(
            "iab,ibc->iac", inner_inverse, inner_values, preferred_element_type=jnp.float32
        ).astype(jnp.bfloat16)
        chosen = jnp.take(solved, outer_index, axis=0)
        outgoing = jnp.einsum(
            "jkab,jkbc->jac", outer_blocks, chosen, preferred_element_type=jnp.float32
        )
        outer_sides = front_sides[:, group * columns : (group + 1) * columns].reshape(
            outer_rows, block_size, columns
        )
        outer_values = (outer_sides.astype(jnp.float32) - outgoing).astype(jnp.bfloat16)
        front_done = jnp.einsum(
            "jab,jbc->jac", front_inverse, outer_values, preferred_element_type=jnp.float32
        ).astype(jnp.bfloat16)
        front_done = front_done.reshape(-1, columns)
        solved_list.append(solved.reshape(-1, columns))
        front_list.append(front_done)
        if group + 1 < groups:
            arrived = passed_along(front_done, "slab", 1)
    solution = jnp.concatenate(solved_list, axis=1)
    front_solution = jnp.concatenate(front_list, axis=1)
    return (solution, front_solution)


def solution(mesh):
    placed = (
        P(("slab", "sub"), None),
        P(("slab", "sub"), None),
        P(("slab", "sub"), None),
        P(("slab", "sub"), None),
        P(("slab", "sub"), None, None, None),
        P(("slab", "sub"), None, None),
        P(("slab", "sub"), None),
        P(("slab", "sub"), None, None, None),
        P(("slab", "sub"), None, None),
    )
    return jax.shard_map(
        shards,
        mesh=mesh,
        in_specs=placed,
        out_specs=(P(("slab", "sub"), None), P(("slab", "sub"), None)),
        check_vma=False,
    )
```

profile of v0, /device:TPU:11, one launch (start us, length us, event | category | flops | bytes accessed | tf_op | source)
XLA Modules:
  0.0 154.8 jit_solution(6264098340672549322)
XLA Ops:
  7.2 0.0 copy-start
  7.2 0.0 all-gather.4.cloned.1.call-start
  7.2 0.7 all-gather.4.cloned.1.call-update
  7.9 0.0 all-gather.6.cloned.1.call-start
  8.0 0.8 compare_and_fusion
  8.8 0.7 compare_select_fusion.1
  9.5 0.1 copy.17
  9.6 0.1 reshape.138
  9.7 0.7 compare_select_fusion
  10.4 0.1 copy.18
  10.5 0.1 reshape.134
  10.6 0.7 compare_and_fusion.1
  11.3 2.0 %fusion.115 = (bf16[512,256]{1,0:T(8,128)(2,1)}, bf16[512,256]{1,0:T(8,128)(2,1)S(1)}, bf16[512,256]{1,0:T(8,128)(2,1)}) fusion(bf16[512,768]{1,0:T(8,128)(2,1)} %param.14), kind=kLoop, calls=%fused_computation.75 | loop fusion | bytes 1572864 | tf_op jit(solution)/shard_map/slice | solution.py:50
  13.2 3.6 %fusion.114 = (bf16[2048,256]{1,0:T(8,128)(2,1)}, bf16[2048,256]{1,0:T(8,128)(2,1)}, bf16[2048,256]{1,0:T(8,128)(2,1)}) fusion(bf16[2048,768]{1,0:T(8,128)(2,1)} %param.13), kind=kLoop, calls=%fused_computation.74 | loop fusion | bytes 6291456 | tf_op jit(solution)/shard_map/slice | solution.py:39
  16.9 10.1 %all-gather.4.cloned.1.call-done = bf16[2048,256]{1,0:T(8,128)(2,1)} async-done(((bf16[512,256]{1,0:T(8,128)(2,1)}), bf16[2048,256]{1,0:T(8,128)(2,1)}) %all-gather.4.cloned.1.call-update) | async-done | bytes 1048592 | tf_op jit(solution)/shard_map/all_gather | solution.py:33
  27.0 7.2 %gather_fusion = bf16[96,128,256]{2,1,0:T(8,128)(2,1)} fusion(bf16[16,128,256]{2,1,0:T(8,128)(2,1)} %bitcast.123, s32[1024]{0:T(1024)S(1)} %pad_clamp_fusion.1), kind=kCustom, calls=%fused_computation.clone | custom fusion | bytes 12583296 | tf_op jit(solution)/shard_map/jit(_take)/gather | solution.py:35
  34.2 0.0 copy-done
  34.2 6.0 %fusion.45 = bf16[16,256,128]{1,2,0:T(8,128)(2,1)} fusion(bf16[16,128,128]{2,1,0:T(8,128)(2,1)} %param.18, bf16[16,128,256]{2,1,0:T(8,128)(2,1)} %bitcast.140, bf16[16,6,128,128]{3,2,1,0:T(8,128)(2,1)S(1)} %copy-done, bf16[16,6,128,256]{3,2,1,0:T(8,128)(2,1)} %bitcast.133, pred[16,6]{1,0:T(8,128)(4,1)S(1)} %copy.17), kind=kOutput, calls=%fused_computation.39 | convolution fusion | flops 944766976 | bytes 12058720 | tf_op jit(solution)/shard_map/iab,ibc->iac/dot_general | solution.py:43
  40.2 0.0 copy-start.5
  40.2 3.3 %gather_fusion.1 = bf16[32,128,256]{2,1,0:T(8,128)(2,1)} fusion(bf16[16,128,256]{2,1,0:T(8,128)(2,1)} %bitcast.126, s32[1024]{0:T(1024)S(1)} %pad_clamp_fusion), kind=kCustom, calls=%fused_computation.1.clone | custom fusion | bytes 4194432 | tf_op jit(solution)/shard_map/jit(_take)/gather | solution.py:46
  43.4 0.0 copy-done.5
  43.5 3.4 %fusion.90 = bf16[4,256,128]{1,2,0:T(8,128)(2,1)} fusion(bf16[4,128,128]{2,1,0:T(8,128)(2,1)S(1)} %copy-done.5, bf16[4,8,128,128]{3,2,1,0:T(8,128)(2,1)} %param.20, bf16[4,8,128,256]{3,2,1,0:T(8,128)(2,1)} %bitcast.136, pred[4,8]{1,0:T(4,128)(4,1)S(1)} %compare_and_fusion.1, bf16[4,128,256]{2,1,0:T(8,128)(2,1)S(1)} %bitcast.147), kind=kOutput, calls=%fused_computation.54 | convolution fusion | flops 303562752 | bytes 3801120 | tf_op jit(solution)/shard_map/jab,jbc->jac/dot_general | solution.py:54
  46.9 3.1 %collective-permute-start = (bf16[512,256]{1,0:T(8,128)(2,1)}, bf16[512,256]{1,0:T(8,128)(2,1)S(1)}, u32[]{:S(2)}, u32[]{:S(2)}) collective-permute-start(bf16[512,256]{1,0:T(8,128)(2,1)} %bitcast.142), channel_id=1, source_target_pairs={{0,4},{4,8},{8,12},{12,16},{16,20},{20,24},{24,28},{1,5},{5,9},{9,... | collective-permute-start | bytes 786440 | tf_op jit(solution)/shard_map/ppermute | solution.py:10
  50.0 7.5 %collective-permute-done = bf16[512,256]{1,0:T(8,128)(2,1)S(1)} collective-permute-done((bf16[512,256]{1,0:T(8,128)(2,1)}, bf16[512,256]{1,0:T(8,128)(2,1)S(1)}, u32[]{:S(2)}, u32[]{:S(2)}) %collective-permute-start) | collective-permute-done | bytes 262176 | tf_op jit(solution)/shard_map/ppermute | solution.py:10
  57.5 0.0 copy-start.1
  57.5 0.7 copy-done.1
  58.2 0.0 all-gather.6.cloned.1.call-update
  58.2 0.0 all-gather.8.cloned.1.call-start
  58.3 16.8 %all-gather.6.cloned.1.call-done = bf16[2048,256]{1,0:T(8,128)(2,1)} async-done(((bf16[512,256]{1,0:T(8,128)(2,1)}), bf16[2048,256]{1,0:T(8,128)(2,1)}) %all-gather.6.cloned.1.call-update) | async-done | bytes 1048592 | tf_op jit(solution)/shard_map/all_gather | solution.py:33
  75.0 7.2 %gather_fusion.2 = bf16[96,128,256]{2,1,0:T(8,128)(2,1)} fusion(bf16[16,128,256]{2,1,0:T(8,128)(2,1)} %bitcast.124, s32[1024]{0:T(1024)S(1)} %pad_clamp_fusion.1), kind=kCustom, calls=%fused_computation.2.clone | custom fusion | bytes 12583296 | tf_op jit(solution)/shard_map/jit(_take)/gather | solution.py:35
  82.3 6.1 %fusion.42 = bf16[16,256,128]{1,2,0:T(8,128)(2,1)} fusion(bf16[16,128,128]{2,1,0:T(8,128)(2,1)} %param.18, bf16[16,128,256]{2,1,0:T(8,128)(2,1)} %bitcast.139, bf16[16,6,128,128]{3,2,1,0:T(8,128)(2,1)S(1)} %copy-done, bf16[16,6,128,256]{3,2,1,0:T(8,128)(2,1)} %bitcast.134, pred[16,6]{1,0:T(8,128)(4,1)S(1)} %copy.17), kind=kOutput, calls=%fused_computation.38 | convolution fusion | flops 944766976 | bytes 12058720 | tf_op jit(solution)/shard_map/iab,ibc->iac/dot_general | solution.py:43
  88.3 0.0 copy-start.4
  88.3 3.3 %gather_fusion.3 = bf16[32,128,256]{2,1,0:T(8,128)(2,1)} fusion(bf16[16,128,256]{2,1,0:T(8,128)(2,1)} %bitcast.128, s32[1024]{0:T(1024)S(1)} %pad_clamp_fusion), kind=kCustom, calls=%fused_computation.4.clone | custom fusion | bytes 4194432 | tf_op jit(solution)/shard_map/jit(_take)/gather | solution.py:46
  91.6 0.0 copy-done.4
  91.6 3.4 %fusion.87 = bf16[4,256,128]{1,2,0:T(8,128)(2,1)} fusion(bf16[4,128,128]{2,1,0:T(8,128)(2,1)S(1)} %copy-done.5, bf16[4,8,128,128]{3,2,1,0:T(8,128)(2,1)} %param.20, bf16[4,8,128,256]{3,2,1,0:T(8,128)(2,1)} %bitcast.137, pred[4,8]{1,0:T(4,128)(4,1)S(1)} %compare_and_fusion.1, bf16[4,128,256]{2,1,0:T(8,128)(2,1)S(1)} %bitcast.144), kind=kOutput, calls=%fused_computation.53 | convolution fusion | flops 303562752 | bytes 3801120 | tf_op jit(solution)/shard_map/jab,jbc->jac/dot_general | solution.py:54
  95.0 3.3 %collective-permute-start.1 = (bf16[512,256]{1,0:T(8,128)(2,1)}, bf16[512,256]{1,0:T(8,128)(2,1)S(1)}, u32[]{:S(2)}, u32[]{:S(2)}) collective-permute-start(bf16[512,256]{1,0:T(8,128)(2,1)} %bitcast.145), channel_id=1, source_target_pairs={{0,4},{4,8},{8,12},{12,16},{16,20},{20,24},{24,28},{1,5},{5,9},{9,... | collective-permute-start | bytes 786440 | tf_op jit(solution)/shard_map/ppermute | solution.py:10
  98.3 7.3 %collective-permute-done.1 = bf16[512,256]{1,0:T(8,128)(2,1)S(1)} collective-permute-done((bf16[512,256]{1,0:T(8,128)(2,1)}, bf16[512,256]{1,0:T(8,128)(2,1)S(1)}, u32[]{:S(2)}, u32[]{:S(2)}) %collective-permute-start.1) | collective-permute-done | bytes 262176 | tf_op jit(solution)/shard_map/ppermute | solution.py:10
  105.6 0.0 copy-start.2
  105.6 0.7 copy-done.2
  106.3 0.0 all-gather.8.cloned.1.call-update
  106.4 16.8 %all-gather.8.cloned.1.call-done = bf16[2048,256]{1,0:T(8,128)(2,1)} async-done(((bf16[512,256]{1,0:T(8,128)(2,1)}), bf16[2048,256]{1,0:T(8,128)(2,1)}) %all-gather.8.cloned.1.call-update) | async-done | bytes 1048592 | tf_op jit(solution)/shard_map/all_gather | solution.py:33
  123.2 7.2 %gather_fusion.4 = bf16[96,128,256]{2,1,0:T(8,128)(2,1)} fusion(bf16[16,128,256]{2,1,0:T(8,128)(2,1)} %bitcast.125, s32[1024]{0:T(1024)S(1)} %pad_clamp_fusion.1), kind=kCustom, calls=%fused_computation.3.clone | custom fusion | bytes 12583296 | tf_op jit(solution)/shard_map/jit(_take)/gather | solution.py:35
  130.4 6.0 %fusion.39 = bf16[16,256,128]{1,2,0:T(8,128)(2,1)} fusion(bf16[16,128,128]{2,1,0:T(8,128)(2,1)} %param.18, bf16[16,128,256]{2,1,0:T(8,128)(2,1)} %bitcast.138, bf16[16,6,128,128]{3,2,1,0:T(8,128)(2,1)S(1)} %copy-done, bf16[16,6,128,256]{3,2,1,0:T(8,128)(2,1)} %bitcast.132, pred[16,6]{1,0:T(8,128)(4,1)S(1)} %copy.17), kind=kOutput, calls=%fused_computation.37 | convolution fusion | flops 944766976 | bytes 12058720 | tf_op jit(solution)/shard_map/iab,ibc->iac/dot_general | solution.py:43
  136.4 3.3 %gather_fusion.5 = bf16[32,128,256]{2,1,0:T(8,128)(2,1)} fusion(bf16[16,128,256]{2,1,0:T(8,128)(2,1)} %bitcast.130, s32[1024]{0:T(1024)S(1)} %pad_clamp_fusion), kind=kCustom, calls=%fused_computation.5.clone | custom fusion | bytes 4194432 | tf_op jit(solution)/shard_map/jit(_take)/gather | solution.py:46
  139.7 0.0 copy-done.3
  139.7 3.4 %fusion.84 = bf16[4,256,128]{1,2,0:T(8,128)(2,1)} fusion(bf16[4,128,128]{2,1,0:T(8,128)(2,1)S(1)} %copy-done.5, bf16[4,8,128,128]{3,2,1,0:T(8,128)(2,1)} %param.20, bf16[4,8,128,256]{3,2,1,0:T(8,128)(2,1)} %bitcast.135, pred[4,8]{1,0:T(4,128)(4,1)S(1)} %compare_and_fusion.1, bf16[4,128,256]{2,1,0:T(8,128)(2,1)S(1)} %bitcast.141), kind=kOutput, calls=%fused_computation.52 | convolution fusion | flops 303562752 | bytes 3801120 | tf_op jit(solution)/shard_map/jab,jbc->jac/dot_general | solution.py:54
  143.1 2.0 %pad_maximum_fusion.1 = bf16[512,768]{1,0:T(8,128)(2,1)} fusion(bf16[512,256]{1,0:T(8,128)(2,1)} %bitcast.148, bf16[512,256]{1,0:T(8,128)(2,1)} %bitcast.146, bf16[512,256]{1,0:T(8,128)(2,1)} %bitcast.143), kind=kLoop, calls=%fused_computation.58 | loop fusion | flops 2359296 | bytes 1572864 | tf_op jit(solution)/shard_map/concatenate | solution.py:63
  145.1 3.1 %pad_maximum_fusion = bf16[2048,768]{1,0:T(8,128)(2,1)} fusion(bf16[2048,256]{1,0:T(8,128)(2,1)} %bitcast.131, bf16[2048,256]{1,0:T(8,128)(2,1)} %bitcast.129, bf16[2048,256]{1,0:T(8,128)(2,1)} %bitcast.127), kind=kLoop, calls=%fused_computation.15 | loop fusion | flops 9437184 | bytes 6291456 | tf_op jit(solution)/shard_map/concatenate | solution.py:62
  (3 shorter events, 0.0 us)
Async XLA Ops:
  7.2 27.0 %copy-start = (bf16[16,6,128,128]{3,2,1,0:T(8,128)(2,1)S(1)}, bf16[16,6,128,128]{3,2,1,0:T(8,128)(2,1)}, u32[]{:S(2)}) copy-start(bf16[16,6,128,128]{3,2,1,0:T(8,128)(2,1)} %param.17) | copy-start | bytes 9437188
  7.2 19.8 %all-gather.4.cloned.1.call-start = ((), (), s32[]{:S(2)}) async-start(), calls=%async_computation | async-start | bytes 1310720 | tf_op jit(solution)/shard_map/all_gather | solution.py:33
  7.9 67.1 %all-gather.6.cloned.1.call-start = ((), (), s32[]{:S(2)}) async-start(), calls=%async_computation.1 | async-start | bytes 1310720 | tf_op jit(solution)/shard_map/all_gather | solution.py:33
  40.2 3.3 %copy-start.5 = (bf16[4,128,128]{2,1,0:T(8,128)(2,1)S(1)}, bf16[4,128,128]{2,1,0:T(8,128)(2,1)}, u32[]{:S(2)}) copy-start(bf16[4,128,128]{2,1,0:T(8,128)(2,1)} %param.21) | copy-start | bytes 393220
  46.9 10.6 %collective-permute-start = (bf16[512,256]{1,0:T(8,128)(2,1)}, bf16[512,256]{1,0:T(8,128)(2,1)S(1)}, u32[]{:S(2)}, u32[]{:S(2)}) collective-permute-start(bf16[512,256]{1,0:T(8,128)(2,1)} %bitcast.142), channel_id=1, source_target_pairs={{0,4},{4,8},{8,12},{12,16},{16,20},{20,24},{24,28},{1,5},{5,9},{9,... | collective-permute-start | bytes 786440 | tf_op jit(solution)/shard_map/ppermute | solution.py:10
  57.5 0.7 copy-start.1
  58.2 64.9 %all-gather.8.cloned.1.call-start = ((), (), s32[]{:S(2)}) async-start(), calls=%async_computation.2 | async-start | bytes 1310720 | tf_op jit(solution)/shard_map/all_gather | solution.py:33
  88.3 3.3 %copy-start.4 = (bf16[512,256]{1,0:T(8,128)(2,1)S(1)}, bf16[512,256]{1,0:T(8,128)(2,1)}, u32[]{:S(2)}) copy-start(bf16[512,256]{1,0:T(8,128)(2,1)} %get-tuple-element.9) | copy-start | bytes 786436
  95.0 10.6 %collective-permute-start.1 = (bf16[512,256]{1,0:T(8,128)(2,1)}, bf16[512,256]{1,0:T(8,128)(2,1)S(1)}, u32[]{:S(2)}, u32[]{:S(2)}) collective-permute-start(bf16[512,256]{1,0:T(8,128)(2,1)} %bitcast.145), channel_id=1, source_target_pairs={{0,4},{4,8},{8,12},{12,16},{16,20},{20,24},{24,28},{1,5},{5,9},{9,... | collective-permute-start | bytes 786440 | tf_op jit(solution)/shard_map/ppermute | solution.py:10
  105.6 0.7 copy-start.2
  136.4 3.3 %copy-start.3 = (bf16[512,256]{1,0:T(8,128)(2,1)S(1)}, bf16[512,256]{1,0:T(8,128)(2,1)}, u32[]{:S(2)}) copy-start(bf16[512,256]{1,0:T(8,128)(2,1)} %get-tuple-element.7) | copy-start | bytes 786436
Sparse Core Ops, SparseCore 0:
  9.6 17.3 all-gather.3
  58.3 16.6 all-gather.5
  106.5 16.6 all-gather.7
where the time goes:
time: 157 us; the launch traced here: 155 us
  waiting for transfers between devices  59.2 us (38%)
  local copies, waits for them, and re-layouts  38.9 us (25%)
  matrix products  28.3 us (18%)
  between operations  13.8 us (9%)
  other arithmetic  8.08 us (5%)
  starting transfers between devices  6.47 us (4%)
    all_gather x3, waiting for transfers between devices, shards(): gathered = lax.all_gather(arrived, 'sub', axis=0, tiled=True)  43.6 us
    gather x3, local copies, waits for them, and re-layouts, shards(): picked = jnp.take(front_blocks, inner_index, axis=0)  21.7 us
    dot_general x3, matrix products, shards(): jnp.einsum('iab,ibc->iac', inner_inverse, inner_values, preferred_element...  18.1 us
    ppermute x2, waiting for transfers between devices, passed_along(): return lax.ppermute(x, axis, pairs)  14.9 us
    dot_general x3, matrix products, shards(): jnp.einsum('jab,jbc->jac', front_inverse, outer_values, preferred_element...  10.2 us
    gather x3, local copies, waits for them, and re-layouts, shards(): chosen = jnp.take(solved, outer_index, axis=0)  9.79 us
    ppermute x2, starting transfers between devices, passed_along(): return lax.ppermute(x, axis, pairs)  6.35 us
    slice x1, local copies, waits for them, and re-layouts, shards(): right_sides[:, group * columns:(group + 1) * columns]  3.63 us
  transfers between devices with their start and end apart: 5, of which 5 were waited for; matrix products, arithmetic and copies ran while one was open for 6% of the time, Pallas kernels for 0%

commit v1 on v0

v1 whole, which is shorter than its diff:
```python
import functools

import jax
import jax.numpy as jnp
from jax import lax
from jax.experimental import pallas as pl
from jax.experimental.pallas import tpu as pltpu
from jax.sharding import PartitionSpec as P

AXES = ("slab", "sub")
VMEM = pltpu.VMEM
MIB = 1 << 20


def permuted(x, slabs, subs, by, flip):
    pairs = [
        (s * subs + q, (s + by) * subs + (q ^ flip))
        for s in range(slabs)
        for q in range(subs)
        if 0 <= s + by < slabs
    ]
    return lax.ppermute(x, AXES, pairs)


def gathered(share, slabs, subs):
    shares = {0: share}
    bit = subs // 2
    while bit:
        for r in list(shares):
            shares[r ^ bit] = permuted(shares[r], slabs, subs, 0, bit)
        bit //= 2
    return [shares[r] for r in range(subs)]


def in_vmem(x):
    return pltpu.with_memory_space_constraint(x, VMEM)


def stage_kernel(count, *refs):
    ins, outs, sems = refs[:count], refs[count : 2 * count], refs[2 * count]
    copies = [
        pltpu.make_async_copy(a, b, sems.at[n])
        for n, (a, b) in enumerate(zip(ins, outs))
    ]
    for c in copies:
        c.start()
    for c in copies:
        c.wait()


def staged(*arrays):
    n = len(arrays)
    size = sum(a.size * a.dtype.itemsize for a in arrays)
    return pl.pallas_call(
        functools.partial(stage_kernel, n),
        out_shape=tuple(VMEM(a.shape, a.dtype) for a in arrays),
        in_specs=[pl.BlockSpec(memory_space=pl.ANY)] * n,
        out_specs=tuple(pl.BlockSpec(memory_space=VMEM) for _ in arrays),
        scratch_shapes=[pltpu.SemaphoreType.DMA((n,))],
        compiler_params=pltpu.CompilerParams(vmem_limit_bytes=2 * MIB),
        cost_estimate=pl.CostEstimate(
            flops=0, bytes_accessed=2 * size, transcendentals=0
        ),
        name="stage",
    )(*[pltpu.with_memory_space_constraint(a, pltpu.HBM) for a in arrays])


def dot(a, b):
    return jnp.dot(a, b, preferred_element_type=jnp.float32)


def part_kernel(subs, width, column, step, aliased, *refs):
    shares, refs = refs[:subs], refs[subs:]
    (in_idx, out_idx, in_blocks, in_inv, out_blocks, out_inv, sides, fronts), refs = (
        refs[:8],
        refs[8:],
    )
    if aliased:
        refs = refs[2:]
    sol_hbm, fsol_hbm, f_ref, inc, sol, sem, fsem = refs
    rows_in, links = in_idx.shape
    rows_out, out_links = out_idx.shape
    size = in_inv.shape[1]
    share = shares[0].shape[0]
    swap = lax.axis_index("sub") * (share // size)
    cols = pl.ds(column * width, width)
    for r, ref in enumerate(shares):
        inc[pl.ds(r * share, share), :] = ref[...]

    def rows_of(ref, block):
        return ref[pl.ds(pl.multiple_of(block * size, size), size), :]

    def out_copy(g):
        rows = pl.ds(pl.multiple_of(g * step * size, size), step * size)
        return pltpu.make_async_copy(
            sol.at[rows, :], sol_hbm.at[rows, cols], sem.at[g]
        )

    def inner(g, _):
        for r in range(step):
            i = g * step + r
            picked = [rows_of(inc, in_idx[i, k] ^ swap) for k in range(links)]
            lhs = jnp.concatenate([in_blocks[i, k] for k in range(links)], axis=1)
            coupled = dot(lhs, jnp.concatenate(picked, axis=0))
            at = pl.ds(pl.multiple_of(i * size, size), size)
            value = (sides[at, cols].astype(jnp.float32) - coupled).astype(jnp.bfloat16)
            sol[at, :] = dot(in_inv[i], value).astype(jnp.bfloat16)
        out_copy(g).start()
        return 0

    lax.fori_loop(0, rows_in // step, inner, 0)
    for j in range(rows_out):
        chosen = [rows_of(sol, out_idx[j, k]) for k in range(out_links)]
        lhs = jnp.concatenate([out_blocks[j, k] for k in range(out_links)], axis=1)
        outgoing = dot(lhs, jnp.concatenate(chosen, axis=0))
        at = pl.ds(j * size, size)
        value = (fronts[at, cols].astype(jnp.float32) - outgoing).astype(jnp.bfloat16)
        f_ref[at, :] = dot(out_inv[j], value).astype(jnp.bfloat16)
    last = pltpu.make_async_copy(f_ref, fsol_hbm.at[:, cols], fsem)
    last.start()
    for g in range(rows_in // step):
        out_copy(g).wait()
    last.wait()


def part(shares, in_idx, out_idx, weights, sides, fronts, outs, column, width):
    subs = len(shares)
    rows, front_rows = sides.shape[0], fronts.shape[0]
    rows_in, links, size, _ = weights[0].shape
    rows_out, out_links = out_idx.shape
    step = next(s for s in (4, 2, 1) if rows_in % s == 0)
    blocks = rows_in * (links + 1) + rows_out * (out_links + 1)
    smem = pl.BlockSpec(memory_space=pltpu.SMEM)
    vmem = pl.BlockSpec(memory_space=VMEM)
    hbm = pl.BlockSpec(memory_space=pl.ANY)
    aliased = outs is not None
    operands = (
        [in_vmem(s) for s in shares]
        + [in_idx, out_idx]
        + [in_vmem(w) for w in weights]
        + [in_vmem(sides), in_vmem(fronts)]
        + (list(outs) if aliased else [])
    )
    n = len(operands)
    return pl.pallas_call(
        functools.partial(part_kernel, subs, width, column, step, aliased),
        out_shape=(
            pltpu.HBM(sides.shape, sides.dtype),
            pltpu.HBM(fronts.shape, fronts.dtype),
            VMEM((front_rows, width), fronts.dtype),
        ),
        in_specs=[vmem] * subs + [smem] * 2 + [vmem] * 6 + [hbm] * (2 * aliased),
        out_specs=(hbm, hbm, vmem),
        scratch_shapes=[
            VMEM((subs * shares[0].shape[0], width), sides.dtype),
            VMEM((rows, width), sides.dtype),
            pltpu.SemaphoreType.DMA((rows_in // step,)),
            pltpu.SemaphoreType.DMA,
        ],
        input_output_aliases={n - 2: 0, n - 1: 1} if aliased else {},
        compiler_params=pltpu.CompilerParams(vmem_limit_bytes=8 * MIB),
        cost_estimate=pl.CostEstimate(
            flops=2 * blocks * size * size * width,
            bytes_accessed=(blocks * size * size + 2 * rows * width) * 2,
            transcendentals=0,
        ),
        name=f"part_{column}",
    )(*operands)


def shards(
    right_sides,
    front_sides,
    pending_front,
    inner_index,
    inner_blocks,
    inner_inverse,
    outer_index,
    outer_blocks,
    front_inverse,
):
    slabs, subs = lax.axis_size("slab"), lax.axis_size("sub")
    columns = pending_front.shape[1]
    groups = right_sides.shape[1] // columns
    halves = 2 if columns % 256 == 0 else 1
    width = columns // halves
    arrived = [
        gathered(pending_front[:, h * width : (h + 1) * width], slabs, subs)
        for h in range(halves)
    ]
    *weights, sides, fronts = staged(
        inner_blocks,
        inner_inverse,
        outer_blocks,
        front_inverse,
        right_sides,
        front_sides,
    )
    outs = None
    for group in range(groups):
        for h in range(halves):
            *outs, front = part(
                arrived[h],
                inner_index,
                outer_index,
                weights,
                sides,
                fronts,
                outs,
                group * halves + h,
                width,
            )
            if group + 1 < groups:
                hop = permuted(front, slabs, subs, 1, 0)
                arrived[h] = gathered(hop, slabs, subs)
    return tuple(outs)


def solution(mesh):
    rows = P(("slab", "sub"), None)
    blocks = P(("slab", "sub"), None, None)
    links = P(("slab", "sub"), None, None, None)
    return jax.shard_map(
        shards,
        mesh=mesh,
        in_specs=(rows, rows, rows, rows, links, blocks, rows, links, blocks),
        out_specs=(rows, rows),
        check_vma=False,
    )
```

time: 157 us -> 87.2 us (0.56); the launches traced: 155 us -> 86.9 us
  waiting for transfers between devices: 59.2 us -> 12.2 us
  Pallas kernels: 0 us -> 42.8 us
  local copies, waits for them, and re-layouts: 38.9 us -> 1.75 us
  matrix products: 28.3 us -> 0 us
  starting transfers between devices: 6.47 us -> 29.4 us
  between operations: 13.8 us -> 0.82 us
  other arithmetic: 8.08 us -> 0 us
    all_gather x3 -> x0, waiting for transfers between devices: 43.6 us -> none  [shards(): gathered = lax.all_gather(arrived, 'sub', axis=0, tiled=True)]
    pallas_call x0 -> x7, Pallas kernels: none -> 42.8 us  [the longest x6 39.3 us: part(): pl.pallas_call(functools.partial(part_kernel, subs, width, column, step,...]
    gather x6 -> x0, local copies, waits for them, and re-layouts: 31.5 us -> none  [the longest x3 21.7 us: shards(): picked = jnp.take(front_blocks, inner_index, axis=0)]
    dot_general x6 -> x0, matrix products: 28.3 us -> none  [the longest x3 18.1 us: shards(): jnp.einsum('iab,ibc->iac', inner_inverse, inner_values, preferred_element...]
    ppermute x2 -> x22, starting transfers between devices: 6.35 us -> 29.4 us  [permuted(): return lax.ppermute(x, AXES, pairs)]
    concatenate x2 -> x0, other arithmetic: 5.16 us -> none  [the longest x1 3.12 us: shards(): solution = jnp.concatenate(solved_list, axis=1)]
    slice x2 -> x1, local copies, waits for them, and re-layouts: 5.61 us -> 0.99 us  [shards(): pending_front[:, h * width:(h + 1) * width]]
    ppermute x2 -> x22, waiting for transfers between devices: 14.9 us -> 12.2 us  [permuted(): return lax.ppermute(x, AXES, pairs)]
  transfers between devices with their start and end apart: 5 -> 22, of which waited for: 5 -> 6; matrix products, arithmetic and copies ran while one was open for 6% -> 1% of each run, Pallas kernels for 0% -> 41%
where the time goes in v1:
time: 87.2 us; the launch traced here: 86.9 us
  Pallas kernels  42.8 us (49%)
  starting transfers between devices  29.4 us (34%)
  waiting for transfers between devices  12.2 us (14%)
  local copies, waits for them, and re-layouts  1.75 us (2%)
    pallas_call x6, Pallas kernels, part(): pl.pallas_call(functools.partial(part_kernel, subs, width, column, step,...  39.3 us
    ppermute x22, starting transfers between devices, permuted(): return lax.ppermute(x, AXES, pairs)  29.4 us
    ppermute x22, waiting for transfers between devices, permuted(): return lax.ppermute(x, AXES, pairs)  12.2 us
    pallas_call x1, Pallas kernels, staged(): pl.pallas_call(functools.partial(stage_kernel, n), out_shape=tuple((VMEM(...  3.55 us
  transfers between devices with their start and end apart: 22, of which 6 were waited for; matrix products, arithmetic and copies ran while one was open for 1% of the time, Pallas kernels for 41%

profile of v1, /device:TPU:11, one launch (start us, length us, event | category | flops | bytes accessed | tf_op | source)
XLA Modules:
  0.0 86.9 jit_solution(17240686989016810540)
XLA Ops:
  0.6 1.0 %fusion = (bf16[512,128]{1,0:T(8,128)(2,1)S(1)}, bf16[512,128]{1,0:T(8,128)(2,1)S(1)}) fusion(bf16[512,256]{1,0:T(8,128)(2,1)} %param.11), kind=kLoop, calls=%fused_computation | loop fusion | bytes 524288 | tf_op jit(solution)/shard_map/slice | solution.py:188
  1.6 0.3 collective-permute-start.4
  1.9 1.2 %collective-permute-start.1 = (bf16[512,128]{1,0:T(8,128)(2,1)S(1)}, bf16[512,128]{1,0:T(8,128)(2,1)S(1)}, u32[]{:S(2)}, u32[]{:S(2)}) collective-permute-start(bf16[512,128]{1,0:T(8,128)(2,1)S(1)} %get-tuple-element.47.refs_0_), channel_id=1, source_target_pairs={{0,2},{1,3},{2,0},{3,1},{4,6},{5,7},{6,4},{7,5},{8,10},{9,11},{10,... | collective-permute-start | bytes 393224 | tf_op jit(solution)/shard_map/ppermute | solution.py:22
  3.2 1.2 %collective-permute-start.3 = (bf16[512,128]{1,0:T(8,128)(2,1)S(1)}, bf16[512,128]{1,0:T(8,128)(2,1)S(1)}, u32[]{:S(2)}, u32[]{:S(2)}) collective-permute-start(bf16[512,128]{1,0:T(8,128)(2,1)S(1)} %get-tuple-element.46.refs_0_), channel_id=1, source_target_pairs={{0,1},{1,0},{2,3},{3,2},{4,5},{5,4},{6,7},{7,6},{8,9},{9,8},{10,11... | collective-permute-start | bytes 393224 | tf_op jit(solution)/shard_map/ppermute | solution.py:22
  4.4 1.7 %collective-permute-done.4.refs_2_ = bf16[512,128]{1,0:T(8,128)(2,1)S(1)} collective-permute-done((bf16[512,128]{1,0:T(8,128)(2,1)S(1)}, bf16[512,128]{1,0:T(8,128)(2,1)S(1)}, u32[]{:S(2)}, u32[]{:S(2)}) %collective-permute-start.4) | collective-permute-done | bytes 131104 | tf_op jit(solution)/shard_map/ppermute | solution.py:22
  6.1 2.7 %collective-permute-start.5 = (bf16[512,128]{1,0:T(8,128)(2,1)S(1)}, bf16[512,128]{1,0:T(8,128)(2,1)S(1)}, u32[]{:S(2)}, u32[]{:S(2)}) collective-permute-start(bf16[512,128]{1,0:T(8,128)(2,1)S(1)} %collective-permute-done.4.refs_2_), channel_id=1, source_target_pairs={{0,1},{1,0},{2,3},{3,2},{4,5},{5,4},{6,7},{7,6},{8,9},{9,8},{10,11... | collective-permute-start | bytes 393224 | tf_op jit(solution)/shard_map/ppermute | solution.py:22
  8.7 0.0 collective-permute-start
  8.7 0.1 collective-permute-done.1.refs_2_
  8.9 1.5 %collective-permute-start.2 = (bf16[512,128]{1,0:T(8,128)(2,1)S(1)}, bf16[512,128]{1,0:T(8,128)(2,1)S(1)}, u32[]{:S(2)}, u32[]{:S(2)}) collective-permute-start(bf16[512,128]{1,0:T(8,128)(2,1)S(1)} %collective-permute-done.1.refs_2_), channel_id=1, source_target_pairs={{0,1},{1,0},{2,3},{3,2},{4,5},{5,4},{6,7},{7,6},{8,9},{9,8},{10,11... | collective-permute-start | bytes 393224 | tf_op jit(solution)/shard_map/ppermute | solution.py:22
  10.4 0.8 copy.22.refs_4_
  11.2 3.6 %stage.1 = (bf16[16,6,128,128]{3,2,1,0:T(8,128)(2,1)S(1)}, bf16[16,128,128]{2,1,0:T(8,128)(2,1)S(1)}, bf16[4,8,128,128]{3,2,1,0:T(8,128)(2,1)S(1)}, bf16[4,128,1...) custom-call(bf16[16,6,128,128]{3,2,1,0:T(8,128)(2,1)} %refs_0_.1, ...), custom_call_target="tpu_custom_call" | custom-call | bytes 17563648 | tf_op jit(solution)/shard_map/stage/pallas_call | solution.py:54
  14.7 0.0 collective-permute-done.3.refs_1_
  14.7 0.0 collective-permute-done.5.refs_3_
  14.8 6.3 %part_0.1 = (bf16[2048,768]{1,0:T(8,128)(2,1)}, bf16[512,768]{1,0:T(8,128)(2,1)}, bf16[512,128]{1,0:T(8,128)(2,1)S(1)}) custom-call(bf16[512,128]{1,0:T(8,128)(2,1)S(1)} %get-tuple-element.46.refs_0_, bf16[512,128]{1,0:T(8,128)(2,1)S(1)} %collective-permute-done.3.refs_1_, bf16[512,128]{1,0:T(8,128)(2,1)S(1)} %collective-permute-done.4.refs_2_, ...), custom_call_target="tpu_custom_call" | custom-call | flops 620756992 | bytes 5898240 | tf_op jit(solution)/shard_map/part_0/pallas_call | solution.py:145
  21.1 3.1 %collective-permute-start.10 = (bf16[512,128]{1,0:T(8,128)(2,1)S(1)}, bf16[512,128]{1,0:T(8,128)(2,1)S(1)}, u32[]{:S(2)}, u32[]{:S(2)}) collective-permute-start(bf16[512,128]{1,0:T(8,128)(2,1)S(1)} %get-tuple-element.33), channel_id=1, source_target_pairs={{0,4},{1,5},{2,6},{3,7},{4,8},{5,9},{6,10},{7,11},{8,12},{9,13},{1... | collective-permute-start | bytes 393224 | tf_op jit(solution)/shard_map/ppermute | solution.py:22
  24.3 0.0 collective-permute-done.refs_1_
  24.3 0.0 collective-permute-done.2.refs_3_
  24.3 6.3 %part_1.1 = (bf16[2048,768]{1,0:T(8,128)(2,1)}, bf16[512,768]{1,0:T(8,128)(2,1)}, bf16[512,128]{1,0:T(8,128)(2,1)S(1)}) custom-call(bf16[512,128]{1,0:T(8,128)(2,1)S(1)} %get-tuple-element.47.refs_0_, bf16[512,128]{1,0:T(8,128)(2,1)S(1)} %collective-permute-done.refs_1_, ...), custom_call_target="tpu_custom_call", output_to_operand_aliasing={{0}: (12, {}), {1}: (13, {})} | custom-call | flops 620756992 | bytes 5898240 | tf_op jit(solution)/shard_map/part_1/pallas_call | solution.py:145
  30.6 3.1 %collective-permute-start.6 = (bf16[512,128]{1,0:T(8,128)(2,1)S(1)}, bf16[512,128]{1,0:T(8,128)(2,1)S(1)}, u32[]{:S(2)}, u32[]{:S(2)}) collective-permute-start(bf16[512,128]{1,0:T(8,128)(2,1)S(1)} %get-tuple-element.32), channel_id=1, source_target_pairs={{0,4},{1,5},{2,6},{3,7},{4,8},{5,9},{6,10},{7,11},{8,12},{9,13},{1... | collective-permute-start | bytes 393224 | tf_op jit(solution)/shard_map/ppermute | solution.py:22
  33.8 0.3 collective-permute-start.12
  34.1 4.1 %collective-permute-done.6.refs_0_ = bf16[512,128]{1,0:T(8,128)(2,1)S(1)} collective-permute-done((bf16[512,128]{1,0:T(8,128)(2,1)S(1)}, bf16[512,128]{1,0:T(8,128)(2,1)S(1)}, u32[]{:S(2)}, u32[]{:S(2)}) %collective-permute-start.6) | collective-permute-done | bytes 131104 | tf_op jit(solution)/shard_map/ppermute | solution.py:22
  38.2 0.3 collective-permute-start.8
  38.5 1.4 %collective-permute-start.11 = (bf16[512,128]{1,0:T(8,128)(2,1)S(1)}, bf16[512,128]{1,0:T(8,128)(2,1)S(1)}, u32[]{:S(2)}, u32[]{:S(2)}) collective-permute-start(bf16[512,128]{1,0:T(8,128)(2,1)S(1)} %collective-permute-done.10.refs_0_), channel_id=1, source_target_pairs={{0,1},{1,0},{2,3},{3,2},{4,5},{5,4},{6,7},{7,6},{8,9},{9,8},{10,11... | collective-permute-start | bytes 393224 | tf_op jit(solution)/shard_map/ppermute | solution.py:22
  39.9 0.0 collective-permute-start.13
  39.9 0.5 collective-permute-start.7
  40.4 1.7 %collective-permute-done.8.refs_2_ = bf16[512,128]{1,0:T(8,128)(2,1)S(1)} collective-permute-done((bf16[512,128]{1,0:T(8,128)(2,1)S(1)}, bf16[512,128]{1,0:T(8,128)(2,1)S(1)}, u32[]{:S(2)}, u32[]{:S(2)}) %collective-permute-start.8) | collective-permute-done | bytes 131104 | tf_op jit(solution)/shard_map/ppermute | solution.py:22
  42.0 2.3 %collective-permute-start.9 = (bf16[512,128]{1,0:T(8,128)(2,1)S(1)}, bf16[512,128]{1,0:T(8,128)(2,1)S(1)}, u32[]{:S(2)}, u32[]{:S(2)}) collective-permute-start(bf16[512,128]{1,0:T(8,128)(2,1)S(1)} %collective-permute-done.8.refs_2_), channel_id=1, source_target_pairs={{0,1},{1,0},{2,3},{3,2},{4,5},{5,4},{6,7},{7,6},{8,9},{9,8},{10,11... | collective-permute-start | bytes 393224 | tf_op jit(solution)/shard_map/ppermute | solution.py:22
  44.3 0.0 collective-permute-done.11.refs_1_
  44.3 0.0 collective-permute-done.13.refs_3_
  44.3 6.3 %part_2.1 = (bf16[2048,768]{1,0:T(8,128)(2,1)}, bf16[512,768]{1,0:T(8,128)(2,1)}, bf16[512,128]{1,0:T(8,128)(2,1)S(1)}) custom-call(bf16[512,128]{1,0:T(8,128)(2,1)S(1)} %collective-permute-done.10.refs_0_, bf16[512,128]{1,0:T(8,128)(2,1)S(1)} %collective-permute-done.11.refs_1_, ...), custom_call_target="tpu_custom_call", output_to_operand_aliasing={{0}: (12, {}), {1}: (13, {})} | custom-call | flops 620756992 | bytes 5898240 | tf_op jit(solution)/shard_map/part_2/pallas_call | solution.py:145
  50.6 2.2 %collective-permute-start.18 = (bf16[512,128]{1,0:T(8,128)(2,1)S(1)}, bf16[512,128]{1,0:T(8,128)(2,1)S(1)}, u32[]{:S(2)}, u32[]{:S(2)}) collective-permute-start(bf16[512,128]{1,0:T(8,128)(2,1)S(1)} %get-tuple-element.39), channel_id=1, source_target_pairs={{0,4},{1,5},{2,6},{3,7},{4,8},{5,9},{6,10},{7,11},{8,12},{9,13},{1... | collective-permute-start | bytes 393224 | tf_op jit(solution)/shard_map/ppermute | solution.py:22
  52.9 0.0 collective-permute-done.7.refs_1_
  52.9 6.3 %part_3.1 = (bf16[2048,768]{1,0:T(8,128)(2,1)}, bf16[512,768]{1,0:T(8,128)(2,1)}, bf16[512,128]{1,0:T(8,128)(2,1)S(1)}) custom-call(bf16[512,128]{1,0:T(8,128)(2,1)S(1)} %collective-permute-done.6.refs_0_, bf16[512,128]{1,0:T(8,128)(2,1)S(1)} %collective-permute-done.7.refs_1_, ...), custom_call_target="tpu_custom_call", output_to_operand_aliasing={{0}: (12, {}), {1}: (13, {})} | custom-call | flops 620756992 | bytes 5898240 | tf_op jit(solution)/shard_map/part_3/pallas_call | solution.py:145
  59.2 4.1 %collective-permute-start.14 = (bf16[512,128]{1,0:T(8,128)(2,1)S(1)}, bf16[512,128]{1,0:T(8,128)(2,1)S(1)}, u32[]{:S(2)}, u32[]{:S(2)}) collective-permute-start(bf16[512,128]{1,0:T(8,128)(2,1)S(1)} %get-tuple-element.38), channel_id=1, source_target_pairs={{0,4},{1,5},{2,6},{3,7},{4,8},{5,9},{6,10},{7,11},{8,12},{9,13},{1... | collective-permute-start | bytes 393224 | tf_op jit(solution)/shard_map/ppermute | solution.py:22
  63.3 0.3 collective-permute-start.20
  63.6 3.2 %collective-permute-done.14.refs_0_ = bf16[512,128]{1,0:T(8,128)(2,1)S(1)} collective-permute-done((bf16[512,128]{1,0:T(8,128)(2,1)S(1)}, bf16[512,128]{1,0:T(8,128)(2,1)S(1)}, u32[]{:S(2)}, u32[]{:S(2)}) %collective-permute-start.14) | collective-permute-done | bytes 131104 | tf_op jit(solution)/shard_map/ppermute | solution.py:22
  66.8 0.3 collective-permute-start.16
  67.1 1.4 %collective-permute-start.19 = (bf16[512,128]{1,0:T(8,128)(2,1)S(1)}, bf16[512,128]{1,0:T(8,128)(2,1)S(1)}, u32[]{:S(2)}, u32[]{:S(2)}) collective-permute-start(bf16[512,128]{1,0:T(8,128)(2,1)S(1)} %collective-permute-done.18.refs_0_), channel_id=1, source_target_pairs={{0,1},{1,0},{2,3},{3,2},{4,5},{5,4},{6,7},{7,6},{8,9},{9,8},{10,11... | collective-permute-start | bytes 393224 | tf_op jit(solution)/shard_map/ppermute | solution.py:22
  68.5 0.8 collective-permute-start.21
  69.3 0.0 collective-permute-start.15
  69.3 1.4 %collective-permute-done.16.refs_2_ = bf16[512,128]{1,0:T(8,128)(2,1)S(1)} collective-permute-done((bf16[512,128]{1,0:T(8,128)(2,1)S(1)}, bf16[512,128]{1,0:T(8,128)(2,1)S(1)}, u32[]{:S(2)}, u32[]{:S(2)}) %collective-permute-start.16) | collective-permute-done | bytes 131104 | tf_op jit(solution)/shard_map/ppermute | solution.py:22
  70.7 2.3 %collective-permute-start.17 = (bf16[512,128]{1,0:T(8,128)(2,1)S(1)}, bf16[512,128]{1,0:T(8,128)(2,1)S(1)}, u32[]{:S(2)}, u32[]{:S(2)}) collective-permute-start(bf16[512,128]{1,0:T(8,128)(2,1)S(1)} %collective-permute-done.16.refs_2_), channel_id=1, source_target_pairs={{0,1},{1,0},{2,3},{3,2},{4,5},{5,4},{6,7},{7,6},{8,9},{9,8},{10,11... | collective-permute-start | bytes 393224 | tf_op jit(solution)/shard_map/ppermute | solution.py:22
  72.9 0.0 collective-permute-done.19.refs_1_
  72.9 0.0 collective-permute-done.21.refs_3_
  72.9 7.0 %part_4.1 = (bf16[2048,768]{1,0:T(8,128)(2,1)}, bf16[512,768]{1,0:T(8,128)(2,1)}, bf16[512,128]{1,0:T(8,128)(2,1)}) custom-call(bf16[512,128]{1,0:T(8,128)(2,1)S(1)} %collective-permute-done.18.refs_0_, bf16[512,128]{1,0:T(8,128)(2,1)S(1)} %collective-permute-done.19.refs_1_, ...), custom_call_target="tpu_custom_call", output_to_operand_aliasing={{0}: (12, {}), {1}: (13, {})} | custom-call | flops 620756992 | bytes 5898240 | tf_op jit(solution)/shard_map/part_4/pallas_call | solution.py:145
  79.9 0.0 collective-permute-done.15.refs_1_
  79.9 0.0 collective-permute-done.17.refs_3_
  79.9 7.0 %part_5.1 = (bf16[2048,768]{1,0:T(8,128)(2,1)}, bf16[512,768]{1,0:T(8,128)(2,1)}, bf16[512,128]{1,0:T(8,128)(2,1)}) custom-call(bf16[512,128]{1,0:T(8,128)(2,1)S(1)} %collective-permute-done.14.refs_0_, bf16[512,128]{1,0:T(8,128)(2,1)S(1)} %collective-permute-done.15.refs_1_, ...), custom_call_target="tpu_custom_call", output_to_operand_aliasing={{0}: (12, {}), {1}: (13, {})} | custom-call | flops 620756992 | bytes 5898240 | tf_op jit(solution)/shard_map/part_5/pallas_call | solution.py:145
  (7 shorter events, 0.0 us)
Async XLA Ops:
  1.6 4.4 %collective-permute-start.4 = (bf16[512,128]{1,0:T(8,128)(2,1)S(1)}, bf16[512,128]{1,0:T(8,128)(2,1)S(1)}, u32[]{:S(2)}, u32[]{:S(2)}) collective-permute-start(bf16[512,128]{1,0:T(8,128)(2,1)S(1)} %get-tuple-element.46.refs_0_), channel_id=1, source_target_pairs={{0,2},{1,3},{2,0},{3,1},{4,6},{5,7},{6,4},{7,5},{8,10},{9,11},{10,... | collective-permute-start | bytes 393224 | tf_op jit(solution)/shard_map/ppermute | solution.py:22
  1.9 6.9 %collective-permute-start.1 = (bf16[512,128]{1,0:T(8,128)(2,1)S(1)}, bf16[512,128]{1,0:T(8,128)(2,1)S(1)}, u32[]{:S(2)}, u32[]{:S(2)}) collective-permute-start(bf16[512,128]{1,0:T(8,128)(2,1)S(1)} %get-tuple-element.47.refs_0_), channel_id=1, source_target_pairs={{0,2},{1,3},{2,0},{3,1},{4,6},{5,7},{6,4},{7,5},{8,10},{9,11},{10,... | collective-permute-start | bytes 393224 | tf_op jit(solution)/shard_map/ppermute | solution.py:22
  3.2 11.6 %collective-permute-start.3 = (bf16[512,128]{1,0:T(8,128)(2,1)S(1)}, bf16[512,128]{1,0:T(8,128)(2,1)S(1)}, u32[]{:S(2)}, u32[]{:S(2)}) collective-permute-start(bf16[512,128]{1,0:T(8,128)(2,1)S(1)} %get-tuple-element.46.refs_0_), channel_id=1, source_target_pairs={{0,1},{1,0},{2,3},{3,2},{4,5},{5,4},{6,7},{7,6},{8,9},{9,8},{10,11... | collective-permute-start | bytes 393224 | tf_op jit(solution)/shard_map/ppermute | solution.py:22
  6.1 8.7 %collective-permute-start.5 = (bf16[512,128]{1,0:T(8,128)(2,1)S(1)}, bf16[512,128]{1,0:T(8,128)(2,1)S(1)}, u32[]{:S(2)}, u32[]{:S(2)}) collective-permute-start(bf16[512,128]{1,0:T(8,128)(2,1)S(1)} %collective-permute-done.4.refs_2_), channel_id=1, source_target_pairs={{0,1},{1,0},{2,3},{3,2},{4,5},{5,4},{6,7},{7,6},{8,9},{9,8},{10,11... | collective-permute-start | bytes 393224 | tf_op jit(solution)/shard_map/ppermute | solution.py:22
  8.7 15.5 %collective-permute-start = (bf16[512,128]{1,0:T(8,128)(2,1)S(1)}, bf16[512,128]{1,0:T(8,128)(2,1)S(1)}, u32[]{:S(2)}, u32[]{:S(2)}) collective-permute-start(bf16[512,128]{1,0:T(8,128)(2,1)S(1)} %get-tuple-element.47.refs_0_), channel_id=1, source_target_pairs={{0,1},{1,0},{2,3},{3,2},{4,5},{5,4},{6,7},{7,6},{8,9},{9,8},{10,11... | collective-permute-start | bytes 393224 | tf_op jit(solution)/shard_map/ppermute | solution.py:22
  8.9 15.4 %collective-permute-start.2 = (bf16[512,128]{1,0:T(8,128)(2,1)S(1)}, bf16[512,128]{1,0:T(8,128)(2,1)S(1)}, u32[]{:S(2)}, u32[]{:S(2)}) collective-permute-start(bf16[512,128]{1,0:T(8,128)(2,1)S(1)} %collective-permute-done.1.refs_2_), channel_id=1, source_target_pairs={{0,1},{1,0},{2,3},{3,2},{4,5},{5,4},{6,7},{7,6},{8,9},{9,8},{10,11... | collective-permute-start | bytes 393224 | tf_op jit(solution)/shard_map/ppermute | solution.py:22
  11.2 3.6 %copy-start = (s32[4,8]{1,0:T(4,128)S(1)}, s32[4,8]{1,0:T(4,128)}, u32[]{:S(2)}) copy-start(s32[4,8]{1,0:T(4,128)} %refs_5_.13) | copy-start | bytes 388
  21.1 12.7 %collective-permute-start.10 = (bf16[512,128]{1,0:T(8,128)(2,1)S(1)}, bf16[512,128]{1,0:T(8,128)(2,1)S(1)}, u32[]{:S(2)}, u32[]{:S(2)}) collective-permute-start(bf16[512,128]{1,0:T(8,128)(2,1)S(1)} %get-tuple-element.33), channel_id=1, source_target_pairs={{0,4},{1,5},{2,6},{3,7},{4,8},{5,9},{6,10},{7,11},{8,12},{9,13},{1... | collective-permute-start | bytes 393224 | tf_op jit(solution)/shard_map/ppermute | solution.py:22
  30.6 7.6 %collective-permute-start.6 = (bf16[512,128]{1,0:T(8,128)(2,1)S(1)}, bf16[512,128]{1,0:T(8,128)(2,1)S(1)}, u32[]{:S(2)}, u32[]{:S(2)}) collective-permute-start(bf16[512,128]{1,0:T(8,128)(2,1)S(1)} %get-tuple-element.32), channel_id=1, source_target_pairs={{0,4},{1,5},{2,6},{3,7},{4,8},{5,9},{6,10},{7,11},{8,12},{9,13},{1... | collective-permute-start | bytes 393224 | tf_op jit(solution)/shard_map/ppermute | solution.py:22
  33.8 6.1 %collective-permute-start.12 = (bf16[512,128]{1,0:T(8,128)(2,1)S(1)}, bf16[512,128]{1,0:T(8,128)(2,1)S(1)}, u32[]{:S(2)}, u32[]{:S(2)}) collective-permute-start(bf16[512,128]{1,0:T(8,128)(2,1)S(1)} %collective-permute-done.10.refs_0_), channel_id=1, source_target_pairs={{0,2},{1,3},{2,0},{3,1},{4,6},{5,7},{6,4},{7,5},{8,10},{9,11},{10,... | collective-permute-start | bytes 393224 | tf_op jit(solution)/shard_map/ppermute | solution.py:22
  38.2 3.8 %collective-permute-start.8 = (bf16[512,128]{1,0:T(8,128)(2,1)S(1)}, bf16[512,128]{1,0:T(8,128)(2,1)S(1)}, u32[]{:S(2)}, u32[]{:S(2)}) collective-permute-start(bf16[512,128]{1,0:T(8,128)(2,1)S(1)} %collective-permute-done.6.refs_0_), channel_id=1, source_target_pairs={{0,2},{1,3},{2,0},{3,1},{4,6},{5,7},{6,4},{7,5},{8,10},{9,11},{10,... | collective-permute-start | bytes 393224 | tf_op jit(solution)/shard_map/ppermute | solution.py:22
  38.5 5.8 %collective-permute-start.11 = (bf16[512,128]{1,0:T(8,128)(2,1)S(1)}, bf16[512,128]{1,0:T(8,128)(2,1)S(1)}, u32[]{:S(2)}, u32[]{:S(2)}) collective-permute-start(bf16[512,128]{1,0:T(8,128)(2,1)S(1)} %collective-permute-done.10.refs_0_), channel_id=1, source_target_pairs={{0,1},{1,0},{2,3},{3,2},{4,5},{5,4},{6,7},{7,6},{8,9},{9,8},{10,11... | collective-permute-start | bytes 393224 | tf_op jit(solution)/shard_map/ppermute | solution.py:22
  39.9 4.4 %collective-permute-start.13 = (bf16[512,128]{1,0:T(8,128)(2,1)S(1)}, bf16[512,128]{1,0:T(8,128)(2,1)S(1)}, u32[]{:S(2)}, u32[]{:S(2)}) collective-permute-start(bf16[512,128]{1,0:T(8,128)(2,1)S(1)} %collective-permute-done.12.refs_2_), channel_id=1, source_target_pairs={{0,1},{1,0},{2,3},{3,2},{4,5},{5,4},{6,7},{7,6},{8,9},{9,8},{10,11... | collective-permute-start | bytes 393224 | tf_op jit(solution)/shard_map/ppermute | solution.py:22
  39.9 13.0 %collective-permute-start.7 = (bf16[512,128]{1,0:T(8,128)(2,1)S(1)}, bf16[512,128]{1,0:T(8,128)(2,1)S(1)}, u32[]{:S(2)}, u32[]{:S(2)}) collective-permute-start(bf16[512,128]{1,0:T(8,128)(2,1)S(1)} %collective-permute-done.6.refs_0_), channel_id=1, source_target_pairs={{0,1},{1,0},{2,3},{3,2},{4,5},{5,4},{6,7},{7,6},{8,9},{9,8},{10,11... | collective-permute-start | bytes 393224 | tf_op jit(solution)/shard_map/ppermute | solution.py:22
  42.0 10.9 %collective-permute-start.9 = (bf16[512,128]{1,0:T(8,128)(2,1)S(1)}, bf16[512,128]{1,0:T(8,128)(2,1)S(1)}, u32[]{:S(2)}, u32[]{:S(2)}) collective-permute-start(bf16[512,128]{1,0:T(8,128)(2,1)S(1)} %collective-permute-done.8.refs_2_), channel_id=1, source_target_pairs={{0,1},{1,0},{2,3},{3,2},{4,5},{5,4},{6,7},{7,6},{8,9},{9,8},{10,11... | collective-permute-start | bytes 393224 | tf_op jit(solution)/shard_map/ppermute | solution.py:22
  50.6 12.7 %collective-permute-start.18 = (bf16[512,128]{1,0:T(8,128)(2,1)S(1)}, bf16[512,128]{1,0:T(8,128)(2,1)S(1)}, u32[]{:S(2)}, u32[]{:S(2)}) collective-permute-start(bf16[512,128]{1,0:T(8,128)(2,1)S(1)} %get-tuple-element.39), channel_id=1, source_target_pairs={{0,4},{1,5},{2,6},{3,7},{4,8},{5,9},{6,10},{7,11},{8,12},{9,13},{1... | collective-permute-start | bytes 393224 | tf_op jit(solution)/shard_map/ppermute | solution.py:22
  59.2 7.6 %collective-permute-start.14 = (bf16[512,128]{1,0:T(8,128)(2,1)S(1)}, bf16[512,128]{1,0:T(8,128)(2,1)S(1)}, u32[]{:S(2)}, u32[]{:S(2)}) collective-permute-start(bf16[512,128]{1,0:T(8,128)(2,1)S(1)} %get-tuple-element.38), channel_id=1, source_target_pairs={{0,4},{1,5},{2,6},{3,7},{4,8},{5,9},{6,10},{7,11},{8,12},{9,13},{1... | collective-permute-start | bytes 393224 | tf_op jit(solution)/shard_map/ppermute | solution.py:22
  63.3 5.2 %collective-permute-start.20 = (bf16[512,128]{1,0:T(8,128)(2,1)S(1)}, bf16[512,128]{1,0:T(8,128)(2,1)S(1)}, u32[]{:S(2)}, u32[]{:S(2)}) collective-permute-start(bf16[512,128]{1,0:T(8,128)(2,1)S(1)} %collective-permute-done.18.refs_0_), channel_id=1, source_target_pairs={{0,2},{1,3},{2,0},{3,1},{4,6},{5,7},{6,4},{7,5},{8,10},{9,11},{10,... | collective-permute-start | bytes 393224 | tf_op jit(solution)/shard_map/ppermute | solution.py:22
  66.8 3.8 %collective-permute-start.16 = (bf16[512,128]{1,0:T(8,128)(2,1)S(1)}, bf16[512,128]{1,0:T(8,128)(2,1)S(1)}, u32[]{:S(2)}, u32[]{:S(2)}) collective-permute-start(bf16[512,128]{1,0:T(8,128)(2,1)S(1)} %collective-permute-done.14.refs_0_), channel_id=1, source_target_pairs={{0,2},{1,3},{2,0},{3,1},{4,6},{5,7},{6,4},{7,5},{8,10},{9,11},{10,... | collective-permute-start | bytes 393224 | tf_op jit(solution)/shard_map/ppermute | solution.py:22
  67.1 5.8 %collective-permute-start.19 = (bf16[512,128]{1,0:T(8,128)(2,1)S(1)}, bf16[512,128]{1,0:T(8,128)(2,1)S(1)}, u32[]{:S(2)}, u32[]{:S(2)}) collective-permute-start(bf16[512,128]{1,0:T(8,128)(2,1)S(1)} %collective-permute-done.18.refs_0_), channel_id=1, source_target_pairs={{0,1},{1,0},{2,3},{3,2},{4,5},{5,4},{6,7},{7,6},{8,9},{9,8},{10,11... | collective-permute-start | bytes 393224 | tf_op jit(solution)/shard_map/ppermute | solution.py:22
  68.5 4.4 %collective-permute-start.21 = (bf16[512,128]{1,0:T(8,128)(2,1)S(1)}, bf16[512,128]{1,0:T(8,128)(2,1)S(1)}, u32[]{:S(2)}, u32[]{:S(2)}) collective-permute-start(bf16[512,128]{1,0:T(8,128)(2,1)S(1)} %collective-permute-done.20.refs_2_), channel_id=1, source_target_pairs={{0,1},{1,0},{2,3},{3,2},{4,5},{5,4},{6,7},{7,6},{8,9},{9,8},{10,11... | collective-permute-start | bytes 393224 | tf_op jit(solution)/shard_map/ppermute | solution.py:22
  69.3 10.6 %collective-permute-start.15 = (bf16[512,128]{1,0:T(8,128)(2,1)S(1)}, bf16[512,128]{1,0:T(8,128)(2,1)S(1)}, u32[]{:S(2)}, u32[]{:S(2)}) collective-permute-start(bf16[512,128]{1,0:T(8,128)(2,1)S(1)} %collective-permute-done.14.refs_0_), channel_id=1, source_target_pairs={{0,1},{1,0},{2,3},{3,2},{4,5},{5,4},{6,7},{7,6},{8,9},{9,8},{10,11... | collective-permute-start | bytes 393224 | tf_op jit(solution)/shard_map/ppermute | solution.py:22
  70.7 9.3 %collective-permute-start.17 = (bf16[512,128]{1,0:T(8,128)(2,1)S(1)}, bf16[512,128]{1,0:T(8,128)(2,1)S(1)}, u32[]{:S(2)}, u32[]{:S(2)}) collective-permute-start(bf16[512,128]{1,0:T(8,128)(2,1)S(1)} %collective-permute-done.16.refs_2_), channel_id=1, source_target_pairs={{0,1},{1,0},{2,3},{3,2},{4,5},{5,4},{6,7},{7,6},{8,9},{9,8},{10,11... | collective-permute-start | bytes 393224 | tf_op jit(solution)/shard_map/ppermute | solution.py:22

commit v2 on v1

--- a/solution.py
+++ b/solution.py
@@ -69,7 +69,7 @@
     return jnp.dot(a, b, preferred_element_type=jnp.float32)
 
 
-def part_kernel(subs, width, column, step, aliased, *refs):
+def part_kernel(subs, width, column, aliased, *refs):
     shares, refs = refs[:subs], refs[subs:]
     (in_idx, out_idx, in_blocks, in_inv, out_blocks, out_inv, sides, fronts), refs = (
         refs[:8],
@@ -77,7 +77,7 @@
     )
     if aliased:
         refs = refs[2:]
-    sol_hbm, fsol_hbm, f_ref, inc, sol, sem, fsem = refs
+    sol_hbm, fsol_hbm, f_ref, inc, val, sol, sem, fsem = refs
     rows_in, links = in_idx.shape
     rows_out, out_links = out_idx.shape
     size = in_inv.shape[1]
@@ -90,36 +90,32 @@
     def rows_of(ref, block):
         return ref[pl.ds(pl.multiple_of(block * size, size), size), :]
 
-    def out_copy(g):
-        rows = pl.ds(pl.multiple_of(g * step * size, size), step * size)
-        return pltpu.make_async_copy(
-            sol.at[rows, :], sol_hbm.at[rows, cols], sem.at[g]
-        )
-
-    def inner(g, _):
-        for r in range(step):
-            i = g * step + r
-            picked = [rows_of(inc, in_idx[i, k] ^ swap) for k in range(links)]
-            lhs = jnp.concatenate([in_blocks[i, k] for k in range(links)], axis=1)
-            coupled = dot(lhs, jnp.concatenate(picked, axis=0))
-            at = pl.ds(pl.multiple_of(i * size, size), size)
-            value = (sides[at, cols].astype(jnp.float32) - coupled).astype(jnp.bfloat16)
-            sol[at, :] = dot(in_inv[i], value).astype(jnp.bfloat16)
-        out_copy(g).start()
-        return 0
-
-    lax.fori_loop(0, rows_in // step, inner, 0)
+    def at(i):
+        return pl.ds(i * size, size)
+
+    def side(ref, i):
+        return ref[at(i), cols].astype(jnp.float32)
+
+    def row_of(ref, index, i, source, count, flip):
+        lhs = jnp.concatenate([ref[i, k] for k in range(count)], axis=1)
+        blocks = [rows_of(source, index[i, k] ^ flip) for k in range(count)]
+        return dot(lhs, jnp.concatenate(blocks, axis=0))
+
+    for i in range(rows_in):
+        coupled = row_of(in_blocks, in_idx, i, inc, links, swap)
+        val[at(i), :] = (side(sides, i) - coupled).astype(val.dtype)
+    for i in range(rows_in):
+        sol[at(i), :] = dot(in_inv[i], val[at(i), :]).astype(sol.dtype)
+    first = pltpu.make_async_copy(sol, sol_hbm.at[:, cols], sem)
+    first.start()
     for j in range(rows_out):
-        chosen = [rows_of(sol, out_idx[j, k]) for k in range(out_links)]
-        lhs = jnp.concatenate([out_blocks[j, k] for k in range(out_links)], axis=1)
-        outgoing = dot(lhs, jnp.concatenate(chosen, axis=0))
-        at = pl.ds(j * size, size)
-        value = (fronts[at, cols].astype(jnp.float32) - outgoing).astype(jnp.bfloat16)
-        f_ref[at, :] = dot(out_inv[j], value).astype(jnp.bfloat16)
+        outgoing = row_of(out_blocks, out_idx, j, sol, out_links, 0)
+        val[at(j), :] = (side(fronts, j) - outgoing).astype(val.dtype)
+    for j in range(rows_out):
+        f_ref[at(j), :] = dot(out_inv[j], val[at(j), :]).astype(f_ref.dtype)
     last = pltpu.make_async_copy(f_ref, fsol_hbm.at[:, cols], fsem)
     last.start()
-    for g in range(rows_in // step):
-        out_copy(g).wait()
+    first.wait()
     last.wait()
 
 
@@ -128,7 +124,6 @@
     rows, front_rows = sides.shape[0], fronts.shape[0]
     rows_in, links, size, _ = weights[0].shape
     rows_out, out_links = out_idx.shape
-    step = next(s for s in (4, 2, 1) if rows_in % s == 0)
     blocks = rows_in * (links + 1) + rows_out * (out_links + 1)
     smem = pl.BlockSpec(memory_space=pltpu.SMEM)
     vmem = pl.BlockSpec(memory_space=VMEM)
@@ -143,7 +138,7 @@
     )
     n = len(operands)
     return pl.pallas_call(
-        functools.partial(part_kernel, subs, width, column, step, aliased),
+        functools.partial(part_kernel, subs, width, column, aliased),
         out_shape=(
             pltpu.HBM(sides.shape, sides.dtype),
             pltpu.HBM(fronts.shape, fronts.dtype),
@@ -154,7 +149,8 @@
         scratch_shapes=[
             VMEM((subs * shares[0].shape[0], width), sides.dtype),
             VMEM((rows, width), sides.dtype),
-            pltpu.SemaphoreType.DMA((rows_in // step,)),
+            VMEM((rows, width), sides.dtype),
+            pltpu.SemaphoreType.DMA,
             pltpu.SemaphoreType.DMA,
         ],
         input_output_aliases={n - 2: 0, n - 1: 1} if aliased else {},

time: 87.2 us -> 68.5 us (0.79)
  Pallas kernels: 42.8 us -> 24.2 us
    pallas_call x6, Pallas kernels: 39.3 us -> 20.6 us  [part(): pl.pallas_call(functools.partial(part_kernel, subs, width, column, aliase...]
  transfers between devices with their start and end apart: 22 -> 22, of which waited for: 6 -> 6; matrix products, arithmetic and copies ran while one was open for 1% -> 1% of each run, Pallas kernels for 41% -> 30%
where the time goes in v2:
time: 68.5 us; the launch traced here: 68.2 us
  starting transfers between devices  29.3 us (43%)
  Pallas kernels  24.2 us (35%)
  waiting for transfers between devices  12.2 us (18%)
  local copies, waits for them, and re-layouts  1.75 us (3%)
  between operations  0.82 us (1%)
    ppermute x22, starting transfers between devices, permuted(): return lax.ppermute(x, AXES, pairs)  29.3 us
    pallas_call x6, Pallas kernels, part(): pl.pallas_call(functools.partial(part_kernel, subs, width, column, aliase...  20.6 us
    ppermute x22, waiting for transfers between devices, permuted(): return lax.ppermute(x, AXES, pairs)  12.2 us
    pallas_call x1, Pallas kernels, staged(): pl.pallas_call(functools.partial(stage_kernel, n), out_shape=tuple((VMEM(...  3.55 us
  transfers between devices with their start and end apart: 22, of which 6 were waited for; matrix products, arithmetic and copies ran while one was open for 1% of the time, Pallas kernels for 30%

profile of v2, /device:TPU:11, one launch (start us, length us, event | category | flops | bytes accessed | tf_op | source)
XLA Modules:
  0.0 68.2 jit_solution(13222145477074283966)
XLA Ops:
  0.6 1.0 %fusion = (bf16[512,128]{1,0:T(8,128)(2,1)S(1)}, bf16[512,128]{1,0:T(8,128)(2,1)S(1)}) fusion(bf16[512,256]{1,0:T(8,128)(2,1)} %param.11), kind=kLoop, calls=%fused_computation | loop fusion | bytes 524288 | tf_op jit(solution)/shard_map/slice | solution.py:184
  1.6 0.3 collective-permute-start.4
  1.9 1.2 %collective-permute-start.1 = (bf16[512,128]{1,0:T(8,128)(2,1)S(1)}, bf16[512,128]{1,0:T(8,128)(2,1)S(1)}, u32[]{:S(2)}, u32[]{:S(2)}) collective-permute-start(bf16[512,128]{1,0:T(8,128)(2,1)S(1)} %get-tuple-element.47.refs_0_), channel_id=1, source_target_pairs={{0,2},{1,3},{2,0},{3,1},{4,6},{5,7},{6,4},{7,5},{8,10},{9,11},{10,... | collective-permute-start | bytes 393224 | tf_op jit(solution)/shard_map/ppermute | solution.py:22
  3.2 1.2 %collective-permute-start.3 = (bf16[512,128]{1,0:T(8,128)(2,1)S(1)}, bf16[512,128]{1,0:T(8,128)(2,1)S(1)}, u32[]{:S(2)}, u32[]{:S(2)}) collective-permute-start(bf16[512,128]{1,0:T(8,128)(2,1)S(1)} %get-tuple-element.46.refs_0_), channel_id=1, source_target_pairs={{0,1},{1,0},{2,3},{3,2},{4,5},{5,4},{6,7},{7,6},{8,9},{9,8},{10,11... | collective-permute-start | bytes 393224 | tf_op jit(solution)/shard_map/ppermute | solution.py:22
  4.4 1.7 %collective-permute-done.4.refs_2_ = bf16[512,128]{1,0:T(8,128)(2,1)S(1)} collective-permute-done((bf16[512,128]{1,0:T(8,128)(2,1)S(1)}, bf16[512,128]{1,0:T(8,128)(2,1)S(1)}, u32[]{:S(2)}, u32[]{:S(2)}) %collective-permute-start.4) | collective-permute-done | bytes 131104 | tf_op jit(solution)/shard_map/ppermute | solution.py:22
  6.1 2.7 %collective-permute-start.5 = (bf16[512,128]{1,0:T(8,128)(2,1)S(1)}, bf16[512,128]{1,0:T(8,128)(2,1)S(1)}, u32[]{:S(2)}, u32[]{:S(2)}) collective-permute-start(bf16[512,128]{1,0:T(8,128)(2,1)S(1)} %collective-permute-done.4.refs_2_), channel_id=1, source_target_pairs={{0,1},{1,0},{2,3},{3,2},{4,5},{5,4},{6,7},{7,6},{8,9},{9,8},{10,11... | collective-permute-start | bytes 393224 | tf_op jit(solution)/shard_map/ppermute | solution.py:22
  8.7 0.0 collective-permute-start
  8.7 0.1 collective-permute-done.1.refs_2_
  8.9 1.5 %collective-permute-start.2 = (bf16[512,128]{1,0:T(8,128)(2,1)S(1)}, bf16[512,128]{1,0:T(8,128)(2,1)S(1)}, u32[]{:S(2)}, u32[]{:S(2)}) collective-permute-start(bf16[512,128]{1,0:T(8,128)(2,1)S(1)} %collective-permute-done.1.refs_2_), channel_id=1, source_target_pairs={{0,1},{1,0},{2,3},{3,2},{4,5},{5,4},{6,7},{7,6},{8,9},{9,8},{10,11... | collective-permute-start | bytes 393224 | tf_op jit(solution)/shard_map/ppermute | solution.py:22
  10.4 0.8 %copy.22.refs_4_ = s32[16,6]{1,0:T(8,128)S(1)} copy(s32[16,6]{0,1:T(8,128)} %param.12) | data formatting | bytes 768 | tf_op args[3]
  11.2 3.6 %stage.1 = (bf16[16,6,128,128]{3,2,1,0:T(8,128)(2,1)S(1)}, bf16[16,128,128]{2,1,0:T(8,128)(2,1)S(1)}, bf16[4,8,128,128]{3,2,1,0:T(8,128)(2,1)S(1)}, bf16[4,128,1...) custom-call(bf16[16,6,128,128]{3,2,1,0:T(8,128)(2,1)} %refs_0_.1, ...), custom_call_target="tpu_custom_call" | custom-call | bytes 17563648 | tf_op jit(solution)/shard_map/stage/pallas_call | solution.py:54
  14.7 0.0 collective-permute-done.3.refs_1_
  14.8 3.2 %part_0.1 = (bf16[2048,768]{1,0:T(8,128)(2,1)}, bf16[512,768]{1,0:T(8,128)(2,1)}, bf16[512,128]{1,0:T(8,128)(2,1)S(1)}) custom-call(bf16[512,128]{1,0:T(8,128)(2,1)S(1)} %get-tuple-element.46.refs_0_, bf16[512,128]{1,0:T(8,128)(2,1)S(1)} %collective-permute-done.3.refs_1_, bf16[512,128]{1,0:T(8,128)(2,1)S(1)} %collective-permute-done.4.refs_2_, ...), custom_call_target="tpu_custom_call" | custom-call | flops 620756992 | bytes 5898240 | tf_op jit(solution)/shard_map/part_0/pallas_call | solution.py:140
  18.0 3.1 %collective-permute-start.10 = (bf16[512,128]{1,0:T(8,128)(2,1)S(1)}, bf16[512,128]{1,0:T(8,128)(2,1)S(1)}, u32[]{:S(2)}, u32[]{:S(2)}) collective-permute-start(bf16[512,128]{1,0:T(8,128)(2,1)S(1)} %get-tuple-element.33), channel_id=1, source_target_pairs={{0,4},{1,5},{2,6},{3,7},{4,8},{5,9},{6,10},{7,11},{8,12},{9,13},{1... | collective-permute-start | bytes 393224 | tf_op jit(solution)/shard_map/ppermute | solution.py:22
  21.1 0.0 collective-permute-done.refs_1_
  21.2 3.2 %part_1.1 = (bf16[2048,768]{1,0:T(8,128)(2,1)}, bf16[512,768]{1,0:T(8,128)(2,1)}, bf16[512,128]{1,0:T(8,128)(2,1)S(1)}) custom-call(bf16[512,128]{1,0:T(8,128)(2,1)S(1)} %get-tuple-element.47.refs_0_, bf16[512,128]{1,0:T(8,128)(2,1)S(1)} %collective-permute-done.refs_1_, ...), custom_call_target="tpu_custom_call", output_to_operand_aliasing={{0}: (12, {}), {1}: (13, {})} | custom-call | flops 620756992 | bytes 5898240 | tf_op jit(solution)/shard_map/part_1/pallas_call | solution.py:140
  24.4 3.1 %collective-permute-start.6 = (bf16[512,128]{1,0:T(8,128)(2,1)S(1)}, bf16[512,128]{1,0:T(8,128)(2,1)S(1)}, u32[]{:S(2)}, u32[]{:S(2)}) collective-permute-start(bf16[512,128]{1,0:T(8,128)(2,1)S(1)} %get-tuple-element.32), channel_id=1, source_target_pairs={{0,4},{1,5},{2,6},{3,7},{4,8},{5,9},{6,10},{7,11},{8,12},{9,13},{1... | collective-permute-start | bytes 393224 | tf_op jit(solution)/shard_map/ppermute | solution.py:22
  27.6 0.3 collective-permute-start.12
  27.9 4.1 %collective-permute-done.6.refs_0_ = bf16[512,128]{1,0:T(8,128)(2,1)S(1)} collective-permute-done((bf16[512,128]{1,0:T(8,128)(2,1)S(1)}, bf16[512,128]{1,0:T(8,128)(2,1)S(1)}, u32[]{:S(2)}, u32[]{:S(2)}) %collective-permute-start.6) | collective-permute-done | bytes 131104 | tf_op jit(solution)/shard_map/ppermute | solution.py:22
  32.0 0.2 collective-permute-start.8
  32.3 1.4 %collective-permute-start.11 = (bf16[512,128]{1,0:T(8,128)(2,1)S(1)}, bf16[512,128]{1,0:T(8,128)(2,1)S(1)}, u32[]{:S(2)}, u32[]{:S(2)}) collective-permute-start(bf16[512,128]{1,0:T(8,128)(2,1)S(1)} %collective-permute-done.10.refs_0_), channel_id=1, source_target_pairs={{0,1},{1,0},{2,3},{3,2},{4,5},{5,4},{6,7},{7,6},{8,9},{9,8},{10,11... | collective-permute-start | bytes 393224 | tf_op jit(solution)/shard_map/ppermute | solution.py:22
  33.6 0.0 collective-permute-done.12.refs_2_
  33.6 0.0 collective-permute-start.13
  33.6 0.5 collective-permute-start.7
  34.2 1.7 %collective-permute-done.8.refs_2_ = bf16[512,128]{1,0:T(8,128)(2,1)S(1)} collective-permute-done((bf16[512,128]{1,0:T(8,128)(2,1)S(1)}, bf16[512,128]{1,0:T(8,128)(2,1)S(1)}, u32[]{:S(2)}, u32[]{:S(2)}) %collective-permute-start.8) | collective-permute-done | bytes 131104 | tf_op jit(solution)/shard_map/ppermute | solution.py:22
  35.8 2.2 %collective-permute-start.9 = (bf16[512,128]{1,0:T(8,128)(2,1)S(1)}, bf16[512,128]{1,0:T(8,128)(2,1)S(1)}, u32[]{:S(2)}, u32[]{:S(2)}) collective-permute-start(bf16[512,128]{1,0:T(8,128)(2,1)S(1)} %collective-permute-done.8.refs_2_), channel_id=1, source_target_pairs={{0,1},{1,0},{2,3},{3,2},{4,5},{5,4},{6,7},{7,6},{8,9},{9,8},{10,11... | collective-permute-start | bytes 393224 | tf_op jit(solution)/shard_map/ppermute | solution.py:22
  38.1 0.0 collective-permute-done.11.refs_1_
  38.1 3.2 %part_2.1 = (bf16[2048,768]{1,0:T(8,128)(2,1)}, bf16[512,768]{1,0:T(8,128)(2,1)}, bf16[512,128]{1,0:T(8,128)(2,1)S(1)}) custom-call(bf16[512,128]{1,0:T(8,128)(2,1)S(1)} %collective-permute-done.10.refs_0_, bf16[512,128]{1,0:T(8,128)(2,1)S(1)} %collective-permute-done.11.refs_1_, ...), custom_call_target="tpu_custom_call", output_to_operand_aliasing={{0}: (12, {}), {1}: (13, {})} | custom-call | flops 620756992 | bytes 5898240 | tf_op jit(solution)/shard_map/part_2/pallas_call | solution.py:140
  41.3 2.2 %collective-permute-start.18 = (bf16[512,128]{1,0:T(8,128)(2,1)S(1)}, bf16[512,128]{1,0:T(8,128)(2,1)S(1)}, u32[]{:S(2)}, u32[]{:S(2)}) collective-permute-start(bf16[512,128]{1,0:T(8,128)(2,1)S(1)} %get-tuple-element.39), channel_id=1, source_target_pairs={{0,4},{1,5},{2,6},{3,7},{4,8},{5,9},{6,10},{7,11},{8,12},{9,13},{1... | collective-permute-start | bytes 393224 | tf_op jit(solution)/shard_map/ppermute | solution.py:22
  43.6 0.0 collective-permute-done.7.refs_1_
  43.6 0.0 collective-permute-done.9.refs_3_
  43.6 3.2 %part_3.1 = (bf16[2048,768]{1,0:T(8,128)(2,1)}, bf16[512,768]{1,0:T(8,128)(2,1)}, bf16[512,128]{1,0:T(8,128)(2,1)S(1)}) custom-call(bf16[512,128]{1,0:T(8,128)(2,1)S(1)} %collective-permute-done.6.refs_0_, bf16[512,128]{1,0:T(8,128)(2,1)S(1)} %collective-permute-done.7.refs_1_, ...), custom_call_target="tpu_custom_call", output_to_operand_aliasing={{0}: (12, {}), {1}: (13, {})} | custom-call | flops 620756992 | bytes 5898240 | tf_op jit(solution)/shard_map/part_3/pallas_call | solution.py:140
  46.8 4.1 %collective-permute-start.14 = (bf16[512,128]{1,0:T(8,128)(2,1)S(1)}, bf16[512,128]{1,0:T(8,128)(2,1)S(1)}, u32[]{:S(2)}, u32[]{:S(2)}) collective-permute-start(bf16[512,128]{1,0:T(8,128)(2,1)S(1)} %get-tuple-element.38), channel_id=1, source_target_pairs={{0,4},{1,5},{2,6},{3,7},{4,8},{5,9},{6,10},{7,11},{8,12},{9,13},{1... | collective-permute-start | bytes 393224 | tf_op jit(solution)/shard_map/ppermute | solution.py:22
  50.9 0.0 collective-permute-done.18.refs_0_
  50.9 0.3 collective-permute-start.20
  51.2 3.2 %collective-permute-done.14.refs_0_ = bf16[512,128]{1,0:T(8,128)(2,1)S(1)} collective-permute-done((bf16[512,128]{1,0:T(8,128)(2,1)S(1)}, bf16[512,128]{1,0:T(8,128)(2,1)S(1)}, u32[]{:S(2)}, u32[]{:S(2)}) %collective-permute-start.14) | collective-permute-done | bytes 131104 | tf_op jit(solution)/shard_map/ppermute | solution.py:22
  54.4 0.2 collective-permute-start.16
  54.6 1.4 %collective-permute-start.19 = (bf16[512,128]{1,0:T(8,128)(2,1)S(1)}, bf16[512,128]{1,0:T(8,128)(2,1)S(1)}, u32[]{:S(2)}, u32[]{:S(2)}) collective-permute-start(bf16[512,128]{1,0:T(8,128)(2,1)S(1)} %collective-permute-done.18.refs_0_), channel_id=1, source_target_pairs={{0,1},{1,0},{2,3},{3,2},{4,5},{5,4},{6,7},{7,6},{8,9},{9,8},{10,11... | collective-permute-start | bytes 393224 | tf_op jit(solution)/shard_map/ppermute | solution.py:22
  56.0 0.0 collective-permute-done.20.refs_2_
  56.0 0.8 %collective-permute-start.21 = (bf16[512,128]{1,0:T(8,128)(2,1)S(1)}, bf16[512,128]{1,0:T(8,128)(2,1)S(1)}, u32[]{:S(2)}, u32[]{:S(2)}) collective-permute-start(bf16[512,128]{1,0:T(8,128)(2,1)S(1)} %collective-permute-done.20.refs_2_), channel_id=1, source_target_pairs={{0,1},{1,0},{2,3},{3,2},{4,5},{5,4},{6,7},{7,6},{8,9},{9,8},{10,11... | collective-permute-start | bytes 393224 | tf_op jit(solution)/shard_map/ppermute | solution.py:22
  56.9 0.0 collective-permute-start.15
  56.9 1.4 %collective-permute-done.16.refs_2_ = bf16[512,128]{1,0:T(8,128)(2,1)S(1)} collective-permute-done((bf16[512,128]{1,0:T(8,128)(2,1)S(1)}, bf16[512,128]{1,0:T(8,128)(2,1)S(1)}, u32[]{:S(2)}, u32[]{:S(2)}) %collective-permute-start.16) | collective-permute-done | bytes 131104 | tf_op jit(solution)/shard_map/ppermute | solution.py:22
  58.2 2.3 %collective-permute-start.17 = (bf16[512,128]{1,0:T(8,128)(2,1)S(1)}, bf16[512,128]{1,0:T(8,128)(2,1)S(1)}, u32[]{:S(2)}, u32[]{:S(2)}) collective-permute-start(bf16[512,128]{1,0:T(8,128)(2,1)S(1)} %collective-permute-done.16.refs_2_), channel_id=1, source_target_pairs={{0,1},{1,0},{2,3},{3,2},{4,5},{5,4},{6,7},{7,6},{8,9},{9,8},{10,11... | collective-permute-start | bytes 393224 | tf_op jit(solution)/shard_map/ppermute | solution.py:22
  60.5 0.0 collective-permute-done.19.refs_1_
  60.5 0.0 collective-permute-done.21.refs_3_
  60.5 3.9 %part_4.1 = (bf16[2048,768]{1,0:T(8,128)(2,1)}, bf16[512,768]{1,0:T(8,128)(2,1)}, bf16[512,128]{1,0:T(8,128)(2,1)}) custom-call(bf16[512,128]{1,0:T(8,128)(2,1)S(1)} %collective-permute-done.18.refs_0_, bf16[512,128]{1,0:T(8,128)(2,1)S(1)} %collective-permute-done.19.refs_1_, ...), custom_call_target="tpu_custom_call", output_to_operand_aliasing={{0}: (12, {}), {1}: (13, {})} | custom-call | flops 620756992 | bytes 5898240 | tf_op jit(solution)/shard_map/part_4/pallas_call | solution.py:140
  64.4 0.0 collective-permute-done.15.refs_1_
  64.4 3.9 %part_5.1 = (bf16[2048,768]{1,0:T(8,128)(2,1)}, bf16[512,768]{1,0:T(8,128)(2,1)}, bf16[512,128]{1,0:T(8,128)(2,1)}) custom-call(bf16[512,128]{1,0:T(8,128)(2,1)S(1)} %collective-permute-done.14.refs_0_, bf16[512,128]{1,0:T(8,128)(2,1)S(1)} %collective-permute-done.15.refs_1_, ...), custom_call_target="tpu_custom_call", output_to_operand_aliasing={{0}: (12, {}), {1}: (13, {})} | custom-call | flops 620756992 | bytes 5898240 | tf_op jit(solution)/shard_map/part_5/pallas_call | solution.py:140
  (7 shorter events, 0.0 us)
Async XLA Ops:
  1.6 4.4 %collective-permute-start.4 = (bf16[512,128]{1,0:T(8,128)(2,1)S(1)}, bf16[512,128]{1,0:T(8,128)(2,1)S(1)}, u32[]{:S(2)}, u32[]{:S(2)}) collective-permute-start(bf16[512,128]{1,0:T(8,128)(2,1)S(1)} %get-tuple-element.46.refs_0_), channel_id=1, source_target_pairs={{0,2},{1,3},{2,0},{3,1},{4,6},{5,7},{6,4},{7,5},{8,10},{9,11},{10,... | collective-permute-start | bytes 393224 | tf_op jit(solution)/shard_map/ppermute | solution.py:22
  1.9 6.9 %collective-permute-start.1 = (bf16[512,128]{1,0:T(8,128)(2,1)S(1)}, bf16[512,128]{1,0:T(8,128)(2,1)S(1)}, u32[]{:S(2)}, u32[]{:S(2)}) collective-permute-start(bf16[512,128]{1,0:T(8,128)(2,1)S(1)} %get-tuple-element.47.refs_0_), channel_id=1, source_target_pairs={{0,2},{1,3},{2,0},{3,1},{4,6},{5,7},{6,4},{7,5},{8,10},{9,11},{10,... | collective-permute-start | bytes 393224 | tf_op jit(solution)/shard_map/ppermute | solution.py:22
  3.2 11.6 %collective-permute-start.3 = (bf16[512,128]{1,0:T(8,128)(2,1)S(1)}, bf16[512,128]{1,0:T(8,128)(2,1)S(1)}, u32[]{:S(2)}, u32[]{:S(2)}) collective-permute-start(bf16[512,128]{1,0:T(8,128)(2,1)S(1)} %get-tuple-element.46.refs_0_), channel_id=1, source_target_pairs={{0,1},{1,0},{2,3},{3,2},{4,5},{5,4},{6,7},{7,6},{8,9},{9,8},{10,11... | collective-permute-start | bytes 393224 | tf_op jit(solution)/shard_map/ppermute | solution.py:22
  6.1 8.7 %collective-permute-start.5 = (bf16[512,128]{1,0:T(8,128)(2,1)S(1)}, bf16[512,128]{1,0:T(8,128)(2,1)S(1)}, u32[]{:S(2)}, u32[]{:S(2)}) collective-permute-start(bf16[512,128]{1,0:T(8,128)(2,1)S(1)} %collective-permute-done.4.refs_2_), channel_id=1, source_target_pairs={{0,1},{1,0},{2,3},{3,2},{4,5},{5,4},{6,7},{7,6},{8,9},{9,8},{10,11... | collective-permute-start | bytes 393224 | tf_op jit(solution)/shard_map/ppermute | solution.py:22
  8.7 12.4 %collective-permute-start = (bf16[512,128]{1,0:T(8,128)(2,1)S(1)}, bf16[512,128]{1,0:T(8,128)(2,1)S(1)}, u32[]{:S(2)}, u32[]{:S(2)}) collective-permute-start(bf16[512,128]{1,0:T(8,128)(2,1)S(1)} %get-tuple-element.47.refs_0_), channel_id=1, source_target_pairs={{0,1},{1,0},{2,3},{3,2},{4,5},{5,4},{6,7},{7,6},{8,9},{9,8},{10,11... | collective-permute-start | bytes 393224 | tf_op jit(solution)/shard_map/ppermute | solution.py:22
  8.9 12.3 %collective-permute-start.2 = (bf16[512,128]{1,0:T(8,128)(2,1)S(1)}, bf16[512,128]{1,0:T(8,128)(2,1)S(1)}, u32[]{:S(2)}, u32[]{:S(2)}) collective-permute-start(bf16[512,128]{1,0:T(8,128)(2,1)S(1)} %collective-permute-done.1.refs_2_), channel_id=1, source_target_pairs={{0,1},{1,0},{2,3},{3,2},{4,5},{5,4},{6,7},{7,6},{8,9},{9,8},{10,11... | collective-permute-start | bytes 393224 | tf_op jit(solution)/shard_map/ppermute | solution.py:22
  11.2 3.6 %copy-start = (s32[4,8]{1,0:T(4,128)S(1)}, s32[4,8]{1,0:T(4,128)}, u32[]{:S(2)}) copy-start(s32[4,8]{1,0:T(4,128)} %refs_5_.13) | copy-start | bytes 388
  18.0 9.6 %collective-permute-start.10 = (bf16[512,128]{1,0:T(8,128)(2,1)S(1)}, bf16[512,128]{1,0:T(8,128)(2,1)S(1)}, u32[]{:S(2)}, u32[]{:S(2)}) collective-permute-start(bf16[512,128]{1,0:T(8,128)(2,1)S(1)} %get-tuple-element.33), channel_id=1, source_target_pairs={{0,4},{1,5},{2,6},{3,7},{4,8},{5,9},{6,10},{7,11},{8,12},{9,13},{1... | collective-permute-start | bytes 393224 | tf_op jit(solution)/shard_map/ppermute | solution.py:22
  24.4 7.6 %collective-permute-start.6 = (bf16[512,128]{1,0:T(8,128)(2,1)S(1)}, bf16[512,128]{1,0:T(8,128)(2,1)S(1)}, u32[]{:S(2)}, u32[]{:S(2)}) collective-permute-start(bf16[512,128]{1,0:T(8,128)(2,1)S(1)} %get-tuple-element.32), channel_id=1, source_target_pairs={{0,4},{1,5},{2,6},{3,7},{4,8},{5,9},{6,10},{7,11},{8,12},{9,13},{1... | collective-permute-start | bytes 393224 | tf_op jit(solution)/shard_map/ppermute | solution.py:22
  27.6 6.1 %collective-permute-start.12 = (bf16[512,128]{1,0:T(8,128)(2,1)S(1)}, bf16[512,128]{1,0:T(8,128)(2,1)S(1)}, u32[]{:S(2)}, u32[]{:S(2)}) collective-permute-start(bf16[512,128]{1,0:T(8,128)(2,1)S(1)} %collective-permute-done.10.refs_0_), channel_id=1, source_target_pairs={{0,2},{1,3},{2,0},{3,1},{4,6},{5,7},{6,4},{7,5},{8,10},{9,11},{10,... | collective-permute-start | bytes 393224 | tf_op jit(solution)/shard_map/ppermute | solution.py:22
  32.0 3.8 %collective-permute-start.8 = (bf16[512,128]{1,0:T(8,128)(2,1)S(1)}, bf16[512,128]{1,0:T(8,128)(2,1)S(1)}, u32[]{:S(2)}, u32[]{:S(2)}) collective-permute-start(bf16[512,128]{1,0:T(8,128)(2,1)S(1)} %collective-permute-done.6.refs_0_), channel_id=1, source_target_pairs={{0,2},{1,3},{2,0},{3,1},{4,6},{5,7},{6,4},{7,5},{8,10},{9,11},{10,... | collective-permute-start | bytes 393224 | tf_op jit(solution)/shard_map/ppermute | solution.py:22
  32.3 5.8 %collective-permute-start.11 = (bf16[512,128]{1,0:T(8,128)(2,1)S(1)}, bf16[512,128]{1,0:T(8,128)(2,1)S(1)}, u32[]{:S(2)}, u32[]{:S(2)}) collective-permute-start(bf16[512,128]{1,0:T(8,128)(2,1)S(1)} %collective-permute-done.10.refs_0_), channel_id=1, source_target_pairs={{0,1},{1,0},{2,3},{3,2},{4,5},{5,4},{6,7},{7,6},{8,9},{9,8},{10,11... | collective-permute-start | bytes 393224 | tf_op jit(solution)/shard_map/ppermute | solution.py:22
  33.6 4.4 %collective-permute-start.13 = (bf16[512,128]{1,0:T(8,128)(2,1)S(1)}, bf16[512,128]{1,0:T(8,128)(2,1)S(1)}, u32[]{:S(2)}, u32[]{:S(2)}) collective-permute-start(bf16[512,128]{1,0:T(8,128)(2,1)S(1)} %collective-permute-done.12.refs_2_), channel_id=1, source_target_pairs={{0,1},{1,0},{2,3},{3,2},{4,5},{5,4},{6,7},{7,6},{8,9},{9,8},{10,11... | collective-permute-start | bytes 393224 | tf_op jit(solution)/shard_map/ppermute | solution.py:22
  33.6 9.9 %collective-permute-start.7 = (bf16[512,128]{1,0:T(8,128)(2,1)S(1)}, bf16[512,128]{1,0:T(8,128)(2,1)S(1)}, u32[]{:S(2)}, u32[]{:S(2)}) collective-permute-start(bf16[512,128]{1,0:T(8,128)(2,1)S(1)} %collective-permute-done.6.refs_0_), channel_id=1, source_target_pairs={{0,1},{1,0},{2,3},{3,2},{4,5},{5,4},{6,7},{7,6},{8,9},{9,8},{10,11... | collective-permute-start | bytes 393224 | tf_op jit(solution)/shard_map/ppermute | solution.py:22
  35.8 7.7 %collective-permute-start.9 = (bf16[512,128]{1,0:T(8,128)(2,1)S(1)}, bf16[512,128]{1,0:T(8,128)(2,1)S(1)}, u32[]{:S(2)}, u32[]{:S(2)}) collective-permute-start(bf16[512,128]{1,0:T(8,128)(2,1)S(1)} %collective-permute-done.8.refs_2_), channel_id=1, source_target_pairs={{0,1},{1,0},{2,3},{3,2},{4,5},{5,4},{6,7},{7,6},{8,9},{9,8},{10,11... | collective-permute-start | bytes 393224 | tf_op jit(solution)/shard_map/ppermute | solution.py:22
  41.3 9.6 %collective-permute-start.18 = (bf16[512,128]{1,0:T(8,128)(2,1)S(1)}, bf16[512,128]{1,0:T(8,128)(2,1)S(1)}, u32[]{:S(2)}, u32[]{:S(2)}) collective-permute-start(bf16[512,128]{1,0:T(8,128)(2,1)S(1)} %get-tuple-element.39), channel_id=1, source_target_pairs={{0,4},{1,5},{2,6},{3,7},{4,8},{5,9},{6,10},{7,11},{8,12},{9,13},{1... | collective-permute-start | bytes 393224 | tf_op jit(solution)/shard_map/ppermute | solution.py:22
  46.8 7.6 %collective-permute-start.14 = (bf16[512,128]{1,0:T(8,128)(2,1)S(1)}, bf16[512,128]{1,0:T(8,128)(2,1)S(1)}, u32[]{:S(2)}, u32[]{:S(2)}) collective-permute-start(bf16[512,128]{1,0:T(8,128)(2,1)S(1)} %get-tuple-element.38), channel_id=1, source_target_pairs={{0,4},{1,5},{2,6},{3,7},{4,8},{5,9},{6,10},{7,11},{8,12},{9,13},{1... | collective-permute-start | bytes 393224 | tf_op jit(solution)/shard_map/ppermute | solution.py:22
  50.9 5.2 %collective-permute-start.20 = (bf16[512,128]{1,0:T(8,128)(2,1)S(1)}, bf16[512,128]{1,0:T(8,128)(2,1)S(1)}, u32[]{:S(2)}, u32[]{:S(2)}) collective-permute-start(bf16[512,128]{1,0:T(8,128)(2,1)S(1)} %collective-permute-done.18.refs_0_), channel_id=1, source_target_pairs={{0,2},{1,3},{2,0},{3,1},{4,6},{5,7},{6,4},{7,5},{8,10},{9,11},{10,... | collective-permute-start | bytes 393224 | tf_op jit(solution)/shard_map/ppermute | solution.py:22
  54.4 3.8 %collective-permute-start.16 = (bf16[512,128]{1,0:T(8,128)(2,1)S(1)}, bf16[512,128]{1,0:T(8,128)(2,1)S(1)}, u32[]{:S(2)}, u32[]{:S(2)}) collective-permute-start(bf16[512,128]{1,0:T(8,128)(2,1)S(1)} %collective-permute-done.14.refs_0_), channel_id=1, source_target_pairs={{0,2},{1,3},{2,0},{3,1},{4,6},{5,7},{6,4},{7,5},{8,10},{9,11},{10,... | collective-permute-start | bytes 393224 | tf_op jit(solution)/shard_map/ppermute | solution.py:22
  54.6 5.8 %collective-permute-start.19 = (bf16[512,128]{1,0:T(8,128)(2,1)S(1)}, bf16[512,128]{1,0:T(8,128)(2,1)S(1)}, u32[]{:S(2)}, u32[]{:S(2)}) collective-permute-start(bf16[512,128]{1,0:T(8,128)(2,1)S(1)} %collective-permute-done.18.refs_0_), channel_id=1, source_target_pairs={{0,1},{1,0},{2,3},{3,2},{4,5},{5,4},{6,7},{7,6},{8,9},{9,8},{10,11... | collective-permute-start | bytes 393224 | tf_op jit(solution)/shard_map/ppermute | solution.py:22
  56.0 4.4 %collective-permute-start.21 = (bf16[512,128]{1,0:T(8,128)(2,1)S(1)}, bf16[512,128]{1,0:T(8,128)(2,1)S(1)}, u32[]{:S(2)}, u32[]{:S(2)}) collective-permute-start(bf16[512,128]{1,0:T(8,128)(2,1)S(1)} %collective-permute-done.20.refs_2_), channel_id=1, source_target_pairs={{0,1},{1,0},{2,3},{3,2},{4,5},{5,4},{6,7},{7,6},{8,9},{9,8},{10,11... | collective-permute-start | bytes 393224 | tf_op jit(solution)/shard_map/ppermute | solution.py:22
  56.9 7.5 %collective-permute-start.15 = (bf16[512,128]{1,0:T(8,128)(2,1)S(1)}, bf16[512,128]{1,0:T(8,128)(2,1)S(1)}, u32[]{:S(2)}, u32[]{:S(2)}) collective-permute-start(bf16[512,128]{1,0:T(8,128)(2,1)S(1)} %collective-permute-done.14.refs_0_), channel_id=1, source_target_pairs={{0,1},{1,0},{2,3},{3,2},{4,5},{5,4},{6,7},{7,6},{8,9},{9,8},{10,11... | collective-permute-start | bytes 393224 | tf_op jit(solution)/shard_map/ppermute | solution.py:22
  58.2 6.1 %collective-permute-start.17 = (bf16[512,128]{1,0:T(8,128)(2,1)S(1)}, bf16[512,128]{1,0:T(8,128)(2,1)S(1)}, u32[]{:S(2)}, u32[]{:S(2)}) collective-permute-start(bf16[512,128]{1,0:T(8,128)(2,1)S(1)} %collective-permute-done.16.refs_2_), channel_id=1, source_target_pairs={{0,1},{1,0},{2,3},{3,2},{4,5},{5,4},{6,7},{7,6},{8,9},{9,8},{10,11... | collective-permute-start | bytes 393224 | tf_op jit(solution)/shard_map/ppermute | solution.py:22

commit v3 on v2

v3 whole, which is shorter than its diff:
```python
import functools

import jax
import jax.numpy as jnp
from jax import lax
from jax.experimental import pallas as pl
from jax.experimental.pallas import tpu as pltpu
from jax.sharding import PartitionSpec as P

AXES = ("slab", "sub")
VMEM = pltpu.VMEM
SCOPED = 16 << 20


def permuted(x, slabs, subs, by, flip, ring=False):
    pairs = [
        (s * subs + q, (s + by) % slabs * subs + (q ^ flip))
        for s in range(slabs)
        for q in range(subs)
        if ring or 0 <= s + by < slabs
    ]
    return lax.ppermute(x, AXES, pairs)


def gathered(share, slabs, subs, before=None):
    shares = {0: share}
    bit = subs // 2
    while bit:
        new = {r ^ bit: permuted(shares[r], slabs, subs, 0, bit) for r in shares}
        if before is not None and bit == 2:
            new, before = lax.optimization_barrier((new, before))
        shares.update(new)
        bit //= 2
    return [shares[r] for r in range(subs)], before


def stage_kernel(counts, *refs):
    ins, outs, (token, sems) = (
        refs[: sum(counts)],
        refs[sum(counts) : -2],
        refs[-2:],
    )
    copies, n = [], 0
    for out, count in zip(outs, counts):
        row = 0
        for _ in range(count):
            at = pl.ds(row, ins[n].shape[0])
            copies.append(pltpu.make_async_copy(ins[n], out.at[at, :], sems.at[n]))
            row += ins[n].shape[0]
            n += 1
    for c in copies:
        c.start()
    token[...] = jnp.zeros_like(token)
    for c in copies:
        c.wait()


def staged(*lists):
    counts = [len(arrays) for arrays in lists]
    flat = [a for arrays in lists for a in arrays]
    size = sum(a.size * a.dtype.itemsize for a in flat)
    rows = [sum(a.shape[0] for a in arrays) for arrays in lists]
    n = len(flat)
    return pl.pallas_call(
        functools.partial(stage_kernel, counts),
        out_shape=(
            *(VMEM((r, a[0].shape[1]), a[0].dtype) for r, a in zip(rows, lists)),
            VMEM((8, 128), jnp.float32),
        ),
        in_specs=[pl.BlockSpec(memory_space=pl.ANY)] * n,
        out_specs=(pl.BlockSpec(memory_space=VMEM),) * (len(lists) + 1),
        scratch_shapes=[pltpu.SemaphoreType.DMA((n,))],
        compiler_params=pltpu.CompilerParams(vmem_limit_bytes=SCOPED),
        cost_estimate=pl.CostEstimate(
            flops=0, bytes_accessed=2 * size, transcendentals=0
        ),
        name="stage",
    )(*[pltpu.with_memory_space_constraint(a, pltpu.HBM) for a in flat])


def dot(a, b):
    return jnp.dot(a, b, preferred_element_type=jnp.float32)


def group_kernel(subs, group, masked, *refs):
    shares, (in_idx, out_idx, blocks, sides) = refs[:subs], refs[subs : subs + 4]
    sol_hbm, fsol_hbm, f_ref, inc, val, sol, sem, fsem = refs[-8:]
    links, rows_in = in_idx.shape
    rows_out, out_links = out_idx.shape
    size = blocks.shape[1]
    share, width = shares[0].shape
    inv_at = rows_in * links
    out_at = inv_at + rows_in
    last_at = out_at + rows_out * out_links
    swap = lax.axis_index("sub") * (share // size)
    cols = pl.ds(group * width, width)
    keep = lax.axis_index("slab") > 0
    for r, ref in enumerate(shares):
        value = ref[...]
        if masked:
            value = jnp.where(keep, value, jnp.zeros_like(value))
        inc[pl.ds(r * share, share), :] = value

    def at(i):
        return pl.ds(i * size, size)

    def side(i):
        return sides[at(i), cols].astype(jnp.float32)

    def block(i):
        return blocks[at(i), :]

    def picked(ref, block):
        return ref[pl.ds(pl.multiple_of(block * size, size), size), :]

    def row_of(first, i, source, places):
        n = len(places)
        lhs = [block(first + i * n + k) for k in range(n)]
        rhs = [picked(source, p) for p in places]
        return dot(jnp.concatenate(lhs, axis=1), jnp.concatenate(rhs, axis=0))

    for i in range(rows_in):
        coupled = row_of(0, i, inc, [in_idx[k, i] ^ swap for k in range(links)])
        val[at(i), :] = (side(i) - coupled).astype(val.dtype)
    for i in range(rows_in):
        sol[at(i), :] = dot(block(inv_at + i), val[at(i), :]).astype(sol.dtype)
    first = pltpu.make_async_copy(sol, sol_hbm.at[:, cols], sem)
    first.start()
    for j in range(rows_out):
        outgoing = row_of(out_at, j, sol, [out_idx[j, k] for k in range(out_links)])
        val[at(j), :] = (side(rows_in + j) - outgoing).astype(val.dtype)
    for j in range(rows_out):
        f_ref[at(j), :] = dot(block(last_at + j), val[at(j), :]).astype(f_ref.dtype)
    last = pltpu.make_async_copy(f_ref, fsol_hbm.at[:, cols], fsem)
    last.start()
    first.wait()
    last.wait()


def group_of(shares, in_idx, out_idx, blocks, sides, outs, token, group, masked):
    subs = len(shares)
    share, width = shares[0].shape
    links, rows_in = in_idx.shape
    rows_out, out_links = out_idx.shape
    size = blocks.shape[1]
    rows, front_rows = rows_in * size, rows_out * size
    count = rows_in * (links + 1) + rows_out * (out_links + 1)
    smem = pl.BlockSpec(memory_space=pltpu.SMEM)
    vmem = pl.BlockSpec(memory_space=VMEM)
    hbm = pl.BlockSpec(memory_space=pl.ANY)
    aliased = outs is not None

    def held(arrays):
        return [pltpu.with_memory_space_constraint(a, VMEM) for a in arrays]

    operands = (
        held(shares)
        + [in_idx, out_idx]
        + held([blocks, sides])
        + (list(outs) if aliased else [])
        + ([] if token is None else [token])
    )
    n = len(operands) - (token is not None)
    return pl.pallas_call(
        functools.partial(group_kernel, subs, group, masked),
        out_shape=(
            pltpu.HBM((rows, sides.shape[1]), sides.dtype),
            pltpu.HBM((front_rows, sides.shape[1]), sides.dtype),
            VMEM((front_rows, width), sides.dtype),
        ),
        in_specs=[vmem] * subs + [smem] * 2 + [vmem] * 2
        + [hbm] * (len(operands) - subs - 4),
        out_specs=(hbm, hbm, vmem),
        scratch_shapes=[
            VMEM((subs * share, width), sides.dtype),
            VMEM((rows, width), sides.dtype),
            VMEM((rows, width), sides.dtype),
            pltpu.SemaphoreType.DMA,
            pltpu.SemaphoreType.DMA,
        ],
        input_output_aliases={n - 2: 0, n - 1: 1} if aliased else {},
        compiler_params=pltpu.CompilerParams(vmem_limit_bytes=SCOPED),
        cost_estimate=pl.CostEstimate(
            flops=2 * count * size * size * width,
            bytes_accessed=(count * size * size + 2 * rows * width) * 2,
            transcendentals=0,
        ),
        name=f"group_{group}",
    )(*operands)


def shards(
    right_sides,
    front_sides,
    pending_front,
    inner_index,
    inner_blocks,
    inner_inverse,
    outer_index,
    outer_blocks,
    front_inverse,
):
    slabs, subs = lax.axis_size("slab"), lax.axis_size("sub")
    columns = pending_front.shape[1]
    groups = right_sides.shape[1] // columns
    in_idx, out_idx = inner_index.T, outer_index
    size = inner_inverse.shape[1]
    weights = (inner_blocks, inner_inverse, outer_blocks, front_inverse)
    blocks, sides, token = staged(
        [w.reshape(-1, size) for w in weights], [right_sides, front_sides]
    )
    arrived, token = gathered(pending_front, slabs, subs, token)
    outs = None
    for group in range(groups):
        ring = group + 2 < groups
        *outs, front = group_of(
            arrived,
            in_idx,
            out_idx,
            blocks,
            sides,
            outs,
            token,
            group,
            0 < group and group + 1 < groups,
        )
        if group + 1 < groups:
            hop = permuted(front, slabs, subs, 1, 0, ring)
            arrived, token = gathered(hop, slabs, subs)
    return tuple(outs)


def solution(mesh):
    rows = P(("slab", "sub"), None)
    blocks = P(("slab", "sub"), None, None)
    links = P(("slab", "sub"), None, None, None)
    return jax.shard_map(
        shards,
        mesh=mesh,
        in_specs=(rows, rows, rows, rows, links, blocks, rows, links, blocks),
        out_specs=(rows, rows),
        check_vma=False,
    )
```

time: 68.5 us -> 60.9 us (0.89)
  waiting for transfers between devices: 12.2 us -> 31 us
  starting transfers between devices: 29.3 us -> 14.1 us
  Pallas kernels: 24.2 us -> 14.9 us
  local copies, waits for them, and re-layouts: 1.75 us -> 0.01 us
    ppermute x22 -> x11, waiting for transfers between devices: 12.2 us -> 31 us  [permuted(): return lax.ppermute(x, AXES, pairs)]
    ppermute x22 -> x11, starting transfers between devices: 29.3 us -> 14.1 us  [permuted(): return lax.ppermute(x, AXES, pairs)]
    pallas_call x7 -> x4, Pallas kernels: 24.2 us -> 14.9 us  [the longest x3 11.3 us: group_of(): pl.pallas_call(functools.partial(group_kernel, subs, group, masked), out_...]
    slice x1 -> x0, local copies, waits for them, and re-layouts: 0.99 us -> none  [shards(): pending_front[:, h * width:(h + 1) * width]]
    unnamed x3 -> x6, local copies, waits for them, and re-layouts: 0.77 us -> 0.01 us
  transfers between devices with their start and end apart: 22 -> 11, of which waited for: 6 -> 8; matrix products, arithmetic and copies ran while one was open for 1% -> 0% of each run, Pallas kernels for 30% -> 6%
where the time goes in v3:
time: 60.9 us; the launch traced here: 60.7 us
  waiting for transfers between devices  31 us (51%)
  Pallas kernels  14.9 us (24%)
  starting transfers between devices  14.1 us (23%)
  between operations  0.68 us (1%)
    ppermute x11, waiting for transfers between devices, permuted(): return lax.ppermute(x, AXES, pairs)  31 us
    ppermute x11, starting transfers between devices, permuted(): return lax.ppermute(x, AXES, pairs)  14.1 us
    pallas_call x3, Pallas kernels, group_of(): pl.pallas_call(functools.partial(group_kernel, subs, group, masked), out_...  11.3 us
    pallas_call x1, Pallas kernels, staged(): pl.pallas_call(functools.partial(stage_kernel, counts), out_shape=(*(VMEM...  3.58 us
  transfers between devices with their start and end apart: 11, of which 8 were waited for; matrix products, arithmetic and copies ran while one was open for 0% of the time, Pallas kernels for 6%

profile of v3, /device:TPU:11, one launch (start us, length us, event | category | flops | bytes accessed | tf_op | source)
XLA Modules:
  0.0 60.7 jit_solution(9960564934399682721)
XLA Ops:
  0.6 0.3 collective-permute-start.1
  1.0 1.0 %collective-permute-start = (bf16[512,256]{1,0:T(8,128)(2,1)}, bf16[512,256]{1,0:T(8,128)(2,1)S(1)}, u32[]{:S(2)}, u32[]{:S(2)}) collective-permute-start(bf16[512,256]{1,0:T(8,128)(2,1)} %refs_0_.1), channel_id=1, source_target_pairs={{0,1},{1,0},{2,3},{3,2},{4,5},{5,4},{6,7},{7,6},{8,9},{9,8},{10,11... | collective-permute-start | bytes 786440 | tf_op jit(solution)/shard_map/ppermute | solution.py:22
  1.9 0.0 copy-start
  1.9 0.0 copy-start.1
  1.9 0.0 copy-start.2
  1.9 3.6 %stage.1 = (bf16[18944,128]{1,0:T(8,128)(2,1)S(1)}, bf16[2560,768]{1,0:T(8,128)(2,1)S(1)}, f32[8,128]{1,0:T(8,128)S(1)}) custom-call(bf16[12288,128]{1,0:T(8,128)(2,1)} %bitcast.8, bf16[2048,128]{1,0:T(8,128)(2,1)} %bitcast.10, bf16[4096,128]{1,0:T(8,128)(2,1)} %bitcast.9, bf16[512,128]{1,0:T(8,128)(2,1)} %bitcast.11, bf16[2048,768]{1,0:T(8,128)(2,1)} %refs_4_.1, ...), custom_call_target="tpu_custom_call" | custom-call | bytes 17563648 | tf_op jit(solution)/shard_map/stage/pallas_call | solution.py:64
  5.5 2.6 %collective-permute-done.1.refs_2_ = bf16[512,256]{1,0:T(8,128)(2,1)S(1)} collective-permute-done((bf16[512,256]{1,0:T(8,128)(2,1)}, bf16[512,256]{1,0:T(8,128)(2,1)S(1)}, u32[]{:S(2)}, u32[]{:S(2)}) %collective-permute-start.1) | collective-permute-done | bytes 262176 | tf_op jit(solution)/shard_map/ppermute | solution.py:22
  8.1 1.5 %collective-permute-start.2 = (bf16[512,256]{1,0:T(8,128)(2,1)S(1)}, bf16[512,256]{1,0:T(8,128)(2,1)S(1)}, u32[]{:S(2)}, u32[]{:S(2)}) collective-permute-start(bf16[512,256]{1,0:T(8,128)(2,1)S(1)} %collective-permute-done.1.refs_2_), channel_id=1, source_target_pairs={{0,1},{1,0},{2,3},{3,2},{4,5},{5,4},{6,7},{7,6},{8,9},{9,8},{10,11... | collective-permute-start | bytes 786440 | tf_op jit(solution)/shard_map/ppermute | solution.py:22
  9.6 0.0 collective-permute-done.refs_1_
  9.6 1.2 %collective-permute-done.2.refs_3_ = bf16[512,256]{1,0:T(8,128)(2,1)S(1)} collective-permute-done((bf16[512,256]{1,0:T(8,128)(2,1)S(1)}, bf16[512,256]{1,0:T(8,128)(2,1)S(1)}, u32[]{:S(2)}, u32[]{:S(2)}) %collective-permute-start.2) | collective-permute-done | bytes 262176 | tf_op jit(solution)/shard_map/ppermute | solution.py:22
  10.8 0.0 copy-done
  10.8 0.0 copy-done.1
  10.8 0.0 copy-done.2
  10.8 3.7 %group_0.1 = (bf16[2048,768]{1,0:T(8,128)(2,1)}, bf16[512,768]{1,0:T(8,128)(2,1)}, bf16[512,256]{1,0:T(8,128)(2,1)S(1)}) custom-call(bf16[512,256]{1,0:T(8,128)(2,1)S(1)} %copy-done, bf16[512,256]{1,0:T(8,128)(2,1)S(1)} %collective-permute-done.refs_1_, bf16[512,256]{1,0:T(8,128)(2,1)S(1)} %collective-permute-done.1.refs_2_, ...), custom_call_target="tpu_custom_call" | custom-call | flops 1241513984 | bytes 6946816 | tf_op jit(solution)/shard_map/group_0/pallas_call | solution.py:164
  14.5 1.3 %collective-permute-start.3 = (bf16[512,256]{1,0:T(8,128)(2,1)S(1)}, bf16[512,256]{1,0:T(8,128)(2,1)S(1)}, u32[]{:S(2)}, u32[]{:S(2)}) collective-permute-start(bf16[512,256]{1,0:T(8,128)(2,1)S(1)} %get-tuple-element.20), channel_id=1, source_target_pairs={{0,4},{1,5},{2,6},{3,7},{4,8},{5,9},{6,10},{7,11},{8,12},{9,13},{1... | collective-permute-start | bytes 786440 | tf_op jit(solution)/shard_map/ppermute | solution.py:22
  15.8 7.2 %collective-permute-done.3.refs_0_ = bf16[512,256]{1,0:T(8,128)(2,1)S(1)} collective-permute-done((bf16[512,256]{1,0:T(8,128)(2,1)S(1)}, bf16[512,256]{1,0:T(8,128)(2,1)S(1)}, u32[]{:S(2)}, u32[]{:S(2)}) %collective-permute-start.3) | collective-permute-done | bytes 262176 | tf_op jit(solution)/shard_map/ppermute | solution.py:22
  23.0 0.2 collective-permute-start.5
  23.2 1.5 %collective-permute-start.4 = (bf16[512,256]{1,0:T(8,128)(2,1)S(1)}, bf16[512,256]{1,0:T(8,128)(2,1)S(1)}, u32[]{:S(2)}, u32[]{:S(2)}) collective-permute-start(bf16[512,256]{1,0:T(8,128)(2,1)S(1)} %collective-permute-done.3.refs_0_), channel_id=1, source_target_pairs={{0,1},{1,0},{2,3},{3,2},{4,5},{5,4},{6,7},{7,6},{8,9},{9,8},{10,11... | collective-permute-start | bytes 786440 | tf_op jit(solution)/shard_map/ppermute | solution.py:22
  24.7 4.9 %collective-permute-done.5.refs_2_ = bf16[512,256]{1,0:T(8,128)(2,1)S(1)} collective-permute-done((bf16[512,256]{1,0:T(8,128)(2,1)S(1)}, bf16[512,256]{1,0:T(8,128)(2,1)S(1)}, u32[]{:S(2)}, u32[]{:S(2)}) %collective-permute-start.5) | collective-permute-done | bytes 262176 | tf_op jit(solution)/shard_map/ppermute | solution.py:22
  29.6 2.1 %collective-permute-start.6 = (bf16[512,256]{1,0:T(8,128)(2,1)S(1)}, bf16[512,256]{1,0:T(8,128)(2,1)S(1)}, u32[]{:S(2)}, u32[]{:S(2)}) collective-permute-start(bf16[512,256]{1,0:T(8,128)(2,1)S(1)} %collective-permute-done.5.refs_2_), channel_id=1, source_target_pairs={{0,1},{1,0},{2,3},{3,2},{4,5},{5,4},{6,7},{7,6},{8,9},{9,8},{10,11... | collective-permute-start | bytes 786440 | tf_op jit(solution)/shard_map/ppermute | solution.py:22
  31.7 0.0 collective-permute-done.4.refs_1_
  31.7 1.2 %collective-permute-done.6.refs_3_ = bf16[512,256]{1,0:T(8,128)(2,1)S(1)} collective-permute-done((bf16[512,256]{1,0:T(8,128)(2,1)S(1)}, bf16[512,256]{1,0:T(8,128)(2,1)S(1)}, u32[]{:S(2)}, u32[]{:S(2)}) %collective-permute-start.6) | collective-permute-done | bytes 262176 | tf_op jit(solution)/shard_map/ppermute | solution.py:22
  32.9 3.5 %group_1.1 = (bf16[2048,768]{1,0:T(8,128)(2,1)}, bf16[512,768]{1,0:T(8,128)(2,1)}, bf16[512,256]{1,0:T(8,128)(2,1)S(1)}) custom-call(bf16[512,256]{1,0:T(8,128)(2,1)S(1)} %collective-permute-done.3.refs_0_, bf16[512,256]{1,0:T(8,128)(2,1)S(1)} %collective-permute-done.4.refs_1_, ...), custom_call_target="tpu_custom_call", output_to_operand_aliasing={{0}: (8, {}), {1}: (9, {})} | custom-call | flops 1241513984 | bytes 6946816 | tf_op jit(solution)/shard_map/group_1/pallas_call | solution.py:164
  36.3 2.2 %collective-permute-start.7 = (bf16[512,256]{1,0:T(8,128)(2,1)S(1)}, bf16[512,256]{1,0:T(8,128)(2,1)S(1)}, u32[]{:S(2)}, u32[]{:S(2)}) collective-permute-start(bf16[512,256]{1,0:T(8,128)(2,1)S(1)} %get-tuple-element.23), channel_id=1, source_target_pairs={{0,4},{1,5},{2,6},{3,7},{4,8},{5,9},{6,10},{7,11},{8,12},{9,13},{1... | collective-permute-start | bytes 786440 | tf_op jit(solution)/shard_map/ppermute | solution.py:22
  38.6 8.1 %collective-permute-done.7.refs_0_ = bf16[512,256]{1,0:T(8,128)(2,1)S(1)} collective-permute-done((bf16[512,256]{1,0:T(8,128)(2,1)S(1)}, bf16[512,256]{1,0:T(8,128)(2,1)S(1)}, u32[]{:S(2)}, u32[]{:S(2)}) %collective-permute-start.7) | collective-permute-done | bytes 262176 | tf_op jit(solution)/shard_map/ppermute | solution.py:22
  46.7 0.2 collective-permute-start.9
  46.9 1.5 %collective-permute-start.8 = (bf16[512,256]{1,0:T(8,128)(2,1)S(1)}, bf16[512,256]{1,0:T(8,128)(2,1)S(1)}, u32[]{:S(2)}, u32[]{:S(2)}) collective-permute-start(bf16[512,256]{1,0:T(8,128)(2,1)S(1)} %collective-permute-done.7.refs_0_), channel_id=1, source_target_pairs={{0,1},{1,0},{2,3},{3,2},{4,5},{5,4},{6,7},{7,6},{8,9},{9,8},{10,11... | collective-permute-start | bytes 786440 | tf_op jit(solution)/shard_map/ppermute | solution.py:22
  48.4 4.9 %collective-permute-done.9.refs_2_ = bf16[512,256]{1,0:T(8,128)(2,1)S(1)} collective-permute-done((bf16[512,256]{1,0:T(8,128)(2,1)S(1)}, bf16[512,256]{1,0:T(8,128)(2,1)S(1)}, u32[]{:S(2)}, u32[]{:S(2)}) %collective-permute-start.9) | collective-permute-done | bytes 262176 | tf_op jit(solution)/shard_map/ppermute | solution.py:22
  53.3 2.1 %collective-permute-start.10 = (bf16[512,256]{1,0:T(8,128)(2,1)S(1)}, bf16[512,256]{1,0:T(8,128)(2,1)S(1)}, u32[]{:S(2)}, u32[]{:S(2)}) collective-permute-start(bf16[512,256]{1,0:T(8,128)(2,1)S(1)} %collective-permute-done.9.refs_2_), channel_id=1, source_target_pairs={{0,1},{1,0},{2,3},{3,2},{4,5},{5,4},{6,7},{7,6},{8,9},{9,8},{10,11... | collective-permute-start | bytes 786440 | tf_op jit(solution)/shard_map/ppermute | solution.py:22
  55.4 0.0 collective-permute-done.8.refs_1_
  55.4 1.2 %collective-permute-done.10.refs_3_ = bf16[512,256]{1,0:T(8,128)(2,1)S(1)} collective-permute-done((bf16[512,256]{1,0:T(8,128)(2,1)S(1)}, bf16[512,256]{1,0:T(8,128)(2,1)S(1)}, u32[]{:S(2)}, u32[]{:S(2)}) %collective-permute-start.10) | collective-permute-done | bytes 262176 | tf_op jit(solution)/shard_map/ppermute | solution.py:22
  56.5 4.2 %group_2.1 = (bf16[2048,768]{1,0:T(8,128)(2,1)}, bf16[512,768]{1,0:T(8,128)(2,1)}, bf16[512,256]{1,0:T(8,128)(2,1)}) custom-call(bf16[512,256]{1,0:T(8,128)(2,1)S(1)} %collective-permute-done.7.refs_0_, bf16[512,256]{1,0:T(8,128)(2,1)S(1)} %collective-permute-done.8.refs_1_, ...), custom_call_target="tpu_custom_call", output_to_operand_aliasing={{0}: (8, {}), {1}: (9, {})} | custom-call | flops 1241513984 | bytes 6946816 | tf_op jit(solution)/shard_map/group_2/pallas_call | solution.py:164
Async XLA Ops:
  0.6 7.5 %collective-permute-start.1 = (bf16[512,256]{1,0:T(8,128)(2,1)}, bf16[512,256]{1,0:T(8,128)(2,1)S(1)}, u32[]{:S(2)}, u32[]{:S(2)}) collective-permute-start(bf16[512,256]{1,0:T(8,128)(2,1)} %refs_0_.1), channel_id=1, source_target_pairs={{0,2},{1,3},{2,0},{3,1},{4,6},{5,7},{6,4},{7,5},{8,10},{9,11},{10,... | collective-permute-start | bytes 786440 | tf_op jit(solution)/shard_map/ppermute | solution.py:22
  1.0 8.7 %collective-permute-start = (bf16[512,256]{1,0:T(8,128)(2,1)}, bf16[512,256]{1,0:T(8,128)(2,1)S(1)}, u32[]{:S(2)}, u32[]{:S(2)}) collective-permute-start(bf16[512,256]{1,0:T(8,128)(2,1)} %refs_0_.1), channel_id=1, source_target_pairs={{0,1},{1,0},{2,3},{3,2},{4,5},{5,4},{6,7},{7,6},{8,9},{9,8},{10,11... | collective-permute-start | bytes 786440 | tf_op jit(solution)/shard_map/ppermute | solution.py:22
  1.9 8.9 %copy-start = (bf16[512,256]{1,0:T(8,128)(2,1)S(1)}, bf16[512,256]{1,0:T(8,128)(2,1)}, u32[]{:S(2)}) copy-start(bf16[512,256]{1,0:T(8,128)(2,1)} %refs_0_.1) | copy-start | bytes 786436
  1.9 8.9 %copy-start.1 = (s32[16,6]{0,1:T(8,128)S(1)}, s32[16,6]{0,1:T(8,128)}, u32[]{:S(2)}) copy-start(s32[16,6]{0,1:T(8,128)} %param.12) | copy-start | bytes 1156
  1.9 8.9 %copy-start.2 = (s32[4,8]{1,0:T(4,128)S(1)}, s32[4,8]{1,0:T(4,128)}, u32[]{:S(2)}) copy-start(s32[4,8]{1,0:T(4,128)} %refs_5_.7) | copy-start | bytes 388
  8.1 2.7 %collective-permute-start.2 = (bf16[512,256]{1,0:T(8,128)(2,1)S(1)}, bf16[512,256]{1,0:T(8,128)(2,1)S(1)}, u32[]{:S(2)}, u32[]{:S(2)}) collective-permute-start(bf16[512,256]{1,0:T(8,128)(2,1)S(1)} %collective-permute-done.1.refs_2_), channel_id=1, source_target_pairs={{0,1},{1,0},{2,3},{3,2},{4,5},{5,4},{6,7},{7,6},{8,9},{9,8},{10,11... | collective-permute-start | bytes 786440 | tf_op jit(solution)/shard_map/ppermute | solution.py:22
  14.5 8.5 %collective-permute-start.3 = (bf16[512,256]{1,0:T(8,128)(2,1)S(1)}, bf16[512,256]{1,0:T(8,128)(2,1)S(1)}, u32[]{:S(2)}, u32[]{:S(2)}) collective-permute-start(bf16[512,256]{1,0:T(8,128)(2,1)S(1)} %get-tuple-element.20), channel_id=1, source_target_pairs={{0,4},{1,5},{2,6},{3,7},{4,8},{5,9},{6,10},{7,11},{8,12},{9,13},{1... | collective-permute-start | bytes 786440 | tf_op jit(solution)/shard_map/ppermute | solution.py:22
  23.0 6.6 %collective-permute-start.5 = (bf16[512,256]{1,0:T(8,128)(2,1)S(1)}, bf16[512,256]{1,0:T(8,128)(2,1)S(1)}, u32[]{:S(2)}, u32[]{:S(2)}) collective-permute-start(bf16[512,256]{1,0:T(8,128)(2,1)S(1)} %collective-permute-done.3.refs_0_), channel_id=1, source_target_pairs={{0,2},{1,3},{2,0},{3,1},{4,6},{5,7},{6,4},{7,5},{8,10},{9,11},{10,... | collective-permute-start | bytes 786440 | tf_op jit(solution)/shard_map/ppermute | solution.py:22
  23.2 8.5 %collective-permute-start.4 = (bf16[512,256]{1,0:T(8,128)(2,1)S(1)}, bf16[512,256]{1,0:T(8,128)(2,1)S(1)}, u32[]{:S(2)}, u32[]{:S(2)}) collective-permute-start(bf16[512,256]{1,0:T(8,128)(2,1)S(1)} %collective-permute-done.3.refs_0_), channel_id=1, source_target_pairs={{0,1},{1,0},{2,3},{3,2},{4,5},{5,4},{6,7},{7,6},{8,9},{9,8},{10,11... | collective-permute-start | bytes 786440 | tf_op jit(solution)/shard_map/ppermute | solution.py:22
  29.6 3.3 %collective-permute-start.6 = (bf16[512,256]{1,0:T(8,128)(2,1)S(1)}, bf16[512,256]{1,0:T(8,128)(2,1)S(1)}, u32[]{:S(2)}, u32[]{:S(2)}) collective-permute-start(bf16[512,256]{1,0:T(8,128)(2,1)S(1)} %collective-permute-done.5.refs_2_), channel_id=1, source_target_pairs={{0,1},{1,0},{2,3},{3,2},{4,5},{5,4},{6,7},{7,6},{8,9},{9,8},{10,11... | collective-permute-start | bytes 786440 | tf_op jit(solution)/shard_map/ppermute | solution.py:22
  36.3 10.3 %collective-permute-start.7 = (bf16[512,256]{1,0:T(8,128)(2,1)S(1)}, bf16[512,256]{1,0:T(8,128)(2,1)S(1)}, u32[]{:S(2)}, u32[]{:S(2)}) collective-permute-start(bf16[512,256]{1,0:T(8,128)(2,1)S(1)} %get-tuple-element.23), channel_id=1, source_target_pairs={{0,4},{1,5},{2,6},{3,7},{4,8},{5,9},{6,10},{7,11},{8,12},{9,13},{1... | collective-permute-start | bytes 786440 | tf_op jit(solution)/shard_map/ppermute | solution.py:22
  46.7 6.6 %collective-permute-start.9 = (bf16[512,256]{1,0:T(8,128)(2,1)S(1)}, bf16[512,256]{1,0:T(8,128)(2,1)S(1)}, u32[]{:S(2)}, u32[]{:S(2)}) collective-permute-start(bf16[512,256]{1,0:T(8,128)(2,1)S(1)} %collective-permute-done.7.refs_0_), channel_id=1, source_target_pairs={{0,2},{1,3},{2,0},{3,1},{4,6},{5,7},{6,4},{7,5},{8,10},{9,11},{10,... | collective-permute-start | bytes 786440 | tf_op jit(solution)/shard_map/ppermute | solution.py:22
  46.9 8.5 %collective-permute-start.8 = (bf16[512,256]{1,0:T(8,128)(2,1)S(1)}, bf16[512,256]{1,0:T(8,128)(2,1)S(1)}, u32[]{:S(2)}, u32[]{:S(2)}) collective-permute-start(bf16[512,256]{1,0:T(8,128)(2,1)S(1)} %collective-permute-done.7.refs_0_), channel_id=1, source_target_pairs={{0,1},{1,0},{2,3},{3,2},{4,5},{5,4},{6,7},{7,6},{8,9},{9,8},{10,11... | collective-permute-start | bytes 786440 | tf_op jit(solution)/shard_map/ppermute | solution.py:22
  53.3 3.3 %collective-permute-start.10 = (bf16[512,256]{1,0:T(8,128)(2,1)S(1)}, bf16[512,256]{1,0:T(8,128)(2,1)S(1)}, u32[]{:S(2)}, u32[]{:S(2)}) collective-permute-start(bf16[512,256]{1,0:T(8,128)(2,1)S(1)} %collective-permute-done.9.refs_2_), channel_id=1, source_target_pairs={{0,1},{1,0},{2,3},{3,2},{4,5},{5,4},{6,7},{7,6},{8,9},{9,8},{10,11... | collective-permute-start | bytes 786440 | tf_op jit(solution)/shard_map/ppermute | solution.py:22

commit v4 on v3

--- a/solution.py
+++ b/solution.py
@@ -82,24 +82,28 @@
     return jnp.dot(a, b, preferred_element_type=jnp.float32)
 
 
-def group_kernel(subs, group, masked, *refs):
-    shares, (in_idx, out_idx, blocks, sides) = refs[:subs], refs[subs : subs + 4]
-    sol_hbm, fsol_hbm, f_ref, inc, val, sol, sem, fsem = refs[-8:]
+def group_kernel(count, group, masked, chunks, *refs):
+    shares, (in_idx, out_idx, blocks, sides) = refs[:count], refs[count : count + 4]
+    (sol_hbm, fsol_hbm), (inc, val, sol, sem, fsem) = (
+        refs[-7 - chunks : -5 - chunks],
+        refs[-5:],
+    )
+    f_refs = refs[-5 - chunks : -5]
     links, rows_in = in_idx.shape
     rows_out, out_links = out_idx.shape
     size = blocks.shape[1]
-    share, width = shares[0].shape
+    part, width = shares[0].shape
     inv_at = rows_in * links
     out_at = inv_at + rows_in
     last_at = out_at + rows_out * out_links
-    swap = lax.axis_index("sub") * (share // size)
+    swap = lax.axis_index("sub") * rows_out
     cols = pl.ds(group * width, width)
     keep = lax.axis_index("slab") > 0
     for r, ref in enumerate(shares):
         value = ref[...]
         if masked:
             value = jnp.where(keep, value, jnp.zeros_like(value))
-        inc[pl.ds(r * share, share), :] = value
+        inc[pl.ds(r * part, part), :] = value
 
     def at(i):
         return pl.ds(i * size, size)
@@ -129,21 +133,29 @@
     for j in range(rows_out):
         outgoing = row_of(out_at, j, sol, [out_idx[j, k] for k in range(out_links)])
         val[at(j), :] = (side(rows_in + j) - outgoing).astype(val.dtype)
-    for j in range(rows_out):
-        f_ref[at(j), :] = dot(block(last_at + j), val[at(j), :]).astype(f_ref.dtype)
-    last = pltpu.make_async_copy(f_ref, fsol_hbm.at[:, cols], fsem)
-    last.start()
-    first.wait()
-    last.wait()
+    each = rows_out // chunks
+    copies = [first]
+    for c, f_ref in enumerate(f_refs):
+        for j in range(each):
+            row = c * each + j
+            f_ref[at(j), :] = dot(block(last_at + row), val[at(row), :]).astype(
+                f_ref.dtype
+            )
+        there = fsol_hbm.at[pl.ds(c * each * size, each * size), cols]
+        copies.append(pltpu.make_async_copy(f_ref, there, fsem.at[c]))
+        copies[-1].start()
+    for c in copies:
+        c.wait()
 
 
 def group_of(shares, in_idx, out_idx, blocks, sides, outs, token, group, masked):
-    subs = len(shares)
-    share, width = shares[0].shape
+    width = shares[0].shape[1]
     links, rows_in = in_idx.shape
     rows_out, out_links = out_idx.shape
     size = blocks.shape[1]
     rows, front_rows = rows_in * size, rows_out * size
+    chunks = 2 if rows_out % 2 == 0 else 1
+    pieces = len(shares)
     count = rows_in * (links + 1) + rows_out * (out_links + 1)
     smem = pl.BlockSpec(memory_space=pltpu.SMEM)
     vmem = pl.BlockSpec(memory_space=VMEM)
@@ -162,21 +174,21 @@
     )
     n = len(operands) - (token is not None)
     return pl.pallas_call(
-        functools.partial(group_kernel, subs, group, masked),
+        functools.partial(group_kernel, pieces, group, masked, chunks),
         out_shape=(
             pltpu.HBM((rows, sides.shape[1]), sides.dtype),
             pltpu.HBM((front_rows, sides.shape[1]), sides.dtype),
-            VMEM((front_rows, width), sides.dtype),
-        ),
-        in_specs=[vmem] * subs + [smem] * 2 + [vmem] * 2
-        + [hbm] * (len(operands) - subs - 4),
-        out_specs=(hbm, hbm, vmem),
+            *[VMEM((front_rows // chunks, width), sides.dtype)] * chunks,
+        ),
+        in_specs=[vmem] * pieces + [smem] * 2 + [vmem] * 2
+        + [hbm] * (len(operands) - pieces - 4),
+        out_specs=(hbm, hbm, *[vmem] * chunks),
         scratch_shapes=[
-            VMEM((subs * share, width), sides.dtype),
+            VMEM((sum(a.shape[0] for a in shares), width), sides.dtype),
             VMEM((rows, width), sides.dtype),
             VMEM((rows, width), sides.dtype),
             pltpu.SemaphoreType.DMA,
-            pltpu.SemaphoreType.DMA,
+            pltpu.SemaphoreType.DMA((chunks,)),
         ],
         input_output_aliases={n - 2: 0, n - 1: 1} if aliased else {},
         compiler_params=pltpu.CompilerParams(vmem_limit_bytes=SCOPED),
@@ -213,7 +225,7 @@
     outs = None
     for group in range(groups):
         ring = group + 2 < groups
-        *outs, front = group_of(
+        made = group_of(
             arrived,
             in_idx,
             out_idx,
@@ -224,9 +236,11 @@
             group,
             0 < group and group + 1 < groups,
         )
+        outs, fronts = made[:2], made[2:]
         if group + 1 < groups:
-            hop = permuted(front, slabs, subs, 1, 0, ring)
-            arrived, token = gathered(hop, slabs, subs)
+            hops = [permuted(f, slabs, subs, 1, 0, ring) for f in fronts]
+            chunks, token = [gathered(hop, slabs, subs)[0] for hop in hops], None
+            arrived = [c[r] for r in range(subs) for c in chunks]
     return tuple(outs)
 
 

time: 60.9 us -> 56.7 us (0.931)
  waiting for transfers between devices: 31 us -> 16.6 us
  starting transfers between devices: 14.1 us -> 24.3 us
    ppermute x11 -> x19, waiting for transfers between devices: 31 us -> 16.6 us  [permuted(): return lax.ppermute(x, AXES, pairs)]
    ppermute x11 -> x19, starting transfers between devices: 14.1 us -> 24.3 us  [permuted(): return lax.ppermute(x, AXES, pairs)]
  transfers between devices with their start and end apart: 11 -> 19, of which waited for: 8 -> 10; matrix products, arithmetic and copies ran while one was open for 0% -> 0% of each run, Pallas kernels for 6% -> 6%
where the time goes in v4:
time: 56.7 us; the launch traced here: 56.5 us
  starting transfers between devices  24.3 us (43%)
  waiting for transfers between devices  16.6 us (29%)
  Pallas kernels  14.9 us (26%)
  between operations  0.7 us (1%)
    ppermute x19, starting transfers between devices, permuted(): return lax.ppermute(x, AXES, pairs)  24.3 us
    ppermute x19, waiting for transfers between devices, permuted(): return lax.ppermute(x, AXES, pairs)  16.6 us
    pallas_call x3, Pallas kernels, group_of(): pl.pallas_call(functools.partial(group_kernel, pieces, group, masked, chu...  11.3 us
    pallas_call x1, Pallas kernels, staged(): pl.pallas_call(functools.partial(stage_kernel, counts), out_shape=(*(VMEM...  3.58 us
  transfers between devices with their start and end apart: 19, of which 10 were waited for; matrix products, arithmetic and copies ran while one was open for 0% of the time, Pallas kernels for 6%

profile of v4, /device:TPU:11, one launch (start us, length us, event | category | flops | bytes accessed | tf_op | source)
XLA Modules:
  0.0 56.5 jit_solution(12976408121385582094)
XLA Ops:
  0.6 0.3 collective-permute-start.1
  1.0 1.0 %collective-permute-start = (bf16[512,256]{1,0:T(8,128)(2,1)}, bf16[512,256]{1,0:T(8,128)(2,1)S(1)}, u32[]{:S(2)}, u32[]{:S(2)}) collective-permute-start(bf16[512,256]{1,0:T(8,128)(2,1)} %refs_0_.1), channel_id=1, source_target_pairs={{0,1},{1,0},{2,3},{3,2},{4,5},{5,4},{6,7},{7,6},{8,9},{9,8},{10,11... | collective-permute-start | bytes 786440 | tf_op jit(solution)/shard_map/ppermute | solution.py:22
  1.9 0.0 copy-start
  1.9 0.0 copy-start.1
  1.9 0.0 copy-start.2
  1.9 3.6 %stage.1 = (bf16[18944,128]{1,0:T(8,128)(2,1)S(1)}, bf16[2560,768]{1,0:T(8,128)(2,1)S(1)}, f32[8,128]{1,0:T(8,128)S(1)}) custom-call(bf16[12288,128]{1,0:T(8,128)(2,1)} %bitcast.8, bf16[2048,128]{1,0:T(8,128)(2,1)} %bitcast.10, bf16[4096,128]{1,0:T(8,128)(2,1)} %bitcast.9, bf16[512,128]{1,0:T(8,128)(2,1)} %bitcast.11, bf16[2048,768]{1,0:T(8,128)(2,1)} %refs_4_.1, ...), custom_call_target="tpu_custom_call" | custom-call | bytes 17563648 | tf_op jit(solution)/shard_map/stage/pallas_call | solution.py:64
  5.5 2.6 %collective-permute-done.1.refs_2_ = bf16[512,256]{1,0:T(8,128)(2,1)S(1)} collective-permute-done((bf16[512,256]{1,0:T(8,128)(2,1)}, bf16[512,256]{1,0:T(8,128)(2,1)S(1)}, u32[]{:S(2)}, u32[]{:S(2)}) %collective-permute-start.1) | collective-permute-done | bytes 262176 | tf_op jit(solution)/shard_map/ppermute | solution.py:22
  8.1 1.5 %collective-permute-start.2 = (bf16[512,256]{1,0:T(8,128)(2,1)S(1)}, bf16[512,256]{1,0:T(8,128)(2,1)S(1)}, u32[]{:S(2)}, u32[]{:S(2)}) collective-permute-start(bf16[512,256]{1,0:T(8,128)(2,1)S(1)} %collective-permute-done.1.refs_2_), channel_id=1, source_target_pairs={{0,1},{1,0},{2,3},{3,2},{4,5},{5,4},{6,7},{7,6},{8,9},{9,8},{10,11... | collective-permute-start | bytes 786440 | tf_op jit(solution)/shard_map/ppermute | solution.py:22
  9.6 0.0 collective-permute-done.refs_1_
  9.6 1.2 %collective-permute-done.2.refs_3_ = bf16[512,256]{1,0:T(8,128)(2,1)S(1)} collective-permute-done((bf16[512,256]{1,0:T(8,128)(2,1)S(1)}, bf16[512,256]{1,0:T(8,128)(2,1)S(1)}, u32[]{:S(2)}, u32[]{:S(2)}) %collective-permute-start.2) | collective-permute-done | bytes 262176 | tf_op jit(solution)/shard_map/ppermute | solution.py:22
  10.8 0.0 copy-done
  10.8 0.0 copy-done.1
  10.8 0.0 copy-done.2
  10.8 3.5 %group_0.1 = (bf16[2048,768]{1,0:T(8,128)(2,1)}, bf16[512,768]{1,0:T(8,128)(2,1)}, bf16[256,256]{1,0:T(8,128)(2,1)S(1)}, bf16[256,256]{1,0:T(8,128)(2,1)S(1)}) custom-call(bf16[512,256]{1,0:T(8,128)(2,1)S(1)} %copy-done, bf16[512,256]{1,0:T(8,128)(2,1)S(1)} %collective-permute-done.refs_1_, bf16[512,256]{1,0:T(8,128)(2,1)S(1)} %collective-permute-done.1.refs_2_, ...), custom_call_target="tpu_custom_call" | custom-call | flops 1241513984 | bytes 6946816 | tf_op jit(solution)/shard_map/group_0/pallas_call | solution.py:176
  14.3 1.3 %collective-permute-start.3 = (bf16[256,256]{1,0:T(8,128)(2,1)S(1)}, bf16[256,256]{1,0:T(8,128)(2,1)S(1)}, u32[]{:S(2)}, u32[]{:S(2)}) collective-permute-start(bf16[256,256]{1,0:T(8,128)(2,1)S(1)} %get-tuple-element.22), channel_id=1, source_target_pairs={{0,4},{1,5},{2,6},{3,7},{4,8},{5,9},{6,10},{7,11},{8,12},{9,13},{1... | collective-permute-start | bytes 393224 | tf_op jit(solution)/shard_map/ppermute | solution.py:22
  15.6 1.2 %collective-permute-start.4 = (bf16[256,256]{1,0:T(8,128)(2,1)S(1)}, bf16[256,256]{1,0:T(8,128)(2,1)S(1)}, u32[]{:S(2)}, u32[]{:S(2)}) collective-permute-start(bf16[256,256]{1,0:T(8,128)(2,1)S(1)} %get-tuple-element.23), channel_id=1, source_target_pairs={{0,4},{1,5},{2,6},{3,7},{4,8},{5,9},{6,10},{7,11},{8,12},{9,13},{1... | collective-permute-start | bytes 393224 | tf_op jit(solution)/shard_map/ppermute | solution.py:22
  16.8 3.1 %collective-permute-done.3.refs_0_ = bf16[256,256]{1,0:T(8,128)(2,1)S(1)} collective-permute-done((bf16[256,256]{1,0:T(8,128)(2,1)S(1)}, bf16[256,256]{1,0:T(8,128)(2,1)S(1)}, u32[]{:S(2)}, u32[]{:S(2)}) %collective-permute-start.3) | collective-permute-done | bytes 131104 | tf_op jit(solution)/shard_map/ppermute | solution.py:22
  19.9 0.2 collective-permute-start.7
  20.2 2.6 %collective-permute-done.4.refs_1_ = bf16[256,256]{1,0:T(8,128)(2,1)S(1)} collective-permute-done((bf16[256,256]{1,0:T(8,128)(2,1)S(1)}, bf16[256,256]{1,0:T(8,128)(2,1)S(1)}, u32[]{:S(2)}, u32[]{:S(2)}) %collective-permute-start.4) | collective-permute-done | bytes 131104 | tf_op jit(solution)/shard_map/ppermute | solution.py:22
  22.7 0.2 collective-permute-start.8
  23.0 1.5 %collective-permute-start.5 = (bf16[256,256]{1,0:T(8,128)(2,1)S(1)}, bf16[256,256]{1,0:T(8,128)(2,1)S(1)}, u32[]{:S(2)}, u32[]{:S(2)}) collective-permute-start(bf16[256,256]{1,0:T(8,128)(2,1)S(1)} %collective-permute-done.3.refs_0_), channel_id=1, source_target_pairs={{0,1},{1,0},{2,3},{3,2},{4,5},{5,4},{6,7},{7,6},{8,9},{9,8},{10,11... | collective-permute-start | bytes 393224 | tf_op jit(solution)/shard_map/ppermute | solution.py:22
  24.5 0.0 collective-permute-start.6
  24.5 0.0 collective-permute-done.7.refs_4_
  24.5 3.5 %collective-permute-start.9 = (bf16[256,256]{1,0:T(8,128)(2,1)S(1)}, bf16[256,256]{1,0:T(8,128)(2,1)S(1)}, u32[]{:S(2)}, u32[]{:S(2)}) collective-permute-start(bf16[256,256]{1,0:T(8,128)(2,1)S(1)} %collective-permute-done.7.refs_4_), channel_id=1, source_target_pairs={{0,1},{1,0},{2,3},{3,2},{4,5},{5,4},{6,7},{7,6},{8,9},{9,8},{10,11... | collective-permute-start | bytes 393224 | tf_op jit(solution)/shard_map/ppermute | solution.py:22
  28.0 0.3 collective-permute-done.8.refs_5_
  28.3 1.5 %collective-permute-start.10 = (bf16[256,256]{1,0:T(8,128)(2,1)S(1)}, bf16[256,256]{1,0:T(8,128)(2,1)S(1)}, u32[]{:S(2)}, u32[]{:S(2)}) collective-permute-start(bf16[256,256]{1,0:T(8,128)(2,1)S(1)} %collective-permute-done.8.refs_5_), channel_id=1, source_target_pairs={{0,1},{1,0},{2,3},{3,2},{4,5},{5,4},{6,7},{7,6},{8,9},{9,8},{10,11... | collective-permute-start | bytes 393224 | tf_op jit(solution)/shard_map/ppermute | solution.py:22
  29.7 0.0 collective-permute-done.5.refs_2_
  29.7 0.0 collective-permute-done.6.refs_3_
  29.7 0.0 collective-permute-done.9.refs_6_
  29.7 1.0 %collective-permute-done.10.refs_7_ = bf16[256,256]{1,0:T(8,128)(2,1)S(1)} collective-permute-done((bf16[256,256]{1,0:T(8,128)(2,1)S(1)}, bf16[256,256]{1,0:T(8,128)(2,1)S(1)}, u32[]{:S(2)}, u32[]{:S(2)}) %collective-permute-start.10) | collective-permute-done | bytes 131104 | tf_op jit(solution)/shard_map/ppermute | solution.py:22
  30.7 3.6 %group_1.1 = (bf16[2048,768]{1,0:T(8,128)(2,1)}, bf16[512,768]{1,0:T(8,128)(2,1)}, bf16[256,256]{1,0:T(8,128)(2,1)S(1)}, bf16[256,256]{1,0:T(8,128)(2,1)S(1)}) custom-call(bf16[256,256]{1,0:T(8,128)(2,1)S(1)} %collective-permute-done.3.refs_0_, bf16[256,256]{1,0:T(8,128)(2,1)S(1)} %collective-permute-done.4.refs_1_, ...), custom_call_target="tpu_custom_call", output_to_operand_aliasing={{0}: (12, {}), {1}: (13, {})} | custom-call | flops 1241513984 | bytes 6946816 | tf_op jit(solution)/shard_map/group_1/pallas_call | solution.py:176
  34.4 2.2 %collective-permute-start.11 = (bf16[256,256]{1,0:T(8,128)(2,1)S(1)}, bf16[256,256]{1,0:T(8,128)(2,1)S(1)}, u32[]{:S(2)}, u32[]{:S(2)}) collective-permute-start(bf16[256,256]{1,0:T(8,128)(2,1)S(1)} %get-tuple-element.26), channel_id=1, source_target_pairs={{0,4},{1,5},{2,6},{3,7},{4,8},{5,9},{6,10},{7,11},{8,12},{9,13},{1... | collective-permute-start | bytes 393224 | tf_op jit(solution)/shard_map/ppermute | solution.py:22
  36.6 4.0 %collective-permute-start.12 = (bf16[256,256]{1,0:T(8,128)(2,1)S(1)}, bf16[256,256]{1,0:T(8,128)(2,1)S(1)}, u32[]{:S(2)}, u32[]{:S(2)}) collective-permute-start(bf16[256,256]{1,0:T(8,128)(2,1)S(1)} %get-tuple-element.27), channel_id=1, source_target_pairs={{0,4},{1,5},{2,6},{3,7},{4,8},{5,9},{6,10},{7,11},{8,12},{9,13},{1... | collective-permute-start | bytes 393224 | tf_op jit(solution)/shard_map/ppermute | solution.py:22
  40.7 1.2 %collective-permute-done.11.refs_0_ = bf16[256,256]{1,0:T(8,128)(2,1)S(1)} collective-permute-done((bf16[256,256]{1,0:T(8,128)(2,1)S(1)}, bf16[256,256]{1,0:T(8,128)(2,1)S(1)}, u32[]{:S(2)}, u32[]{:S(2)}) %collective-permute-start.11) | collective-permute-done | bytes 131104 | tf_op jit(solution)/shard_map/ppermute | solution.py:22
  41.9 0.3 collective-permute-start.15
  42.1 2.8 %collective-permute-done.12.refs_1_ = bf16[256,256]{1,0:T(8,128)(2,1)S(1)} collective-permute-done((bf16[256,256]{1,0:T(8,128)(2,1)S(1)}, bf16[256,256]{1,0:T(8,128)(2,1)S(1)}, u32[]{:S(2)}, u32[]{:S(2)}) %collective-permute-start.12) | collective-permute-done | bytes 131104 | tf_op jit(solution)/shard_map/ppermute | solution.py:22
  44.9 0.2 collective-permute-start.16
  45.2 1.2 %collective-permute-start.13 = (bf16[256,256]{1,0:T(8,128)(2,1)S(1)}, bf16[256,256]{1,0:T(8,128)(2,1)S(1)}, u32[]{:S(2)}, u32[]{:S(2)}) collective-permute-start(bf16[256,256]{1,0:T(8,128)(2,1)S(1)} %collective-permute-done.11.refs_0_), channel_id=1, source_target_pairs={{0,1},{1,0},{2,3},{3,2},{4,5},{5,4},{6,7},{7,6},{8,9},{9,8},{10,11... | collective-permute-start | bytes 393224 | tf_op jit(solution)/shard_map/ppermute | solution.py:22
  46.4 0.0 collective-permute-start.14
  46.4 0.0 collective-permute-done.15.refs_4_
  46.4 2.6 %collective-permute-start.17 = (bf16[256,256]{1,0:T(8,128)(2,1)S(1)}, bf16[256,256]{1,0:T(8,128)(2,1)S(1)}, u32[]{:S(2)}, u32[]{:S(2)}) collective-permute-start(bf16[256,256]{1,0:T(8,128)(2,1)S(1)} %collective-permute-done.15.refs_4_), channel_id=1, source_target_pairs={{0,1},{1,0},{2,3},{3,2},{4,5},{5,4},{6,7},{7,6},{8,9},{9,8},{10,11... | collective-permute-start | bytes 393224 | tf_op jit(solution)/shard_map/ppermute | solution.py:22
  49.0 0.9 %collective-permute-done.16.refs_5_ = bf16[256,256]{1,0:T(8,128)(2,1)S(1)} collective-permute-done((bf16[256,256]{1,0:T(8,128)(2,1)S(1)}, bf16[256,256]{1,0:T(8,128)(2,1)S(1)}, u32[]{:S(2)}, u32[]{:S(2)}) %collective-permute-start.16) | collective-permute-done | bytes 131104 | tf_op jit(solution)/shard_map/ppermute | solution.py:22
  50.0 1.4 %collective-permute-start.18 = (bf16[256,256]{1,0:T(8,128)(2,1)S(1)}, bf16[256,256]{1,0:T(8,128)(2,1)S(1)}, u32[]{:S(2)}, u32[]{:S(2)}) collective-permute-start(bf16[256,256]{1,0:T(8,128)(2,1)S(1)} %collective-permute-done.16.refs_5_), channel_id=1, source_target_pairs={{0,1},{1,0},{2,3},{3,2},{4,5},{5,4},{6,7},{7,6},{8,9},{9,8},{10,11... | collective-permute-start | bytes 393224 | tf_op jit(solution)/shard_map/ppermute | solution.py:22
  51.3 0.0 collective-permute-done.13.refs_2_
  51.3 0.0 collective-permute-done.14.refs_3_
  51.3 0.0 collective-permute-done.17.refs_6_
  51.4 1.0 %collective-permute-done.18.refs_7_ = bf16[256,256]{1,0:T(8,128)(2,1)S(1)} collective-permute-done((bf16[256,256]{1,0:T(8,128)(2,1)S(1)}, bf16[256,256]{1,0:T(8,128)(2,1)S(1)}, u32[]{:S(2)}, u32[]{:S(2)}) %collective-permute-start.18) | collective-permute-done | bytes 131104 | tf_op jit(solution)/shard_map/ppermute | solution.py:22
  52.3 4.2 %group_2.1 = (bf16[2048,768]{1,0:T(8,128)(2,1)}, bf16[512,768]{1,0:T(8,128)(2,1)}, bf16[256,256]{1,0:T(8,128)(2,1)}, bf16[256,256]{1,0:T(8,128)(2,1)}) custom-call(bf16[256,256]{1,0:T(8,128)(2,1)S(1)} %collective-permute-done.11.refs_0_, bf16[256,256]{1,0:T(8,128)(2,1)S(1)} %collective-permute-done.12.refs_1_, ...), custom_call_target="tpu_custom_call", output_to_operand_aliasing={{0}: (12, {}), {1}: (13, {})} | custom-call | flops 1241513984 | bytes 6946816 | tf_op jit(solution)/shard_map/group_2/pallas_call | solution.py:176
Async XLA Ops:
  0.6 7.5 %collective-permute-start.1 = (bf16[512,256]{1,0:T(8,128)(2,1)}, bf16[512,256]{1,0:T(8,128)(2,1)S(1)}, u32[]{:S(2)}, u32[]{:S(2)}) collective-permute-start(bf16[512,256]{1,0:T(8,128)(2,1)} %refs_0_.1), channel_id=1, source_target_pairs={{0,2},{1,3},{2,0},{3,1},{4,6},{5,7},{6,4},{7,5},{8,10},{9,11},{10,... | collective-permute-start | bytes 786440 | tf_op jit(solution)/shard_map/ppermute | solution.py:22
  1.0 8.7 %collective-permute-start = (bf16[512,256]{1,0:T(8,128)(2,1)}, bf16[512,256]{1,0:T(8,128)(2,1)S(1)}, u32[]{:S(2)}, u32[]{:S(2)}) collective-permute-start(bf16[512,256]{1,0:T(8,128)(2,1)} %refs_0_.1), channel_id=1, source_target_pairs={{0,1},{1,0},{2,3},{3,2},{4,5},{5,4},{6,7},{7,6},{8,9},{9,8},{10,11... | collective-permute-start | bytes 786440 | tf_op jit(solution)/shard_map/ppermute | solution.py:22
  1.9 8.9 %copy-start = (bf16[512,256]{1,0:T(8,128)(2,1)S(1)}, bf16[512,256]{1,0:T(8,128)(2,1)}, u32[]{:S(2)}) copy-start(bf16[512,256]{1,0:T(8,128)(2,1)} %refs_0_.1) | copy-start | bytes 786436
  1.9 8.9 %copy-start.1 = (s32[16,6]{0,1:T(8,128)S(1)}, s32[16,6]{0,1:T(8,128)}, u32[]{:S(2)}) copy-start(s32[16,6]{0,1:T(8,128)} %param.12) | copy-start | bytes 1156
  1.9 8.9 %copy-start.2 = (s32[4,8]{1,0:T(4,128)S(1)}, s32[4,8]{1,0:T(4,128)}, u32[]{:S(2)}) copy-start(s32[4,8]{1,0:T(4,128)} %refs_9_.3) | copy-start | bytes 388
  8.1 2.7 %collective-permute-start.2 = (bf16[512,256]{1,0:T(8,128)(2,1)S(1)}, bf16[512,256]{1,0:T(8,128)(2,1)S(1)}, u32[]{:S(2)}, u32[]{:S(2)}) collective-permute-start(bf16[512,256]{1,0:T(8,128)(2,1)S(1)} %collective-permute-done.1.refs_2_), channel_id=1, source_target_pairs={{0,1},{1,0},{2,3},{3,2},{4,5},{5,4},{6,7},{7,6},{8,9},{9,8},{10,11... | collective-permute-start | bytes 786440 | tf_op jit(solution)/shard_map/ppermute | solution.py:22
  14.3 5.7 %collective-permute-start.3 = (bf16[256,256]{1,0:T(8,128)(2,1)S(1)}, bf16[256,256]{1,0:T(8,128)(2,1)S(1)}, u32[]{:S(2)}, u32[]{:S(2)}) collective-permute-start(bf16[256,256]{1,0:T(8,128)(2,1)S(1)} %get-tuple-element.22), channel_id=1, source_target_pairs={{0,4},{1,5},{2,6},{3,7},{4,8},{5,9},{6,10},{7,11},{8,12},{9,13},{1... | collective-permute-start | bytes 393224 | tf_op jit(solution)/shard_map/ppermute | solution.py:22
  15.6 7.2 %collective-permute-start.4 = (bf16[256,256]{1,0:T(8,128)(2,1)S(1)}, bf16[256,256]{1,0:T(8,128)(2,1)S(1)}, u32[]{:S(2)}, u32[]{:S(2)}) collective-permute-start(bf16[256,256]{1,0:T(8,128)(2,1)S(1)} %get-tuple-element.23), channel_id=1, source_target_pairs={{0,4},{1,5},{2,6},{3,7},{4,8},{5,9},{6,10},{7,11},{8,12},{9,13},{1... | collective-permute-start | bytes 393224 | tf_op jit(solution)/shard_map/ppermute | solution.py:22
  19.9 4.6 %collective-permute-start.7 = (bf16[256,256]{1,0:T(8,128)(2,1)S(1)}, bf16[256,256]{1,0:T(8,128)(2,1)S(1)}, u32[]{:S(2)}, u32[]{:S(2)}) collective-permute-start(bf16[256,256]{1,0:T(8,128)(2,1)S(1)} %collective-permute-done.3.refs_0_), channel_id=1, source_target_pairs={{0,2},{1,3},{2,0},{3,1},{4,6},{5,7},{6,4},{7,5},{8,10},{9,11},{10,... | collective-permute-start | bytes 393224 | tf_op jit(solution)/shard_map/ppermute | solution.py:22
  22.7 5.5 %collective-permute-start.8 = (bf16[256,256]{1,0:T(8,128)(2,1)S(1)}, bf16[256,256]{1,0:T(8,128)(2,1)S(1)}, u32[]{:S(2)}, u32[]{:S(2)}) collective-permute-start(bf16[256,256]{1,0:T(8,128)(2,1)S(1)} %collective-permute-done.4.refs_1_), channel_id=1, source_target_pairs={{0,2},{1,3},{2,0},{3,1},{4,6},{5,7},{6,4},{7,5},{8,10},{9,11},{10,... | collective-permute-start | bytes 393224 | tf_op jit(solution)/shard_map/ppermute | solution.py:22
  23.0 6.7 %collective-permute-start.5 = (bf16[256,256]{1,0:T(8,128)(2,1)S(1)}, bf16[256,256]{1,0:T(8,128)(2,1)S(1)}, u32[]{:S(2)}, u32[]{:S(2)}) collective-permute-start(bf16[256,256]{1,0:T(8,128)(2,1)S(1)} %collective-permute-done.3.refs_0_), channel_id=1, source_target_pairs={{0,1},{1,0},{2,3},{3,2},{4,5},{5,4},{6,7},{7,6},{8,9},{9,8},{10,11... | collective-permute-start | bytes 393224 | tf_op jit(solution)/shard_map/ppermute | solution.py:22
  24.5 5.3 %collective-permute-start.6 = (bf16[256,256]{1,0:T(8,128)(2,1)S(1)}, bf16[256,256]{1,0:T(8,128)(2,1)S(1)}, u32[]{:S(2)}, u32[]{:S(2)}) collective-permute-start(bf16[256,256]{1,0:T(8,128)(2,1)S(1)} %collective-permute-done.4.refs_1_), channel_id=1, source_target_pairs={{0,1},{1,0},{2,3},{3,2},{4,5},{5,4},{6,7},{7,6},{8,9},{9,8},{10,11... | collective-permute-start | bytes 393224 | tf_op jit(solution)/shard_map/ppermute | solution.py:22
  24.5 5.2 %collective-permute-start.9 = (bf16[256,256]{1,0:T(8,128)(2,1)S(1)}, bf16[256,256]{1,0:T(8,128)(2,1)S(1)}, u32[]{:S(2)}, u32[]{:S(2)}) collective-permute-start(bf16[256,256]{1,0:T(8,128)(2,1)S(1)} %collective-permute-done.7.refs_4_), channel_id=1, source_target_pairs={{0,1},{1,0},{2,3},{3,2},{4,5},{5,4},{6,7},{7,6},{8,9},{9,8},{10,11... | collective-permute-start | bytes 393224 | tf_op jit(solution)/shard_map/ppermute | solution.py:22
  28.3 2.5 %collective-permute-start.10 = (bf16[256,256]{1,0:T(8,128)(2,1)S(1)}, bf16[256,256]{1,0:T(8,128)(2,1)S(1)}, u32[]{:S(2)}, u32[]{:S(2)}) collective-permute-start(bf16[256,256]{1,0:T(8,128)(2,1)S(1)} %collective-permute-done.8.refs_5_), channel_id=1, source_target_pairs={{0,1},{1,0},{2,3},{3,2},{4,5},{5,4},{6,7},{7,6},{8,9},{9,8},{10,11... | collective-permute-start | bytes 393224 | tf_op jit(solution)/shard_map/ppermute | solution.py:22
  34.4 7.5 %collective-permute-start.11 = (bf16[256,256]{1,0:T(8,128)(2,1)S(1)}, bf16[256,256]{1,0:T(8,128)(2,1)S(1)}, u32[]{:S(2)}, u32[]{:S(2)}) collective-permute-start(bf16[256,256]{1,0:T(8,128)(2,1)S(1)} %get-tuple-element.26), channel_id=1, source_target_pairs={{0,4},{1,5},{2,6},{3,7},{4,8},{5,9},{6,10},{7,11},{8,12},{9,13},{1... | collective-permute-start | bytes 393224 | tf_op jit(solution)/shard_map/ppermute | solution.py:22
  36.6 8.3 %collective-permute-start.12 = (bf16[256,256]{1,0:T(8,128)(2,1)S(1)}, bf16[256,256]{1,0:T(8,128)(2,1)S(1)}, u32[]{:S(2)}, u32[]{:S(2)}) collective-permute-start(bf16[256,256]{1,0:T(8,128)(2,1)S(1)} %get-tuple-element.27), channel_id=1, source_target_pairs={{0,4},{1,5},{2,6},{3,7},{4,8},{5,9},{6,10},{7,11},{8,12},{9,13},{1... | collective-permute-start | bytes 393224 | tf_op jit(solution)/shard_map/ppermute | solution.py:22
  41.9 4.5 %collective-permute-start.15 = (bf16[256,256]{1,0:T(8,128)(2,1)S(1)}, bf16[256,256]{1,0:T(8,128)(2,1)S(1)}, u32[]{:S(2)}, u32[]{:S(2)}) collective-permute-start(bf16[256,256]{1,0:T(8,128)(2,1)S(1)} %collective-permute-done.11.refs_0_), channel_id=1, source_target_pairs={{0,2},{1,3},{2,0},{3,1},{4,6},{5,7},{6,4},{7,5},{8,10},{9,11},{10,... | collective-permute-start | bytes 393224 | tf_op jit(solution)/shard_map/ppermute | solution.py:22
  44.9 5.0 %collective-permute-start.16 = (bf16[256,256]{1,0:T(8,128)(2,1)S(1)}, bf16[256,256]{1,0:T(8,128)(2,1)S(1)}, u32[]{:S(2)}, u32[]{:S(2)}) collective-permute-start(bf16[256,256]{1,0:T(8,128)(2,1)S(1)} %collective-permute-done.12.refs_1_), channel_id=1, source_target_pairs={{0,2},{1,3},{2,0},{3,1},{4,6},{5,7},{6,4},{7,5},{8,10},{9,11},{10,... | collective-permute-start | bytes 393224 | tf_op jit(solution)/shard_map/ppermute | solution.py:22
  45.2 6.2 %collective-permute-start.13 = (bf16[256,256]{1,0:T(8,128)(2,1)S(1)}, bf16[256,256]{1,0:T(8,128)(2,1)S(1)}, u32[]{:S(2)}, u32[]{:S(2)}) collective-permute-start(bf16[256,256]{1,0:T(8,128)(2,1)S(1)} %collective-permute-done.11.refs_0_), channel_id=1, source_target_pairs={{0,1},{1,0},{2,3},{3,2},{4,5},{5,4},{6,7},{7,6},{8,9},{9,8},{10,11... | collective-permute-start | bytes 393224 | tf_op jit(solution)/shard_map/ppermute | solution.py:22
  46.4 4.9 %collective-permute-start.14 = (bf16[256,256]{1,0:T(8,128)(2,1)S(1)}, bf16[256,256]{1,0:T(8,128)(2,1)S(1)}, u32[]{:S(2)}, u32[]{:S(2)}) collective-permute-start(bf16[256,256]{1,0:T(8,128)(2,1)S(1)} %collective-permute-done.12.refs_1_), channel_id=1, source_target_pairs={{0,1},{1,0},{2,3},{3,2},{4,5},{5,4},{6,7},{7,6},{8,9},{9,8},{10,11... | collective-permute-start | bytes 393224 | tf_op jit(solution)/shard_map/ppermute | solution.py:22
  46.4 4.9 %collective-permute-start.17 = (bf16[256,256]{1,0:T(8,128)(2,1)S(1)}, bf16[256,256]{1,0:T(8,128)(2,1)S(1)}, u32[]{:S(2)}, u32[]{:S(2)}) collective-permute-start(bf16[256,256]{1,0:T(8,128)(2,1)S(1)} %collective-permute-done.15.refs_4_), channel_id=1, source_target_pairs={{0,1},{1,0},{2,3},{3,2},{4,5},{5,4},{6,7},{7,6},{8,9},{9,8},{10,11... | collective-permute-start | bytes 393224 | tf_op jit(solution)/shard_map/ppermute | solution.py:22
  50.0 2.4 %collective-permute-start.18 = (bf16[256,256]{1,0:T(8,128)(2,1)S(1)}, bf16[256,256]{1,0:T(8,128)(2,1)S(1)}, u32[]{:S(2)}, u32[]{:S(2)}) collective-permute-start(bf16[256,256]{1,0:T(8,128)(2,1)S(1)} %collective-permute-done.16.refs_5_), channel_id=1, source_target_pairs={{0,1},{1,0},{2,3},{3,2},{4,5},{5,4},{6,7},{7,6},{8,9},{9,8},{10,11... | collective-permute-start | bytes 393224 | tf_op jit(solution)/shard_map/ppermute | solution.py:22

commit v5 on v4

--- a/solution.py
+++ b/solution.py
@@ -10,6 +10,7 @@
 AXES = ("slab", "sub")
 VMEM = pltpu.VMEM
 SCOPED = 16 << 20
+PARTS = 1
 
 
 def permuted(x, slabs, subs, by, flip, ring=False):
@@ -82,22 +83,31 @@
     return jnp.dot(a, b, preferred_element_type=jnp.float32)
 
 
-def group_kernel(count, group, masked, chunks, *refs):
+def group_kernel(count, group, groups, masked, chunks, *refs):
     shares, (in_idx, out_idx, blocks, sides) = refs[:count], refs[count : count + 4]
-    (sol_hbm, fsol_hbm), (inc, val, sol, sem, fsem) = (
-        refs[-7 - chunks : -5 - chunks],
-        refs[-5:],
-    )
-    f_refs = refs[-5 - chunks : -5]
+    refs = refs[count + 4 :]
+    done = group + 1 == groups
+    if done:
+        sol_hbm, fsol_hbm, sol, *f_refs, inc, val, sems = refs[-6 - chunks :]
+    else:
+        sol, *f_refs, inc, val = refs[-3 - chunks :]
     links, rows_in = in_idx.shape
     rows_out, out_links = out_idx.shape
     size = blocks.shape[1]
     part, width = shares[0].shape
+    each = rows_out // chunks
     inv_at = rows_in * links
     out_at = inv_at + rows_in
     last_at = out_at + rows_out * out_links
     swap = lax.axis_index("sub") * rows_out
     cols = pl.ds(group * width, width)
+    copies = []
+
+    def write(source, target, first, count):
+        there = target.at[pl.ds(first, count), cols]
+        copies.append(pltpu.make_async_copy(source, there, sems.at[len(copies)]))
+        copies[-1].start()
+
     keep = lax.axis_index("slab") > 0
     for r, ref in enumerate(shares):
         value = ref[...]
@@ -126,33 +136,34 @@
     for i in range(rows_in):
         coupled = row_of(0, i, inc, [in_idx[k, i] ^ swap for k in range(links)])
         val[at(i), :] = (side(i) - coupled).astype(val.dtype)
+    some = rows_in // PARTS
     for i in range(rows_in):
         sol[at(i), :] = dot(block(inv_at + i), val[at(i), :]).astype(sol.dtype)
-    first = pltpu.make_async_copy(sol, sol_hbm.at[:, cols], sem)
-    first.start()
+        if done and (i + 1) % some == 0:
+            start, count = (i + 1 - some) * size, some * size
+            piece = sol.at[pl.ds(start, count), :]
+            write(piece, sol_hbm, start, count)
     for j in range(rows_out):
         outgoing = row_of(out_at, j, sol, [out_idx[j, k] for k in range(out_links)])
         val[at(j), :] = (side(rows_in + j) - outgoing).astype(val.dtype)
-    each = rows_out // chunks
-    copies = [first]
     for c, f_ref in enumerate(f_refs):
         for j in range(each):
             row = c * each + j
             f_ref[at(j), :] = dot(block(last_at + row), val[at(row), :]).astype(
                 f_ref.dtype
             )
-        there = fsol_hbm.at[pl.ds(c * each * size, each * size), cols]
-        copies.append(pltpu.make_async_copy(f_ref, there, fsem.at[c]))
-        copies[-1].start()
+        if done:
+            count = each * size
+            write(f_ref, fsol_hbm, c * count, count)
     for c in copies:
         c.wait()
 
 
-def group_of(shares, in_idx, out_idx, blocks, sides, outs, token, group, masked):
+def group_of(shares, in_idx, out_idx, blocks, sides, outs, token, group, groups, masked):
     width = shares[0].shape[1]
     links, rows_in = in_idx.shape
     rows_out, out_links = out_idx.shape
-    size = blocks.shape[1]
+    size, dtype = blocks.shape[1], blocks.dtype
     rows, front_rows = rows_in * size, rows_out * size
     chunks = 2 if rows_out % 2 == 0 else 1
     pieces = len(shares)
@@ -160,37 +171,35 @@
     smem = pl.BlockSpec(memory_space=pltpu.SMEM)
     vmem = pl.BlockSpec(memory_space=VMEM)
     hbm = pl.BlockSpec(memory_space=pl.ANY)
-    aliased = outs is not None
+    done = group + 1 == groups
 
     def held(arrays):
         return [pltpu.with_memory_space_constraint(a, VMEM) for a in arrays]
 
-    operands = (
-        held(shares)
-        + [in_idx, out_idx]
-        + held([blocks, sides])
-        + (list(outs) if aliased else [])
-        + ([] if token is None else [token])
-    )
-    n = len(operands) - (token is not None)
+    operands = held(shares) + [in_idx, out_idx] + held([blocks, sides])
+    in_specs = [vmem] * pieces + [smem] * 2 + [vmem] * 2
+    aliases = {len(operands) + n: n for n in range(len(outs))}
+    operands += [*outs] if token is None else [*outs, token]
+    in_specs += [hbm] * (len(operands) - len(in_specs))
+    own = [VMEM((rows, width), dtype)]
+    own += [VMEM((front_rows // chunks, width), dtype)] * chunks
+    out_shape, out_specs = own, [vmem] * len(own)
+    scratch = [
+        VMEM((sum(a.shape[0] for a in shares), width), dtype),
+        VMEM((rows, width), dtype),
+    ]
+    if done:
+        wide = sides.shape[1]
+        scratch = own + scratch + [pltpu.SemaphoreType.DMA((PARTS + chunks,))]
+        out_shape = [pltpu.HBM((r, wide), dtype) for r in (rows, front_rows)]
+        out_specs = [hbm, hbm]
     return pl.pallas_call(
-        functools.partial(group_kernel, pieces, group, masked, chunks),
-        out_shape=(
-            pltpu.HBM((rows, sides.shape[1]), sides.dtype),
-            pltpu.HBM((front_rows, sides.shape[1]), sides.dtype),
-            *[VMEM((front_rows // chunks, width), sides.dtype)] * chunks,
-        ),
-        in_specs=[vmem] * pieces + [smem] * 2 + [vmem] * 2
-        + [hbm] * (len(operands) - pieces - 4),
-        out_specs=(hbm, hbm, *[vmem] * chunks),
-        scratch_shapes=[
-            VMEM((sum(a.shape[0] for a in shares), width), sides.dtype),
-            VMEM((rows, width), sides.dtype),
-            VMEM((rows, width), sides.dtype),
-            pltpu.SemaphoreType.DMA,
-            pltpu.SemaphoreType.DMA((chunks,)),
-        ],
-        input_output_aliases={n - 2: 0, n - 1: 1} if aliased else {},
+        functools.partial(group_kernel, pieces, group, groups, masked, chunks),
+        out_shape=tuple(out_shape),
+        in_specs=in_specs,
+        out_specs=tuple(out_specs),
+        scratch_shapes=scratch,
+        input_output_aliases=aliases,
         compiler_params=pltpu.CompilerParams(vmem_limit_bytes=SCOPED),
         cost_estimate=pl.CostEstimate(
             flops=2 * count * size * size * width,
@@ -199,6 +208,42 @@
         ),
         name=f"group_{group}",
     )(*operands)
+
+
+def flush_kernel(count, column, *refs):
+    sources, (sol_hbm, fsol_hbm, sems) = refs[:count], refs[-3:]
+    copies, row = [], 0
+    for n, ref in enumerate(sources):
+        rows, width = ref.shape
+        out = fsol_hbm if n else sol_hbm
+        there = out.at[pl.ds(row, rows), pl.ds(column * width, width)]
+        row += rows if n else 0
+        copies.append(pltpu.make_async_copy(ref, there, sems.at[n]))
+        copies[-1].start()
+    for c in copies:
+        c.wait()
+
+
+def flushed(sources, outs, column, groups):
+    n, dtype = len(sources), sources[0].dtype
+    wide = groups * sources[0].shape[1]
+    rows = (sources[0].shape[0], sum(f.shape[0] for f in sources[1:]))
+    hbm = pl.BlockSpec(memory_space=pl.ANY)
+    return pl.pallas_call(
+        functools.partial(flush_kernel, n, column),
+        out_shape=tuple(pltpu.HBM((r, wide), dtype) for r in rows),
+        in_specs=[pl.BlockSpec(memory_space=VMEM)] * n + [hbm] * len(outs),
+        out_specs=(hbm, hbm),
+        scratch_shapes=[pltpu.SemaphoreType.DMA((n,))],
+        input_output_aliases={n + k: k for k in range(len(outs))},
+        compiler_params=pltpu.CompilerParams(vmem_limit_bytes=SCOPED),
+        cost_estimate=pl.CostEstimate(
+            flops=0,
+            bytes_accessed=2 * sum(s.size for s in sources) * dtype.itemsize,
+            transcendentals=0,
+        ),
+        name=f"flush_{column}",
+    )(*[pltpu.with_memory_space_constraint(s, VMEM) for s in sources], *outs)
 
 
 def shards(
@@ -222,26 +267,31 @@
         [w.reshape(-1, size) for w in weights], [right_sides, front_sides]
     )
     arrived, token = gathered(pending_front, slabs, subs, token)
-    outs = None
+    outs = ()
     for group in range(groups):
-        ring = group + 2 < groups
         made = group_of(
             arrived,
             in_idx,
             out_idx,
             blocks,
             sides,
-            outs,
-            token,
+            outs if group + 1 == groups else (),
+            token if group == 0 else None,
             group,
+            groups,
             0 < group and group + 1 < groups,
         )
-        outs, fronts = made[:2], made[2:]
         if group + 1 < groups:
-            hops = [permuted(f, slabs, subs, 1, 0, ring) for f in fronts]
-            chunks, token = [gathered(hop, slabs, subs)[0] for hop in hops], None
+            ring = group + 2 < groups
+            hops = [permuted(f, slabs, subs, 1, 0, ring) for f in made[1:]]
+            outs = flushed(made, outs, group, groups)
+            chunks = []
+            for n, hop in enumerate(hops):
+                chunk, ahead = gathered(hop, slabs, subs, None if n else outs)
+                outs = outs if n else ahead
+                chunks.append(chunk)
             arrived = [c[r] for r in range(subs) for c in chunks]
-    return tuple(outs)
+    return tuple(made[:2])
 
 
 def solution(mesh):

time: 56.7 us -> 54.8 us (0.966)
  starting transfers between devices: 24.3 us -> 19.8 us
  waiting for transfers between devices: 16.6 us -> 19.4 us
    ppermute x19, starting transfers between devices: 24.3 us -> 19.8 us  [permuted(): return lax.ppermute(x, AXES, pairs)]
    ppermute x19, waiting for transfers between devices: 16.6 us -> 19.4 us  [permuted(): return lax.ppermute(x, AXES, pairs)]
    pallas_call x3 -> x5, Pallas kernels: 11.3 us -> 11.1 us  [the longest x3 9 us: group_of(): pl.pallas_call(functools.partial(group_kernel, pieces, group, groups, mas...]
  transfers between devices with their start and end apart: 19 -> 19, of which waited for: 10 -> 11; matrix products, arithmetic and copies ran while one was open for 0% -> 0% of each run, Pallas kernels for 6% -> 10%
where the time goes in v5:
time: 54.8 us; the launch traced here: 54.6 us
  starting transfers between devices  19.8 us (36%)
  waiting for transfers between devices  19.4 us (35%)
  Pallas kernels  14.7 us (27%)
  between operations  0.72 us (1%)
    ppermute x19, starting transfers between devices, permuted(): return lax.ppermute(x, AXES, pairs)  19.8 us
    ppermute x19, waiting for transfers between devices, permuted(): return lax.ppermute(x, AXES, pairs)  19.4 us
    pallas_call x3, Pallas kernels, group_of(): pl.pallas_call(functools.partial(group_kernel, pieces, group, groups, mas...  9 us
    pallas_call x1, Pallas kernels, staged(): pl.pallas_call(functools.partial(stage_kernel, counts), out_shape=(*(VMEM...  3.58 us
    pallas_call x2, Pallas kernels, flushed(): pl.pallas_call(functools.partial(flush_kernel, n, column), out_shape=tupl...  2.13 us
  transfers between devices with their start and end apart: 19, of which 11 were waited for; matrix products, arithmetic and copies ran while one was open for 0% of the time, Pallas kernels for 10%

profile of v5, /device:TPU:11, one launch (start us, length us, event | category | flops | bytes accessed | tf_op | source)
XLA Modules:
  0.0 54.6 jit_solution(10198046141732035771)
XLA Ops:
  0.6 0.3 collective-permute-start.1
  1.0 1.0 %collective-permute-start = (bf16[512,256]{1,0:T(8,128)(2,1)}, bf16[512,256]{1,0:T(8,128)(2,1)S(1)}, u32[]{:S(2)}, u32[]{:S(2)}) collective-permute-start(bf16[512,256]{1,0:T(8,128)(2,1)} %refs_0_.1), channel_id=1, source_target_pairs={{0,1},{1,0},{2,3},{3,2},{4,5},{5,4},{6,7},{7,6},{8,9},{9,8},{10,11... | collective-permute-start | bytes 786440 | tf_op jit(solution)/shard_map/ppermute | solution.py:23
  1.9 0.0 copy-start
  1.9 3.6 %stage.1 = (bf16[18944,128]{1,0:T(8,128)(2,1)S(1)}, bf16[2560,768]{1,0:T(8,128)(2,1)S(1)}, f32[8,128]{1,0:T(8,128)S(1)}) custom-call(bf16[12288,128]{1,0:T(8,128)(2,1)} %bitcast.8, bf16[2048,128]{1,0:T(8,128)(2,1)} %bitcast.10, bf16[4096,128]{1,0:T(8,128)(2,1)} %bitcast.9, bf16[512,128]{1,0:T(8,128)(2,1)} %bitcast.11, bf16[2048,768]{1,0:T(8,128)(2,1)} %refs_4_.1, ...), custom_call_target="tpu_custom_call" | custom-call | bytes 17563648 | tf_op jit(solution)/shard_map/stage/pallas_call | solution.py:65
  5.5 2.6 %collective-permute-done.1.refs_2_ = bf16[512,256]{1,0:T(8,128)(2,1)S(1)} collective-permute-done((bf16[512,256]{1,0:T(8,128)(2,1)}, bf16[512,256]{1,0:T(8,128)(2,1)S(1)}, u32[]{:S(2)}, u32[]{:S(2)}) %collective-permute-start.1) | collective-permute-done | bytes 262176 | tf_op jit(solution)/shard_map/ppermute | solution.py:23
  8.1 1.5 %collective-permute-start.2 = (bf16[512,256]{1,0:T(8,128)(2,1)S(1)}, bf16[512,256]{1,0:T(8,128)(2,1)S(1)}, u32[]{:S(2)}, u32[]{:S(2)}) collective-permute-start(bf16[512,256]{1,0:T(8,128)(2,1)S(1)} %collective-permute-done.1.refs_2_), channel_id=1, source_target_pairs={{0,1},{1,0},{2,3},{3,2},{4,5},{5,4},{6,7},{7,6},{8,9},{9,8},{10,11... | collective-permute-start | bytes 786440 | tf_op jit(solution)/shard_map/ppermute | solution.py:23
  9.6 0.0 collective-permute-done.refs_1_
  9.6 1.2 %collective-permute-done.2.refs_3_ = bf16[512,256]{1,0:T(8,128)(2,1)S(1)} collective-permute-done((bf16[512,256]{1,0:T(8,128)(2,1)S(1)}, bf16[512,256]{1,0:T(8,128)(2,1)S(1)}, u32[]{:S(2)}, u32[]{:S(2)}) %collective-permute-start.2) | collective-permute-done | bytes 262176 | tf_op jit(solution)/shard_map/ppermute | solution.py:23
  10.8 0.0 copy-done
  10.8 0.0 copy-done.1
  10.8 0.0 copy-done.2
  10.8 2.8 %group_0.1 = (bf16[2048,256]{1,0:T(8,128)(2,1)S(1)}, bf16[256,256]{1,0:T(8,128)(2,1)S(1)}, bf16[256,256]{1,0:T(8,128)(2,1)S(1)}) custom-call(bf16[512,256]{1,0:T(8,128)(2,1)S(1)} %copy-done, bf16[512,256]{1,0:T(8,128)(2,1)S(1)} %collective-permute-done.refs_1_, bf16[512,256]{1,0:T(8,128)(2,1)S(1)} %collective-permute-done.1.refs_2_, ...), custom_call_target="tpu_custom_call" | custom-call | flops 1241513984 | bytes 6946816 | tf_op jit(solution)/shard_map/group_0/pallas_call | solution.py:196
  13.6 1.3 %collective-permute-start.3 = (bf16[256,256]{1,0:T(8,128)(2,1)S(1)}, bf16[256,256]{1,0:T(8,128)(2,1)S(1)}, u32[]{:S(2)}, u32[]{:S(2)}) collective-permute-start(bf16[256,256]{1,0:T(8,128)(2,1)S(1)} %get-tuple-element.28.refs_1_), channel_id=1, source_target_pairs={{0,4},{1,5},{2,6},{3,7},{4,8},{5,9},{6,10},{7,11},{8,12},{9,13},{1... | collective-permute-start | bytes 393224 | tf_op jit(solution)/shard_map/ppermute | solution.py:23
  14.9 1.2 %collective-permute-start.4 = (bf16[256,256]{1,0:T(8,128)(2,1)S(1)}, bf16[256,256]{1,0:T(8,128)(2,1)S(1)}, u32[]{:S(2)}, u32[]{:S(2)}) collective-permute-start(bf16[256,256]{1,0:T(8,128)(2,1)S(1)} %get-tuple-element.29.refs_2_), channel_id=1, source_target_pairs={{0,4},{1,5},{2,6},{3,7},{4,8},{5,9},{6,10},{7,11},{8,12},{9,13},{1... | collective-permute-start | bytes 393224 | tf_op jit(solution)/shard_map/ppermute | solution.py:23
  16.1 3.1 %collective-permute-done.3.refs_0_ = bf16[256,256]{1,0:T(8,128)(2,1)S(1)} collective-permute-done((bf16[256,256]{1,0:T(8,128)(2,1)S(1)}, bf16[256,256]{1,0:T(8,128)(2,1)S(1)}, u32[]{:S(2)}, u32[]{:S(2)}) %collective-permute-start.3) | collective-permute-done | bytes 131104 | tf_op jit(solution)/shard_map/ppermute | solution.py:23
  19.2 0.3 collective-permute-start.7
  19.5 2.6 %collective-permute-done.4.refs_1_ = bf16[256,256]{1,0:T(8,128)(2,1)S(1)} collective-permute-done((bf16[256,256]{1,0:T(8,128)(2,1)S(1)}, bf16[256,256]{1,0:T(8,128)(2,1)S(1)}, u32[]{:S(2)}, u32[]{:S(2)}) %collective-permute-start.4) | collective-permute-done | bytes 131104 | tf_op jit(solution)/shard_map/ppermute | solution.py:23
  22.0 0.3 collective-permute-start.8
  22.3 1.1 %flush_0.1 = (bf16[2048,768]{1,0:T(8,128)(2,1)}, bf16[512,768]{1,0:T(8,128)(2,1)}) custom-call(bf16[2048,256]{1,0:T(8,128)(2,1)S(1)} %get-tuple-element.30.refs_0_, bf16[256,256]{1,0:T(8,128)(2,1)S(1)} %get-tuple-element.28.refs_1_, bf16[256,256]{1,0:T(8,128)(2,1)S(1)} %get-tuple-element.29.refs_2_), custom_call_target="tpu_custom_call" | custom-call | bytes 2621440 | tf_op jit(solution)/shard_map/flush_0/pallas_call | solution.py:232
  23.4 1.6 %collective-permute-start.5 = (bf16[256,256]{1,0:T(8,128)(2,1)S(1)}, bf16[256,256]{1,0:T(8,128)(2,1)S(1)}, u32[]{:S(2)}, u32[]{:S(2)}) collective-permute-start(bf16[256,256]{1,0:T(8,128)(2,1)S(1)} %collective-permute-done.3.refs_0_), channel_id=1, source_target_pairs={{0,1},{1,0},{2,3},{3,2},{4,5},{5,4},{6,7},{7,6},{8,9},{9,8},{10,11... | collective-permute-start | bytes 393224 | tf_op jit(solution)/shard_map/ppermute | solution.py:23
  24.9 0.1 collective-permute-start.6
  25.0 0.0 collective-permute-done.7.refs_4_
  25.0 2.5 %collective-permute-done.8.refs_5_ = bf16[256,256]{1,0:T(8,128)(2,1)S(1)} collective-permute-done((bf16[256,256]{1,0:T(8,128)(2,1)S(1)}, bf16[256,256]{1,0:T(8,128)(2,1)S(1)}, u32[]{:S(2)}, u32[]{:S(2)}) %collective-permute-start.8) | collective-permute-done | bytes 131104 | tf_op jit(solution)/shard_map/ppermute | solution.py:23
  27.5 1.5 %collective-permute-start.10 = (bf16[256,256]{1,0:T(8,128)(2,1)S(1)}, bf16[256,256]{1,0:T(8,128)(2,1)S(1)}, u32[]{:S(2)}, u32[]{:S(2)}) collective-permute-start(bf16[256,256]{1,0:T(8,128)(2,1)S(1)} %collective-permute-done.8.refs_5_), channel_id=1, source_target_pairs={{0,1},{1,0},{2,3},{3,2},{4,5},{5,4},{6,7},{7,6},{8,9},{9,8},{10,11... | collective-permute-start | bytes 393224 | tf_op jit(solution)/shard_map/ppermute | solution.py:23
  29.0 0.0 collective-permute-start.9
  29.0 0.0 collective-permute-done.5.refs_2_
  29.0 0.0 collective-permute-done.6.refs_3_
  29.0 1.0 %collective-permute-done.10.refs_7_ = bf16[256,256]{1,0:T(8,128)(2,1)S(1)} collective-permute-done((bf16[256,256]{1,0:T(8,128)(2,1)S(1)}, bf16[256,256]{1,0:T(8,128)(2,1)S(1)}, u32[]{:S(2)}, u32[]{:S(2)}) %collective-permute-start.10) | collective-permute-done | bytes 131104 | tf_op jit(solution)/shard_map/ppermute | solution.py:23
  30.0 0.4 collective-permute-done.9.refs_6_
  30.4 2.7 %group_1.1 = (bf16[2048,256]{1,0:T(8,128)(2,1)S(1)}, bf16[256,256]{1,0:T(8,128)(2,1)S(1)}, bf16[256,256]{1,0:T(8,128)(2,1)S(1)}) custom-call(bf16[256,256]{1,0:T(8,128)(2,1)S(1)} %collective-permute-done.3.refs_0_, bf16[256,256]{1,0:T(8,128)(2,1)S(1)} %collective-permute-done.4.refs_1_, bf16[256,256]{1,0:T(8,128)(2,1)S(1)} %collective-permute-done.5.refs_2_, ...), custom_call_target="tpu_custom_call" | custom-call | flops 1241513984 | bytes 6946816 | tf_op jit(solution)/shard_map/group_1/pallas_call | solution.py:196
  33.1 2.2 %collective-permute-start.11 = (bf16[256,256]{1,0:T(8,128)(2,1)S(1)}, bf16[256,256]{1,0:T(8,128)(2,1)S(1)}, u32[]{:S(2)}, u32[]{:S(2)}) collective-permute-start(bf16[256,256]{1,0:T(8,128)(2,1)S(1)} %get-tuple-element.34.refs_1_), channel_id=1, source_target_pairs={{0,4},{1,5},{2,6},{3,7},{4,8},{5,9},{6,10},{7,11},{8,12},{9,13},{1... | collective-permute-start | bytes 393224 | tf_op jit(solution)/shard_map/ppermute | solution.py:23
  35.4 4.0 %collective-permute-start.12 = (bf16[256,256]{1,0:T(8,128)(2,1)S(1)}, bf16[256,256]{1,0:T(8,128)(2,1)S(1)}, u32[]{:S(2)}, u32[]{:S(2)}) collective-permute-start(bf16[256,256]{1,0:T(8,128)(2,1)S(1)} %get-tuple-element.35.refs_2_), channel_id=1, source_target_pairs={{0,4},{1,5},{2,6},{3,7},{4,8},{5,9},{6,10},{7,11},{8,12},{9,13},{1... | collective-permute-start | bytes 393224 | tf_op jit(solution)/shard_map/ppermute | solution.py:23
  39.4 1.4 %collective-permute-done.11.refs_0_ = bf16[256,256]{1,0:T(8,128)(2,1)S(1)} collective-permute-done((bf16[256,256]{1,0:T(8,128)(2,1)S(1)}, bf16[256,256]{1,0:T(8,128)(2,1)S(1)}, u32[]{:S(2)}, u32[]{:S(2)}) %collective-permute-start.11) | collective-permute-done | bytes 131104 | tf_op jit(solution)/shard_map/ppermute | solution.py:23
  40.8 0.3 collective-permute-start.15
  41.1 2.7 %collective-permute-done.12.refs_1_ = bf16[256,256]{1,0:T(8,128)(2,1)S(1)} collective-permute-done((bf16[256,256]{1,0:T(8,128)(2,1)S(1)}, bf16[256,256]{1,0:T(8,128)(2,1)S(1)}, u32[]{:S(2)}, u32[]{:S(2)}) %collective-permute-start.12) | collective-permute-done | bytes 131104 | tf_op jit(solution)/shard_map/ppermute | solution.py:23
  43.8 0.3 collective-permute-start.16
  44.0 1.1 %flush_1.1 = (bf16[2048,768]{1,0:T(8,128)(2,1)}, bf16[512,768]{1,0:T(8,128)(2,1)}) custom-call(bf16[2048,256]{1,0:T(8,128)(2,1)S(1)} %get-tuple-element.36.refs_0_, bf16[256,256]{1,0:T(8,128)(2,1)S(1)} %get-tuple-element.34.refs_1_, bf16[256,256]{1,0:T(8,128)(2,1)S(1)} %get-tuple-element.35.refs_2_, ...), custom_call_target="tpu_custom_call", output_to_operand_aliasing={{0}: (3, {}), {1}: (4, {})} | custom-call | bytes 2621440 | tf_op jit(solution)/shard_map/flush_1/pallas_call | solution.py:232
  45.1 1.2 %collective-permute-start.13 = (bf16[256,256]{1,0:T(8,128)(2,1)S(1)}, bf16[256,256]{1,0:T(8,128)(2,1)S(1)}, u32[]{:S(2)}, u32[]{:S(2)}) collective-permute-start(bf16[256,256]{1,0:T(8,128)(2,1)S(1)} %collective-permute-done.11.refs_0_), channel_id=1, source_target_pairs={{0,1},{1,0},{2,3},{3,2},{4,5},{5,4},{6,7},{7,6},{8,9},{9,8},{10,11... | collective-permute-start | bytes 393224 | tf_op jit(solution)/shard_map/ppermute | solution.py:23
  46.3 0.1 collective-permute-start.14
  46.4 0.0 collective-permute-done.15.refs_4_
  46.4 1.3 %collective-permute-start.17 = (bf16[256,256]{1,0:T(8,128)(2,1)S(1)}, bf16[256,256]{1,0:T(8,128)(2,1)S(1)}, u32[]{:S(2)}, u32[]{:S(2)}) collective-permute-start(bf16[256,256]{1,0:T(8,128)(2,1)S(1)} %collective-permute-done.15.refs_4_), channel_id=1, source_target_pairs={{0,1},{1,0},{2,3},{3,2},{4,5},{5,4},{6,7},{7,6},{8,9},{9,8},{10,11... | collective-permute-start | bytes 393224 | tf_op jit(solution)/shard_map/ppermute | solution.py:23
  47.7 1.0 %collective-permute-done.16.refs_5_ = bf16[256,256]{1,0:T(8,128)(2,1)S(1)} collective-permute-done((bf16[256,256]{1,0:T(8,128)(2,1)S(1)}, bf16[256,256]{1,0:T(8,128)(2,1)S(1)}, u32[]{:S(2)}, u32[]{:S(2)}) %collective-permute-start.16) | collective-permute-done | bytes 131104 | tf_op jit(solution)/shard_map/ppermute | solution.py:23
  48.8 1.4 %collective-permute-start.18 = (bf16[256,256]{1,0:T(8,128)(2,1)S(1)}, bf16[256,256]{1,0:T(8,128)(2,1)S(1)}, u32[]{:S(2)}, u32[]{:S(2)}) collective-permute-start(bf16[256,256]{1,0:T(8,128)(2,1)S(1)} %collective-permute-done.16.refs_5_), channel_id=1, source_target_pairs={{0,1},{1,0},{2,3},{3,2},{4,5},{5,4},{6,7},{7,6},{8,9},{9,8},{10,11... | collective-permute-start | bytes 393224 | tf_op jit(solution)/shard_map/ppermute | solution.py:23
  50.1 0.0 collective-permute-done.13.refs_2_
  50.1 0.0 collective-permute-done.14.refs_3_
  50.1 0.0 collective-permute-done.17.refs_6_
  50.1 1.0 %collective-permute-done.18.refs_7_ = bf16[256,256]{1,0:T(8,128)(2,1)S(1)} collective-permute-done((bf16[256,256]{1,0:T(8,128)(2,1)S(1)}, bf16[256,256]{1,0:T(8,128)(2,1)S(1)}, u32[]{:S(2)}, u32[]{:S(2)}) %collective-permute-start.18) | collective-permute-done | bytes 131104 | tf_op jit(solution)/shard_map/ppermute | solution.py:23
  51.1 3.5 %group_2.1 = (bf16[2048,768]{1,0:T(8,128)(2,1)}, bf16[512,768]{1,0:T(8,128)(2,1)}) custom-call(bf16[256,256]{1,0:T(8,128)(2,1)S(1)} %collective-permute-done.11.refs_0_, bf16[256,256]{1,0:T(8,128)(2,1)S(1)} %collective-permute-done.12.refs_1_, bf16[256,256]{1,0:T(8,128)(2,1)S(1)} %collective-permute-done.13.refs_2_, ...), custom_call_target="tpu_custom_call", output_to_operand_aliasing={{0}: (12, {}), {1}: (13, {})} | custom-call | flops 1241513984 | bytes 6946816 | tf_op jit(solution)/shard_map/group_2/pallas_call | solution.py:196
  (2 shorter events, 0.0 us)
Async XLA Ops:
  0.6 7.5 %collective-permute-start.1 = (bf16[512,256]{1,0:T(8,128)(2,1)}, bf16[512,256]{1,0:T(8,128)(2,1)S(1)}, u32[]{:S(2)}, u32[]{:S(2)}) collective-permute-start(bf16[512,256]{1,0:T(8,128)(2,1)} %refs_0_.1), channel_id=1, source_target_pairs={{0,2},{1,3},{2,0},{3,1},{4,6},{5,7},{6,4},{7,5},{8,10},{9,11},{10,... | collective-permute-start | bytes 786440 | tf_op jit(solution)/shard_map/ppermute | solution.py:23
  1.0 8.7 %collective-permute-start = (bf16[512,256]{1,0:T(8,128)(2,1)}, bf16[512,256]{1,0:T(8,128)(2,1)S(1)}, u32[]{:S(2)}, u32[]{:S(2)}) collective-permute-start(bf16[512,256]{1,0:T(8,128)(2,1)} %refs_0_.1), channel_id=1, source_target_pairs={{0,1},{1,0},{2,3},{3,2},{4,5},{5,4},{6,7},{7,6},{8,9},{9,8},{10,11... | collective-permute-start | bytes 786440 | tf_op jit(solution)/shard_map/ppermute | solution.py:23
  1.9 8.9 %copy-start = (bf16[512,256]{1,0:T(8,128)(2,1)S(1)}, bf16[512,256]{1,0:T(8,128)(2,1)}, u32[]{:S(2)}) copy-start(bf16[512,256]{1,0:T(8,128)(2,1)} %refs_0_.1) | copy-start | bytes 786436
  1.9 8.9 %copy-start.1 = (s32[16,6]{0,1:T(8,128)S(1)}, s32[16,6]{0,1:T(8,128)}, u32[]{:S(2)}) copy-start(s32[16,6]{0,1:T(8,128)} %param.12) | copy-start | bytes 1156
  1.9 8.9 %copy-start.2 = (s32[4,8]{1,0:T(4,128)S(1)}, s32[4,8]{1,0:T(4,128)}, u32[]{:S(2)}) copy-start(s32[4,8]{1,0:T(4,128)} %refs_9_.3) | copy-start | bytes 388
  8.1 2.7 %collective-permute-start.2 = (bf16[512,256]{1,0:T(8,128)(2,1)S(1)}, bf16[512,256]{1,0:T(8,128)(2,1)S(1)}, u32[]{:S(2)}, u32[]{:S(2)}) collective-permute-start(bf16[512,256]{1,0:T(8,128)(2,1)S(1)} %collective-permute-done.1.refs_2_), channel_id=1, source_target_pairs={{0,1},{1,0},{2,3},{3,2},{4,5},{5,4},{6,7},{7,6},{8,9},{9,8},{10,11... | collective-permute-start | bytes 786440 | tf_op jit(solution)/shard_map/ppermute | solution.py:23
  13.6 5.6 %collective-permute-start.3 = (bf16[256,256]{1,0:T(8,128)(2,1)S(1)}, bf16[256,256]{1,0:T(8,128)(2,1)S(1)}, u32[]{:S(2)}, u32[]{:S(2)}) collective-permute-start(bf16[256,256]{1,0:T(8,128)(2,1)S(1)} %get-tuple-element.28.refs_1_), channel_id=1, source_target_pairs={{0,4},{1,5},{2,6},{3,7},{4,8},{5,9},{6,10},{7,11},{8,12},{9,13},{1... | collective-permute-start | bytes 393224 | tf_op jit(solution)/shard_map/ppermute | solution.py:23
  14.9 7.2 %collective-permute-start.4 = (bf16[256,256]{1,0:T(8,128)(2,1)S(1)}, bf16[256,256]{1,0:T(8,128)(2,1)S(1)}, u32[]{:S(2)}, u32[]{:S(2)}) collective-permute-start(bf16[256,256]{1,0:T(8,128)(2,1)S(1)} %get-tuple-element.29.refs_2_), channel_id=1, source_target_pairs={{0,4},{1,5},{2,6},{3,7},{4,8},{5,9},{6,10},{7,11},{8,12},{9,13},{1... | collective-permute-start | bytes 393224 | tf_op jit(solution)/shard_map/ppermute | solution.py:23
  19.2 5.8 %collective-permute-start.7 = (bf16[256,256]{1,0:T(8,128)(2,1)S(1)}, bf16[256,256]{1,0:T(8,128)(2,1)S(1)}, u32[]{:S(2)}, u32[]{:S(2)}) collective-permute-start(bf16[256,256]{1,0:T(8,128)(2,1)S(1)} %collective-permute-done.3.refs_0_), channel_id=1, source_target_pairs={{0,2},{1,3},{2,0},{3,1},{4,6},{5,7},{6,4},{7,5},{8,10},{9,11},{10,... | collective-permute-start | bytes 393224 | tf_op jit(solution)/shard_map/ppermute | solution.py:23
  22.0 5.5 %collective-permute-start.8 = (bf16[256,256]{1,0:T(8,128)(2,1)S(1)}, bf16[256,256]{1,0:T(8,128)(2,1)S(1)}, u32[]{:S(2)}, u32[]{:S(2)}) collective-permute-start(bf16[256,256]{1,0:T(8,128)(2,1)S(1)} %collective-permute-done.4.refs_1_), channel_id=1, source_target_pairs={{0,2},{1,3},{2,0},{3,1},{4,6},{5,7},{6,4},{7,5},{8,10},{9,11},{10,... | collective-permute-start | bytes 393224 | tf_op jit(solution)/shard_map/ppermute | solution.py:23
  23.4 5.7 %collective-permute-start.5 = (bf16[256,256]{1,0:T(8,128)(2,1)S(1)}, bf16[256,256]{1,0:T(8,128)(2,1)S(1)}, u32[]{:S(2)}, u32[]{:S(2)}) collective-permute-start(bf16[256,256]{1,0:T(8,128)(2,1)S(1)} %collective-permute-done.3.refs_0_), channel_id=1, source_target_pairs={{0,1},{1,0},{2,3},{3,2},{4,5},{5,4},{6,7},{7,6},{8,9},{9,8},{10,11... | collective-permute-start | bytes 393224 | tf_op jit(solution)/shard_map/ppermute | solution.py:23
  24.9 4.1 %collective-permute-start.6 = (bf16[256,256]{1,0:T(8,128)(2,1)S(1)}, bf16[256,256]{1,0:T(8,128)(2,1)S(1)}, u32[]{:S(2)}, u32[]{:S(2)}) collective-permute-start(bf16[256,256]{1,0:T(8,128)(2,1)S(1)} %collective-permute-done.4.refs_1_), channel_id=1, source_target_pairs={{0,1},{1,0},{2,3},{3,2},{4,5},{5,4},{6,7},{7,6},{8,9},{9,8},{10,11... | collective-permute-start | bytes 393224 | tf_op jit(solution)/shard_map/ppermute | solution.py:23
  27.5 2.5 %collective-permute-start.10 = (bf16[256,256]{1,0:T(8,128)(2,1)S(1)}, bf16[256,256]{1,0:T(8,128)(2,1)S(1)}, u32[]{:S(2)}, u32[]{:S(2)}) collective-permute-start(bf16[256,256]{1,0:T(8,128)(2,1)S(1)} %collective-permute-done.8.refs_5_), channel_id=1, source_target_pairs={{0,1},{1,0},{2,3},{3,2},{4,5},{5,4},{6,7},{7,6},{8,9},{9,8},{10,11... | collective-permute-start | bytes 393224 | tf_op jit(solution)/shard_map/ppermute | solution.py:23
  29.0 1.3 %collective-permute-start.9 = (bf16[256,256]{1,0:T(8,128)(2,1)S(1)}, bf16[256,256]{1,0:T(8,128)(2,1)S(1)}, u32[]{:S(2)}, u32[]{:S(2)}) collective-permute-start(bf16[256,256]{1,0:T(8,128)(2,1)S(1)} %collective-permute-done.7.refs_4_), channel_id=1, source_target_pairs={{0,1},{1,0},{2,3},{3,2},{4,5},{5,4},{6,7},{7,6},{8,9},{9,8},{10,11... | collective-permute-start | bytes 393224 | tf_op jit(solution)/shard_map/ppermute | solution.py:23
  33.1 7.7 %collective-permute-start.11 = (bf16[256,256]{1,0:T(8,128)(2,1)S(1)}, bf16[256,256]{1,0:T(8,128)(2,1)S(1)}, u32[]{:S(2)}, u32[]{:S(2)}) collective-permute-start(bf16[256,256]{1,0:T(8,128)(2,1)S(1)} %get-tuple-element.34.refs_1_), channel_id=1, source_target_pairs={{0,4},{1,5},{2,6},{3,7},{4,8},{5,9},{6,10},{7,11},{8,12},{9,13},{1... | collective-permute-start | bytes 393224 | tf_op jit(solution)/shard_map/ppermute | solution.py:23
  35.4 8.4 %collective-permute-start.12 = (bf16[256,256]{1,0:T(8,128)(2,1)S(1)}, bf16[256,256]{1,0:T(8,128)(2,1)S(1)}, u32[]{:S(2)}, u32[]{:S(2)}) collective-permute-start(bf16[256,256]{1,0:T(8,128)(2,1)S(1)} %get-tuple-element.35.refs_2_), channel_id=1, source_target_pairs={{0,4},{1,5},{2,6},{3,7},{4,8},{5,9},{6,10},{7,11},{8,12},{9,13},{1... | collective-permute-start | bytes 393224 | tf_op jit(solution)/shard_map/ppermute | solution.py:23
  40.8 5.6 %collective-permute-start.15 = (bf16[256,256]{1,0:T(8,128)(2,1)S(1)}, bf16[256,256]{1,0:T(8,128)(2,1)S(1)}, u32[]{:S(2)}, u32[]{:S(2)}) collective-permute-start(bf16[256,256]{1,0:T(8,128)(2,1)S(1)} %collective-permute-done.11.refs_0_), channel_id=1, source_target_pairs={{0,2},{1,3},{2,0},{3,1},{4,6},{5,7},{6,4},{7,5},{8,10},{9,11},{10,... | collective-permute-start | bytes 393224 | tf_op jit(solution)/shard_map/ppermute | solution.py:23
  43.8 5.0 %collective-permute-start.16 = (bf16[256,256]{1,0:T(8,128)(2,1)S(1)}, bf16[256,256]{1,0:T(8,128)(2,1)S(1)}, u32[]{:S(2)}, u32[]{:S(2)}) collective-permute-start(bf16[256,256]{1,0:T(8,128)(2,1)S(1)} %collective-permute-done.12.refs_1_), channel_id=1, source_target_pairs={{0,2},{1,3},{2,0},{3,1},{4,6},{5,7},{6,4},{7,5},{8,10},{9,11},{10,... | collective-permute-start | bytes 393224 | tf_op jit(solution)/shard_map/ppermute | solution.py:23
  45.1 5.0 %collective-permute-start.13 = (bf16[256,256]{1,0:T(8,128)(2,1)S(1)}, bf16[256,256]{1,0:T(8,128)(2,1)S(1)}, u32[]{:S(2)}, u32[]{:S(2)}) collective-permute-start(bf16[256,256]{1,0:T(8,128)(2,1)S(1)} %collective-permute-done.11.refs_0_), channel_id=1, source_target_pairs={{0,1},{1,0},{2,3},{3,2},{4,5},{5,4},{6,7},{7,6},{8,9},{9,8},{10,11... | collective-permute-start | bytes 393224 | tf_op jit(solution)/shard_map/ppermute | solution.py:23
  46.3 3.8 %collective-permute-start.14 = (bf16[256,256]{1,0:T(8,128)(2,1)S(1)}, bf16[256,256]{1,0:T(8,128)(2,1)S(1)}, u32[]{:S(2)}, u32[]{:S(2)}) collective-permute-start(bf16[256,256]{1,0:T(8,128)(2,1)S(1)} %collective-permute-done.12.refs_1_), channel_id=1, source_target_pairs={{0,1},{1,0},{2,3},{3,2},{4,5},{5,4},{6,7},{7,6},{8,9},{9,8},{10,11... | collective-permute-start | bytes 393224 | tf_op jit(solution)/shard_map/ppermute | solution.py:23
  46.4 3.7 %collective-permute-start.17 = (bf16[256,256]{1,0:T(8,128)(2,1)S(1)}, bf16[256,256]{1,0:T(8,128)(2,1)S(1)}, u32[]{:S(2)}, u32[]{:S(2)}) collective-permute-start(bf16[256,256]{1,0:T(8,128)(2,1)S(1)} %collective-permute-done.15.refs_4_), channel_id=1, source_target_pairs={{0,1},{1,0},{2,3},{3,2},{4,5},{5,4},{6,7},{7,6},{8,9},{9,8},{10,11... | collective-permute-start | bytes 393224 | tf_op jit(solution)/shard_map/ppermute | solution.py:23
  48.8 2.3 %collective-permute-start.18 = (bf16[256,256]{1,0:T(8,128)(2,1)S(1)}, bf16[256,256]{1,0:T(8,128)(2,1)S(1)}, u32[]{:S(2)}, u32[]{:S(2)}) collective-permute-start(bf16[256,256]{1,0:T(8,128)(2,1)S(1)} %collective-permute-done.16.refs_5_), channel_id=1, source_target_pairs={{0,1},{1,0},{2,3},{3,2},{4,5},{5,4},{6,7},{7,6},{8,9},{9,8},{10,11... | collective-permute-start | bytes 393224 | tf_op jit(solution)/shard_map/ppermute | solution.py:23

commit v6 on v5

--- a/solution.py
+++ b/solution.py
@@ -83,83 +83,114 @@
     return jnp.dot(a, b, preferred_element_type=jnp.float32)
 
 
-def group_kernel(count, group, groups, masked, chunks, *refs):
-    shares, (in_idx, out_idx, blocks, sides) = refs[:count], refs[count : count + 4]
-    refs = refs[count + 4 :]
+def rows_of(ref, i, size):
+    return ref[pl.ds(i * size, size), :]
+
+
+def row_sum(blocks, first, i, source, places):
+    size, n = blocks.shape[1], len(places)
+    lhs = [rows_of(blocks, first + i * n + k, size) for k in range(n)]
+    rhs = [source[pl.ds(pl.multiple_of(p * size, size), size), :] for p in places]
+    return dot(jnp.concatenate(lhs, axis=1), jnp.concatenate(rhs, axis=0))
+
+
+def finish(blocks, first, out_idx, sides, cols, val, sol, f_refs, write):
+    rows_out, out_links = out_idx.shape
+    size = blocks.shape[1]
+    rows_in = val.shape[0] // size
+    out_at = first + rows_in
+    last_at = out_at + rows_out * out_links
+    some, each = rows_in // PARTS, rows_out // len(f_refs)
+    where = out_idx[...]
+    for i in range(rows_in):
+        at = pl.ds(i * size, size)
+        sol[at, :] = dot(rows_of(blocks, first + i, size), val[at, :]).astype(sol.dtype)
+        if write and (i + 1) % some == 0:
+            start, count = (i + 1 - some) * size, some * size
+            write(sol.at[pl.ds(start, count), :], 0, start, count)
+    for j in range(rows_out):
+        at = pl.ds(j * size, size)
+        places = [where[j, k] for k in range(out_links)]
+        outgoing = row_sum(blocks, out_at, j, sol, places)
+        side = sides[pl.ds((rows_in + j) * size, size), cols].astype(jnp.float32)
+        val[at, :] = (side - outgoing).astype(val.dtype)
+    for c, f_ref in enumerate(f_refs):
+        for j in range(each):
+            row = c * each + j
+            value = dot(rows_of(blocks, last_at + row, size), rows_of(val, row, size))
+            f_ref[pl.ds(j * size, size), :] = value.astype(f_ref.dtype)
+        if write:
+            write(f_ref, 1, c * each * size, each * size)
+
+
+def writer(targets, cols, sems):
+    copies = []
+
+    def write(source, target, first, count):
+        there = targets[target].at[pl.ds(first, count), cols]
+        copies.append(pltpu.make_async_copy(source, there, sems.at[len(copies)]))
+        copies[-1].start()
+
+    return write, copies
+
+
+def group_kernel(pieces, group, groups, chunks, *refs):
+    shares, (in_idx, out_idx, blocks, sides) = refs[:pieces], refs[pieces : pieces + 4]
     done = group + 1 == groups
     if done:
         sol_hbm, fsol_hbm, sol, *f_refs, inc, val, sems = refs[-6 - chunks :]
     else:
         sol, *f_refs, inc, val = refs[-3 - chunks :]
     links, rows_in = in_idx.shape
-    rows_out, out_links = out_idx.shape
     size = blocks.shape[1]
     part, width = shares[0].shape
-    each = rows_out // chunks
-    inv_at = rows_in * links
-    out_at = inv_at + rows_in
-    last_at = out_at + rows_out * out_links
-    swap = lax.axis_index("sub") * rows_out
     cols = pl.ds(group * width, width)
-    copies = []
-
-    def write(source, target, first, count):
-        there = target.at[pl.ds(first, count), cols]
-        copies.append(pltpu.make_async_copy(source, there, sems.at[len(copies)]))
-        copies[-1].start()
-
-    keep = lax.axis_index("slab") > 0
-    for r, ref in enumerate(shares):
-        value = ref[...]
-        if masked:
-            value = jnp.where(keep, value, jnp.zeros_like(value))
-        inc[pl.ds(r * part, part), :] = value
-
-    def at(i):
-        return pl.ds(i * size, size)
-
-    def side(i):
-        return sides[at(i), cols].astype(jnp.float32)
-
-    def block(i):
-        return blocks[at(i), :]
-
-    def picked(ref, block):
-        return ref[pl.ds(pl.multiple_of(block * size, size), size), :]
-
-    def row_of(first, i, source, places):
-        n = len(places)
-        lhs = [block(first + i * n + k) for k in range(n)]
-        rhs = [picked(source, p) for p in places]
-        return dot(jnp.concatenate(lhs, axis=1), jnp.concatenate(rhs, axis=0))
-
-    for i in range(rows_in):
-        coupled = row_of(0, i, inc, [in_idx[k, i] ^ swap for k in range(links)])
-        val[at(i), :] = (side(i) - coupled).astype(val.dtype)
-    some = rows_in // PARTS
-    for i in range(rows_in):
-        sol[at(i), :] = dot(block(inv_at + i), val[at(i), :]).astype(sol.dtype)
-        if done and (i + 1) % some == 0:
-            start, count = (i + 1 - some) * size, some * size
-            piece = sol.at[pl.ds(start, count), :]
-            write(piece, sol_hbm, start, count)
-    for j in range(rows_out):
-        outgoing = row_of(out_at, j, sol, [out_idx[j, k] for k in range(out_links)])
-        val[at(j), :] = (side(rows_in + j) - outgoing).astype(val.dtype)
-    for c, f_ref in enumerate(f_refs):
-        for j in range(each):
-            row = c * each + j
-            f_ref[at(j), :] = dot(block(last_at + row), val[at(row), :]).astype(
-                f_ref.dtype
-            )
-        if done:
-            count = each * size
-            write(f_ref, fsol_hbm, c * count, count)
-    for c in copies:
-        c.wait()
-
-
-def group_of(shares, in_idx, out_idx, blocks, sides, outs, token, group, groups, masked):
+    swap = lax.axis_index("sub") * out_idx.shape[0]
+    behind = lax.axis_index("slab") > 0
+
+    def couple():
+        for r, ref in enumerate(shares):
+            inc[pl.ds(r * part, part), :] = ref[...]
+        where = in_idx[...] ^ swap
+        for i in range(rows_in):
+            at = pl.ds(i * size, size)
+            places = [where[k, i] for k in range(links)]
+            coupled = row_sum(blocks, 0, i, inc, places)
+            value = sides[at, cols].astype(jnp.float32) - coupled
+            val[at, :] = value.astype(val.dtype)
+
+    def rest(write=None):
+        finish(
+            blocks, rows_in * links, out_idx, sides, cols, val, sol, f_refs, write
+        )
+
+    if done:
+
+        def whole():
+            couple()
+            write, copies = writer((sol_hbm, fsol_hbm), cols, sems)
+            rest(write)
+            for c in copies:
+                c.wait()
+
+        if group == 0:
+            whole()
+        else:
+            pl.when(behind)(whole)
+        return
+    if group == 0:
+        couple()
+    else:
+        pl.when(behind)(couple)
+
+        @pl.when(jnp.logical_not(behind))
+        def _():
+            val[...] = sides[pl.ds(0, rows_in * size), cols]
+
+    rest()
+
+
+def group_of(shares, in_idx, out_idx, blocks, sides, outs, token, group, groups):
     width = shares[0].shape[1]
     links, rows_in = in_idx.shape
     rows_out, out_links = out_idx.shape
@@ -168,7 +199,6 @@
     chunks = 2 if rows_out % 2 == 0 else 1
     pieces = len(shares)
     count = rows_in * (links + 1) + rows_out * (out_links + 1)
-    smem = pl.BlockSpec(memory_space=pltpu.SMEM)
     vmem = pl.BlockSpec(memory_space=VMEM)
     hbm = pl.BlockSpec(memory_space=pl.ANY)
     done = group + 1 == groups
@@ -176,8 +206,8 @@
     def held(arrays):
         return [pltpu.with_memory_space_constraint(a, VMEM) for a in arrays]
 
-    operands = held(shares) + [in_idx, out_idx] + held([blocks, sides])
-    in_specs = [vmem] * pieces + [smem] * 2 + [vmem] * 2
+    operands = held([*shares, in_idx, out_idx, blocks, sides])
+    in_specs = [vmem] * len(operands)
     aliases = {len(operands) + n: n for n in range(len(outs))}
     operands += [*outs] if token is None else [*outs, token]
     in_specs += [hbm] * (len(operands) - len(in_specs))
@@ -194,7 +224,7 @@
         out_shape = [pltpu.HBM((r, wide), dtype) for r in (rows, front_rows)]
         out_specs = [hbm, hbm]
     return pl.pallas_call(
-        functools.partial(group_kernel, pieces, group, groups, masked, chunks),
+        functools.partial(group_kernel, pieces, group, groups, chunks),
         out_shape=tuple(out_shape),
         in_specs=in_specs,
         out_specs=tuple(out_specs),
@@ -210,40 +240,66 @@
     )(*operands)
 
 
-def flush_kernel(count, column, *refs):
-    sources, (sol_hbm, fsol_hbm, sems) = refs[:count], refs[-3:]
-    copies, row = [], 0
+def flush_kernel(count, column, ahead, *refs):
+    sources = refs[:count]
+    width = sources[0].shape[1]
+    if ahead:
+        out_idx, blocks, sides = refs[count : count + 3]
+        *outs, val, sol = refs[-5 - count : -1 - count]
+        *f_refs, more, sems = refs[-1 - count :]
+    else:
+        *outs, sems = refs[-3:]
+    write, copies = writer(outs, pl.ds(column * width, width), sems)
+    row = 0
     for n, ref in enumerate(sources):
-        rows, width = ref.shape
-        out = fsol_hbm if n else sol_hbm
-        there = out.at[pl.ds(row, rows), pl.ds(column * width, width)]
+        rows = ref.shape[0]
+        write(ref, min(n, 1), row, rows)
         row += rows if n else 0
-        copies.append(pltpu.make_async_copy(ref, there, sems.at[n]))
-        copies[-1].start()
+    if ahead:
+
+        @pl.when(lax.axis_index("slab") == 0)
+        def _():
+            cols = pl.ds((column + 1) * width, width)
+            to, made = writer(outs, cols, more)
+            val[...] = sides[pl.ds(0, val.shape[0]), cols]
+            size = blocks.shape[1]
+            rows_out, links = out_idx.shape
+            later = val.shape[0] // size + rows_out * (links + 1)
+            first = blocks.shape[0] // size - later
+            finish(blocks, first, out_idx, sides, cols, val, sol, f_refs, to)
+            for c in made:
+                c.wait()
+
     for c in copies:
         c.wait()
 
 
-def flushed(sources, outs, column, groups):
+def flushed(sources, out_idx, blocks, sides, outs, column, groups):
     n, dtype = len(sources), sources[0].dtype
-    wide = groups * sources[0].shape[1]
+    wide = sides.shape[1]
     rows = (sources[0].shape[0], sum(f.shape[0] for f in sources[1:]))
     hbm = pl.BlockSpec(memory_space=pl.ANY)
+    vmem = pl.BlockSpec(memory_space=VMEM)
+    ahead = column + 2 == groups
+    ins = [*sources, out_idx, blocks, sides] if ahead else [*sources]
+    held = [pltpu.with_memory_space_constraint(a, VMEM) for a in ins]
+    own = [VMEM(sources[0].shape, dtype), *[VMEM(a.shape, dtype) for a in sources]]
+    own.append(pltpu.SemaphoreType.DMA((PARTS + n - 1,)))
     return pl.pallas_call(
-        functools.partial(flush_kernel, n, column),
+        functools.partial(flush_kernel, n, column, ahead),
         out_shape=tuple(pltpu.HBM((r, wide), dtype) for r in rows),
-        in_specs=[pl.BlockSpec(memory_space=VMEM)] * n + [hbm] * len(outs),
+        in_specs=[vmem] * len(ins) + [hbm] * len(outs),
         out_specs=(hbm, hbm),
-        scratch_shapes=[pltpu.SemaphoreType.DMA((n,))],
-        input_output_aliases={n + k: k for k in range(len(outs))},
+        scratch_shapes=own * ahead + [pltpu.SemaphoreType.DMA((n,))],
+        input_output_aliases={len(ins) + k: k for k in range(len(outs))},
         compiler_params=pltpu.CompilerParams(vmem_limit_bytes=SCOPED),
         cost_estimate=pl.CostEstimate(
             flops=0,
-            bytes_accessed=2 * sum(s.size for s in sources) * dtype.itemsize,
+            bytes_accessed=2 * sum(a.size for a in sources) * dtype.itemsize,
             transcendentals=0,
         ),
         name=f"flush_{column}",
-    )(*[pltpu.with_memory_space_constraint(s, VMEM) for s in sources], *outs)
+    )(*held, *outs)
 
 
 def shards(
@@ -279,12 +335,11 @@
             token if group == 0 else None,
             group,
             groups,
-            0 < group and group + 1 < groups,
         )
         if group + 1 < groups:
-            ring = group + 2 < groups
+            ring = True
             hops = [permuted(f, slabs, subs, 1, 0, ring) for f in made[1:]]
-            outs = flushed(made, outs, group, groups)
+            outs = flushed(made, out_idx, blocks, sides, outs, group, groups)
             chunks = []
             for n, hop in enumerate(hops):
                 chunk, ahead = gathered(hop, slabs, subs, None if n else outs)

time: 54.8 us -> 51.9 us (0.947)
  starting transfers between devices: 19.8 us -> 16.4 us
  waiting for transfers between devices: 19.4 us -> 21 us
  Pallas kernels: 14.7 us -> 13.2 us
    ppermute x19, starting transfers between devices: 19.8 us -> 16.4 us  [permuted(): return lax.ppermute(x, AXES, pairs)]
    ppermute x19, waiting for transfers between devices: 19.4 us -> 21 us  [permuted(): return lax.ppermute(x, AXES, pairs)]
    pallas_call x5, Pallas kernels: 11.1 us -> 9.65 us  [the longest x3 7.49 us: group_of(): pl.pallas_call(functools.partial(group_kernel, pieces, group, groups, chu...]
  transfers between devices with their start and end apart: 19 -> 19, of which waited for: 11 -> 11; matrix products, arithmetic and copies ran while one was open for 0% -> 0% of each run, Pallas kernels for 10% -> 11%
where the time goes in v6:
time: 51.9 us; the launch traced here: 51.3 us
  waiting for transfers between devices  21 us (40%)
  starting transfers between devices  16.4 us (32%)
  Pallas kernels  13.2 us (25%)
  between operations  0.7 us (1%)
    ppermute x19, waiting for transfers between devices, permuted(): return lax.ppermute(x, AXES, pairs)  21 us
    ppermute x19, starting transfers between devices, permuted(): return lax.ppermute(x, AXES, pairs)  16.4 us
    pallas_call x3, Pallas kernels, group_of(): pl.pallas_call(functools.partial(group_kernel, pieces, group, groups, chu...  7.49 us
    pallas_call x1, Pallas kernels, staged(): pl.pallas_call(functools.partial(stage_kernel, counts), out_shape=(*(VMEM...  3.58 us
    pallas_call x2, Pallas kernels, flushed(): pl.pallas_call(functools.partial(flush_kernel, n, column, ahead), out_sha...  2.16 us
  transfers between devices with their start and end apart: 19, of which 11 were waited for; matrix products, arithmetic and copies ran while one was open for 0% of the time, Pallas kernels for 11%

profile of v6, /device:TPU:11, one launch (start us, length us, event | category | flops | bytes accessed | tf_op | source)
XLA Modules:
  0.0 51.3 jit_solution(1837547058553381664)
XLA Ops:
  0.6 0.3 collective-permute-start.1
  1.0 1.0 %collective-permute-start = (bf16[512,256]{1,0:T(8,128)(2,1)}, bf16[512,256]{1,0:T(8,128)(2,1)S(1)}, u32[]{:S(2)}, u32[]{:S(2)}) collective-permute-start(bf16[512,256]{1,0:T(8,128)(2,1)} %refs_0_.1), channel_id=1, source_target_pairs={{0,1},{1,0},{2,3},{3,2},{4,5},{5,4},{6,7},{7,6},{8,9},{9,8},{10,11... | collective-permute-start | bytes 786440 | tf_op jit(solution)/shard_map/ppermute | solution.py:23
  1.9 0.0 copy-start
  1.9 3.6 %stage.1 = (bf16[18944,128]{1,0:T(8,128)(2,1)S(1)}, bf16[2560,768]{1,0:T(8,128)(2,1)S(1)}, f32[8,128]{1,0:T(8,128)S(1)}) custom-call(bf16[12288,128]{1,0:T(8,128)(2,1)} %bitcast.8, bf16[2048,128]{1,0:T(8,128)(2,1)} %bitcast.10, bf16[4096,128]{1,0:T(8,128)(2,1)} %bitcast.9, bf16[512,128]{1,0:T(8,128)(2,1)} %bitcast.11, bf16[2048,768]{1,0:T(8,128)(2,1)} %refs_4_.1, ...), custom_call_target="tpu_custom_call" | custom-call | bytes 17563648 | tf_op jit(solution)/shard_map/stage/pallas_call | solution.py:65
  5.5 2.6 %collective-permute-done.1.refs_2_ = bf16[512,256]{1,0:T(8,128)(2,1)S(1)} collective-permute-done((bf16[512,256]{1,0:T(8,128)(2,1)}, bf16[512,256]{1,0:T(8,128)(2,1)S(1)}, u32[]{:S(2)}, u32[]{:S(2)}) %collective-permute-start.1) | collective-permute-done | bytes 262176 | tf_op jit(solution)/shard_map/ppermute | solution.py:23
  8.1 1.5 %collective-permute-start.2 = (bf16[512,256]{1,0:T(8,128)(2,1)S(1)}, bf16[512,256]{1,0:T(8,128)(2,1)S(1)}, u32[]{:S(2)}, u32[]{:S(2)}) collective-permute-start(bf16[512,256]{1,0:T(8,128)(2,1)S(1)} %collective-permute-done.1.refs_2_), channel_id=1, source_target_pairs={{0,1},{1,0},{2,3},{3,2},{4,5},{5,4},{6,7},{7,6},{8,9},{9,8},{10,11... | collective-permute-start | bytes 786440 | tf_op jit(solution)/shard_map/ppermute | solution.py:23
  9.6 0.0 collective-permute-done.refs_1_
  9.6 1.2 %collective-permute-done.2.refs_3_ = bf16[512,256]{1,0:T(8,128)(2,1)S(1)} collective-permute-done((bf16[512,256]{1,0:T(8,128)(2,1)S(1)}, bf16[512,256]{1,0:T(8,128)(2,1)S(1)}, u32[]{:S(2)}, u32[]{:S(2)}) %collective-permute-start.2) | collective-permute-done | bytes 262176 | tf_op jit(solution)/shard_map/ppermute | solution.py:23
  10.8 0.0 copy-done
  10.8 0.0 copy-done.1
  10.8 0.0 copy-done.2
  10.8 2.2 %group_0.1 = (bf16[2048,256]{1,0:T(8,128)(2,1)S(1)}, bf16[256,256]{1,0:T(8,128)(2,1)S(1)}, bf16[256,256]{1,0:T(8,128)(2,1)S(1)}) custom-call(bf16[512,256]{1,0:T(8,128)(2,1)S(1)} %copy-done, bf16[512,256]{1,0:T(8,128)(2,1)S(1)} %collective-permute-done.refs_1_, bf16[512,256]{1,0:T(8,128)(2,1)S(1)} %collective-permute-done.1.refs_2_, ...), custom_call_target="tpu_custom_call" | custom-call | flops 1241513984 | bytes 6946816 | tf_op jit(solution)/shard_map/group_0/pallas_call | solution.py:226
  13.0 1.3 %collective-permute-start.3 = (bf16[256,256]{1,0:T(8,128)(2,1)S(1)}, bf16[256,256]{1,0:T(8,128)(2,1)S(1)}, u32[]{:S(2)}, u32[]{:S(2)}) collective-permute-start(bf16[256,256]{1,0:T(8,128)(2,1)S(1)} %get-tuple-element.28.refs_1_), channel_id=1, source_target_pairs={{0,4},{1,5},{2,6},{3,7},{4,8},{5,9},{6,10},{7,11},{8,12},{9,13},{1... | collective-permute-start | bytes 393224 | tf_op jit(solution)/shard_map/ppermute | solution.py:23
  14.3 1.2 %collective-permute-start.4 = (bf16[256,256]{1,0:T(8,128)(2,1)S(1)}, bf16[256,256]{1,0:T(8,128)(2,1)S(1)}, u32[]{:S(2)}, u32[]{:S(2)}) collective-permute-start(bf16[256,256]{1,0:T(8,128)(2,1)S(1)} %get-tuple-element.29.refs_2_), channel_id=1, source_target_pairs={{0,4},{1,5},{2,6},{3,7},{4,8},{5,9},{6,10},{7,11},{8,12},{9,13},{1... | collective-permute-start | bytes 393224 | tf_op jit(solution)/shard_map/ppermute | solution.py:23
  15.6 3.1 %collective-permute-done.3.refs_0_ = bf16[256,256]{1,0:T(8,128)(2,1)S(1)} collective-permute-done((bf16[256,256]{1,0:T(8,128)(2,1)S(1)}, bf16[256,256]{1,0:T(8,128)(2,1)S(1)}, u32[]{:S(2)}, u32[]{:S(2)}) %collective-permute-start.3) | collective-permute-done | bytes 131104 | tf_op jit(solution)/shard_map/ppermute | solution.py:23
  18.7 0.3 collective-permute-start.7
  18.9 2.5 %collective-permute-done.4.refs_1_ = bf16[256,256]{1,0:T(8,128)(2,1)S(1)} collective-permute-done((bf16[256,256]{1,0:T(8,128)(2,1)S(1)}, bf16[256,256]{1,0:T(8,128)(2,1)S(1)}, u32[]{:S(2)}, u32[]{:S(2)}) %collective-permute-start.4) | collective-permute-done | bytes 131104 | tf_op jit(solution)/shard_map/ppermute | solution.py:23
  21.5 0.3 collective-permute-start.8
  21.8 1.1 %flush_0.1 = (bf16[2048,768]{1,0:T(8,128)(2,1)}, bf16[512,768]{1,0:T(8,128)(2,1)}) custom-call(bf16[2048,256]{1,0:T(8,128)(2,1)S(1)} %get-tuple-element.30.refs_0_, bf16[256,256]{1,0:T(8,128)(2,1)S(1)} %get-tuple-element.28.refs_1_, bf16[256,256]{1,0:T(8,128)(2,1)S(1)} %get-tuple-element.29.refs_2_), custom_call_target="tpu_custom_call" | custom-call | bytes 2621440 | tf_op jit(solution)/shard_map/flush_0/pallas_call | solution.py:288
  22.8 1.5 %collective-permute-start.5 = (bf16[256,256]{1,0:T(8,128)(2,1)S(1)}, bf16[256,256]{1,0:T(8,128)(2,1)S(1)}, u32[]{:S(2)}, u32[]{:S(2)}) collective-permute-start(bf16[256,256]{1,0:T(8,128)(2,1)S(1)} %collective-permute-done.3.refs_0_), channel_id=1, source_target_pairs={{0,1},{1,0},{2,3},{3,2},{4,5},{5,4},{6,7},{7,6},{8,9},{9,8},{10,11... | collective-permute-start | bytes 393224 | tf_op jit(solution)/shard_map/ppermute | solution.py:23
  24.4 0.1 collective-permute-start.6
  24.5 0.0 collective-permute-done.7.refs_4_
  24.5 2.5 %collective-permute-done.8.refs_5_ = bf16[256,256]{1,0:T(8,128)(2,1)S(1)} collective-permute-done((bf16[256,256]{1,0:T(8,128)(2,1)S(1)}, bf16[256,256]{1,0:T(8,128)(2,1)S(1)}, u32[]{:S(2)}, u32[]{:S(2)}) %collective-permute-start.8) | collective-permute-done | bytes 131104 | tf_op jit(solution)/shard_map/ppermute | solution.py:23
  27.0 1.5 %collective-permute-start.10 = (bf16[256,256]{1,0:T(8,128)(2,1)S(1)}, bf16[256,256]{1,0:T(8,128)(2,1)S(1)}, u32[]{:S(2)}, u32[]{:S(2)}) collective-permute-start(bf16[256,256]{1,0:T(8,128)(2,1)S(1)} %collective-permute-done.8.refs_5_), channel_id=1, source_target_pairs={{0,1},{1,0},{2,3},{3,2},{4,5},{5,4},{6,7},{7,6},{8,9},{9,8},{10,11... | collective-permute-start | bytes 393224 | tf_op jit(solution)/shard_map/ppermute | solution.py:23
  28.5 0.0 collective-permute-start.9
  28.5 0.0 collective-permute-done.5.refs_2_
  28.5 0.0 collective-permute-done.6.refs_3_
  28.5 1.0 %collective-permute-done.10.refs_7_ = bf16[256,256]{1,0:T(8,128)(2,1)S(1)} collective-permute-done((bf16[256,256]{1,0:T(8,128)(2,1)S(1)}, bf16[256,256]{1,0:T(8,128)(2,1)S(1)}, u32[]{:S(2)}, u32[]{:S(2)}) %collective-permute-start.10) | collective-permute-done | bytes 131104 | tf_op jit(solution)/shard_map/ppermute | solution.py:23
  29.5 0.4 collective-permute-done.9.refs_6_
  29.8 2.3 %group_1.1 = (bf16[2048,256]{1,0:T(8,128)(2,1)S(1)}, bf16[256,256]{1,0:T(8,128)(2,1)S(1)}, bf16[256,256]{1,0:T(8,128)(2,1)S(1)}) custom-call(bf16[256,256]{1,0:T(8,128)(2,1)S(1)} %collective-permute-done.3.refs_0_, bf16[256,256]{1,0:T(8,128)(2,1)S(1)} %collective-permute-done.4.refs_1_, bf16[256,256]{1,0:T(8,128)(2,1)S(1)} %collective-permute-done.5.refs_2_, ...), custom_call_target="tpu_custom_call" | custom-call | flops 1241513984 | bytes 6946816 | tf_op jit(solution)/shard_map/group_1/pallas_call | solution.py:226
  32.1 0.4 collective-permute-start.11
  32.5 2.1 %collective-permute-start.12 = (bf16[256,256]{1,0:T(8,128)(2,1)S(1)}, bf16[256,256]{1,0:T(8,128)(2,1)S(1)}, u32[]{:S(2)}, u32[]{:S(2)}) collective-permute-start(bf16[256,256]{1,0:T(8,128)(2,1)S(1)} %get-tuple-element.35.refs_2_), channel_id=1, source_target_pairs={{0,4},{1,5},{2,6},{3,7},{4,8},{5,9},{6,10},{7,11},{8,12},{9,13},{1... | collective-permute-start | bytes 393224 | tf_op jit(solution)/shard_map/ppermute | solution.py:23
  34.7 3.3 %collective-permute-done.11.refs_0_ = bf16[256,256]{1,0:T(8,128)(2,1)S(1)} collective-permute-done((bf16[256,256]{1,0:T(8,128)(2,1)S(1)}, bf16[256,256]{1,0:T(8,128)(2,1)S(1)}, u32[]{:S(2)}, u32[]{:S(2)}) %collective-permute-start.11) | collective-permute-done | bytes 131104 | tf_op jit(solution)/shard_map/ppermute | solution.py:23
  38.0 0.3 collective-permute-start.15
  38.3 2.5 %collective-permute-done.12.refs_1_ = bf16[256,256]{1,0:T(8,128)(2,1)S(1)} collective-permute-done((bf16[256,256]{1,0:T(8,128)(2,1)S(1)}, bf16[256,256]{1,0:T(8,128)(2,1)S(1)}, u32[]{:S(2)}, u32[]{:S(2)}) %collective-permute-start.12) | collective-permute-done | bytes 131104 | tf_op jit(solution)/shard_map/ppermute | solution.py:23
  40.8 0.3 collective-permute-start.16
  41.1 1.1 %flush_1.1 = (bf16[2048,768]{1,0:T(8,128)(2,1)}, bf16[512,768]{1,0:T(8,128)(2,1)}) custom-call(bf16[2048,256]{1,0:T(8,128)(2,1)S(1)} %get-tuple-element.36.refs_0_, bf16[256,256]{1,0:T(8,128)(2,1)S(1)} %get-tuple-element.34.refs_1_, bf16[256,256]{1,0:T(8,128)(2,1)S(1)} %get-tuple-element.35.refs_2_, ...), custom_call_target="tpu_custom_call", output_to_operand_aliasing={{0}: (6, {}), {1}: (7, {})} | custom-call | bytes 2621440 | tf_op jit(solution)/shard_map/flush_1/pallas_call | solution.py:288
  42.2 1.3 %collective-permute-start.13 = (bf16[256,256]{1,0:T(8,128)(2,1)S(1)}, bf16[256,256]{1,0:T(8,128)(2,1)S(1)}, u32[]{:S(2)}, u32[]{:S(2)}) collective-permute-start(bf16[256,256]{1,0:T(8,128)(2,1)S(1)} %collective-permute-done.11.refs_0_), channel_id=1, source_target_pairs={{0,1},{1,0},{2,3},{3,2},{4,5},{5,4},{6,7},{7,6},{8,9},{9,8},{10,11... | collective-permute-start | bytes 393224 | tf_op jit(solution)/shard_map/ppermute | solution.py:23
  43.5 0.1 collective-permute-start.14
  43.6 0.0 collective-permute-done.15.refs_4_
  43.6 1.6 %collective-permute-start.17 = (bf16[256,256]{1,0:T(8,128)(2,1)S(1)}, bf16[256,256]{1,0:T(8,128)(2,1)S(1)}, u32[]{:S(2)}, u32[]{:S(2)}) collective-permute-start(bf16[256,256]{1,0:T(8,128)(2,1)S(1)} %collective-permute-done.15.refs_4_), channel_id=1, source_target_pairs={{0,1},{1,0},{2,3},{3,2},{4,5},{5,4},{6,7},{7,6},{8,9},{9,8},{10,11... | collective-permute-start | bytes 393224 | tf_op jit(solution)/shard_map/ppermute | solution.py:23
  45.2 0.9 %collective-permute-done.16.refs_5_ = bf16[256,256]{1,0:T(8,128)(2,1)S(1)} collective-permute-done((bf16[256,256]{1,0:T(8,128)(2,1)S(1)}, bf16[256,256]{1,0:T(8,128)(2,1)S(1)}, u32[]{:S(2)}, u32[]{:S(2)}) %collective-permute-start.16) | collective-permute-done | bytes 131104 | tf_op jit(solution)/shard_map/ppermute | solution.py:23
  46.1 1.3 %collective-permute-start.18 = (bf16[256,256]{1,0:T(8,128)(2,1)S(1)}, bf16[256,256]{1,0:T(8,128)(2,1)S(1)}, u32[]{:S(2)}, u32[]{:S(2)}) collective-permute-start(bf16[256,256]{1,0:T(8,128)(2,1)S(1)} %collective-permute-done.16.refs_5_), channel_id=1, source_target_pairs={{0,1},{1,0},{2,3},{3,2},{4,5},{5,4},{6,7},{7,6},{8,9},{9,8},{10,11... | collective-permute-start | bytes 393224 | tf_op jit(solution)/shard_map/ppermute | solution.py:23
  47.4 0.0 collective-permute-done.13.refs_2_
  47.4 0.0 collective-permute-done.14.refs_3_
  47.4 0.0 collective-permute-done.17.refs_6_
  47.4 1.0 %collective-permute-done.18.refs_7_ = bf16[256,256]{1,0:T(8,128)(2,1)S(1)} collective-permute-done((bf16[256,256]{1,0:T(8,128)(2,1)S(1)}, bf16[256,256]{1,0:T(8,128)(2,1)S(1)}, u32[]{:S(2)}, u32[]{:S(2)}) %collective-permute-start.18) | collective-permute-done | bytes 131104 | tf_op jit(solution)/shard_map/ppermute | solution.py:23
  48.4 3.0 %group_2.1 = (bf16[2048,768]{1,0:T(8,128)(2,1)}, bf16[512,768]{1,0:T(8,128)(2,1)}) custom-call(bf16[256,256]{1,0:T(8,128)(2,1)S(1)} %collective-permute-done.11.refs_0_, bf16[256,256]{1,0:T(8,128)(2,1)S(1)} %collective-permute-done.12.refs_1_, bf16[256,256]{1,0:T(8,128)(2,1)S(1)} %collective-permute-done.13.refs_2_, ...), custom_call_target="tpu_custom_call", output_to_operand_aliasing={{0}: (12, {}), {1}: (13, {})} | custom-call | flops 1241513984 | bytes 6946816 | tf_op jit(solution)/shard_map/group_2/pallas_call | solution.py:226
  (2 shorter events, 0.0 us)
Async XLA Ops:
  0.6 7.5 %collective-permute-start.1 = (bf16[512,256]{1,0:T(8,128)(2,1)}, bf16[512,256]{1,0:T(8,128)(2,1)S(1)}, u32[]{:S(2)}, u32[]{:S(2)}) collective-permute-start(bf16[512,256]{1,0:T(8,128)(2,1)} %refs_0_.1), channel_id=1, source_target_pairs={{0,2},{1,3},{2,0},{3,1},{4,6},{5,7},{6,4},{7,5},{8,10},{9,11},{10,... | collective-permute-start | bytes 786440 | tf_op jit(solution)/shard_map/ppermute | solution.py:23
  1.0 8.7 %collective-permute-start = (bf16[512,256]{1,0:T(8,128)(2,1)}, bf16[512,256]{1,0:T(8,128)(2,1)S(1)}, u32[]{:S(2)}, u32[]{:S(2)}) collective-permute-start(bf16[512,256]{1,0:T(8,128)(2,1)} %refs_0_.1), channel_id=1, source_target_pairs={{0,1},{1,0},{2,3},{3,2},{4,5},{5,4},{6,7},{7,6},{8,9},{9,8},{10,11... | collective-permute-start | bytes 786440 | tf_op jit(solution)/shard_map/ppermute | solution.py:23
  1.9 8.9 %copy-start = (bf16[512,256]{1,0:T(8,128)(2,1)S(1)}, bf16[512,256]{1,0:T(8,128)(2,1)}, u32[]{:S(2)}) copy-start(bf16[512,256]{1,0:T(8,128)(2,1)} %refs_0_.1) | copy-start | bytes 786436
  1.9 8.9 %copy-start.1 = (s32[16,6]{0,1:T(8,128)S(1)}, s32[16,6]{0,1:T(8,128)}, u32[]{:S(2)}) copy-start(s32[16,6]{0,1:T(8,128)} %param.12) | copy-start | bytes 1156
  1.9 8.9 %copy-start.2 = (s32[4,8]{1,0:T(4,128)S(1)}, s32[4,8]{1,0:T(4,128)}, u32[]{:S(2)}) copy-start(s32[4,8]{1,0:T(4,128)} %refs_9_.3) | copy-start | bytes 388
  8.1 2.7 %collective-permute-start.2 = (bf16[512,256]{1,0:T(8,128)(2,1)S(1)}, bf16[512,256]{1,0:T(8,128)(2,1)S(1)}, u32[]{:S(2)}, u32[]{:S(2)}) collective-permute-start(bf16[512,256]{1,0:T(8,128)(2,1)S(1)} %collective-permute-done.1.refs_2_), channel_id=1, source_target_pairs={{0,1},{1,0},{2,3},{3,2},{4,5},{5,4},{6,7},{7,6},{8,9},{9,8},{10,11... | collective-permute-start | bytes 786440 | tf_op jit(solution)/shard_map/ppermute | solution.py:23
  13.0 5.7 %collective-permute-start.3 = (bf16[256,256]{1,0:T(8,128)(2,1)S(1)}, bf16[256,256]{1,0:T(8,128)(2,1)S(1)}, u32[]{:S(2)}, u32[]{:S(2)}) collective-permute-start(bf16[256,256]{1,0:T(8,128)(2,1)S(1)} %get-tuple-element.28.refs_1_), channel_id=1, source_target_pairs={{0,4},{1,5},{2,6},{3,7},{4,8},{5,9},{6,10},{7,11},{8,12},{9,13},{1... | collective-permute-start | bytes 393224 | tf_op jit(solution)/shard_map/ppermute | solution.py:23
  14.3 7.2 %collective-permute-start.4 = (bf16[256,256]{1,0:T(8,128)(2,1)S(1)}, bf16[256,256]{1,0:T(8,128)(2,1)S(1)}, u32[]{:S(2)}, u32[]{:S(2)}) collective-permute-start(bf16[256,256]{1,0:T(8,128)(2,1)S(1)} %get-tuple-element.29.refs_2_), channel_id=1, source_target_pairs={{0,4},{1,5},{2,6},{3,7},{4,8},{5,9},{6,10},{7,11},{8,12},{9,13},{1... | collective-permute-start | bytes 393224 | tf_op jit(solution)/shard_map/ppermute | solution.py:23
  18.7 5.8 %collective-permute-start.7 = (bf16[256,256]{1,0:T(8,128)(2,1)S(1)}, bf16[256,256]{1,0:T(8,128)(2,1)S(1)}, u32[]{:S(2)}, u32[]{:S(2)}) collective-permute-start(bf16[256,256]{1,0:T(8,128)(2,1)S(1)} %collective-permute-done.3.refs_0_), channel_id=1, source_target_pairs={{0,2},{1,3},{2,0},{3,1},{4,6},{5,7},{6,4},{7,5},{8,10},{9,11},{10,... | collective-permute-start | bytes 393224 | tf_op jit(solution)/shard_map/ppermute | solution.py:23
  21.5 5.5 %collective-permute-start.8 = (bf16[256,256]{1,0:T(8,128)(2,1)S(1)}, bf16[256,256]{1,0:T(8,128)(2,1)S(1)}, u32[]{:S(2)}, u32[]{:S(2)}) collective-permute-start(bf16[256,256]{1,0:T(8,128)(2,1)S(1)} %collective-permute-done.4.refs_1_), channel_id=1, source_target_pairs={{0,2},{1,3},{2,0},{3,1},{4,6},{5,7},{6,4},{7,5},{8,10},{9,11},{10,... | collective-permute-start | bytes 393224 | tf_op jit(solution)/shard_map/ppermute | solution.py:23
  22.8 5.7 %collective-permute-start.5 = (bf16[256,256]{1,0:T(8,128)(2,1)S(1)}, bf16[256,256]{1,0:T(8,128)(2,1)S(1)}, u32[]{:S(2)}, u32[]{:S(2)}) collective-permute-start(bf16[256,256]{1,0:T(8,128)(2,1)S(1)} %collective-permute-done.3.refs_0_), channel_id=1, source_target_pairs={{0,1},{1,0},{2,3},{3,2},{4,5},{5,4},{6,7},{7,6},{8,9},{9,8},{10,11... | collective-permute-start | bytes 393224 | tf_op jit(solution)/shard_map/ppermute | solution.py:23
  24.4 4.1 %collective-permute-start.6 = (bf16[256,256]{1,0:T(8,128)(2,1)S(1)}, bf16[256,256]{1,0:T(8,128)(2,1)S(1)}, u32[]{:S(2)}, u32[]{:S(2)}) collective-permute-start(bf16[256,256]{1,0:T(8,128)(2,1)S(1)} %collective-permute-done.4.refs_1_), channel_id=1, source_target_pairs={{0,1},{1,0},{2,3},{3,2},{4,5},{5,4},{6,7},{7,6},{8,9},{9,8},{10,11... | collective-permute-start | bytes 393224 | tf_op jit(solution)/shard_map/ppermute | solution.py:23
  27.0 2.5 %collective-permute-start.10 = (bf16[256,256]{1,0:T(8,128)(2,1)S(1)}, bf16[256,256]{1,0:T(8,128)(2,1)S(1)}, u32[]{:S(2)}, u32[]{:S(2)}) collective-permute-start(bf16[256,256]{1,0:T(8,128)(2,1)S(1)} %collective-permute-done.8.refs_5_), channel_id=1, source_target_pairs={{0,1},{1,0},{2,3},{3,2},{4,5},{5,4},{6,7},{7,6},{8,9},{9,8},{10,11... | collective-permute-start | bytes 393224 | tf_op jit(solution)/shard_map/ppermute | solution.py:23
  28.5 1.3 %collective-permute-start.9 = (bf16[256,256]{1,0:T(8,128)(2,1)S(1)}, bf16[256,256]{1,0:T(8,128)(2,1)S(1)}, u32[]{:S(2)}, u32[]{:S(2)}) collective-permute-start(bf16[256,256]{1,0:T(8,128)(2,1)S(1)} %collective-permute-done.7.refs_4_), channel_id=1, source_target_pairs={{0,1},{1,0},{2,3},{3,2},{4,5},{5,4},{6,7},{7,6},{8,9},{9,8},{10,11... | collective-permute-start | bytes 393224 | tf_op jit(solution)/shard_map/ppermute | solution.py:23
  32.1 5.9 %collective-permute-start.11 = (bf16[256,256]{1,0:T(8,128)(2,1)S(1)}, bf16[256,256]{1,0:T(8,128)(2,1)S(1)}, u32[]{:S(2)}, u32[]{:S(2)}) collective-permute-start(bf16[256,256]{1,0:T(8,128)(2,1)S(1)} %get-tuple-element.34.refs_1_), channel_id=1, source_target_pairs={{0,4},{1,5},{2,6},{3,7},{4,8},{5,9},{6,10},{7,11},{8,12},{9,13},{1... | collective-permute-start | bytes 393224 | tf_op jit(solution)/shard_map/ppermute | solution.py:23
  32.5 8.3 %collective-permute-start.12 = (bf16[256,256]{1,0:T(8,128)(2,1)S(1)}, bf16[256,256]{1,0:T(8,128)(2,1)S(1)}, u32[]{:S(2)}, u32[]{:S(2)}) collective-permute-start(bf16[256,256]{1,0:T(8,128)(2,1)S(1)} %get-tuple-element.35.refs_2_), channel_id=1, source_target_pairs={{0,4},{1,5},{2,6},{3,7},{4,8},{5,9},{6,10},{7,11},{8,12},{9,13},{1... | collective-permute-start | bytes 393224 | tf_op jit(solution)/shard_map/ppermute | solution.py:23
  38.0 5.6 %collective-permute-start.15 = (bf16[256,256]{1,0:T(8,128)(2,1)S(1)}, bf16[256,256]{1,0:T(8,128)(2,1)S(1)}, u32[]{:S(2)}, u32[]{:S(2)}) collective-permute-start(bf16[256,256]{1,0:T(8,128)(2,1)S(1)} %collective-permute-done.11.refs_0_), channel_id=1, source_target_pairs={{0,2},{1,3},{2,0},{3,1},{4,6},{5,7},{6,4},{7,5},{8,10},{9,11},{10,... | collective-permute-start | bytes 393224 | tf_op jit(solution)/shard_map/ppermute | solution.py:23
  40.8 5.3 %collective-permute-start.16 = (bf16[256,256]{1,0:T(8,128)(2,1)S(1)}, bf16[256,256]{1,0:T(8,128)(2,1)S(1)}, u32[]{:S(2)}, u32[]{:S(2)}) collective-permute-start(bf16[256,256]{1,0:T(8,128)(2,1)S(1)} %collective-permute-done.12.refs_1_), channel_id=1, source_target_pairs={{0,2},{1,3},{2,0},{3,1},{4,6},{5,7},{6,4},{7,5},{8,10},{9,11},{10,... | collective-permute-start | bytes 393224 | tf_op jit(solution)/shard_map/ppermute | solution.py:23
  42.2 5.2 %collective-permute-start.13 = (bf16[256,256]{1,0:T(8,128)(2,1)S(1)}, bf16[256,256]{1,0:T(8,128)(2,1)S(1)}, u32[]{:S(2)}, u32[]{:S(2)}) collective-permute-start(bf16[256,256]{1,0:T(8,128)(2,1)S(1)} %collective-permute-done.11.refs_0_), channel_id=1, source_target_pairs={{0,1},{1,0},{2,3},{3,2},{4,5},{5,4},{6,7},{7,6},{8,9},{9,8},{10,11... | collective-permute-start | bytes 393224 | tf_op jit(solution)/shard_map/ppermute | solution.py:23
  43.5 3.9 %collective-permute-start.14 = (bf16[256,256]{1,0:T(8,128)(2,1)S(1)}, bf16[256,256]{1,0:T(8,128)(2,1)S(1)}, u32[]{:S(2)}, u32[]{:S(2)}) collective-permute-start(bf16[256,256]{1,0:T(8,128)(2,1)S(1)} %collective-permute-done.12.refs_1_), channel_id=1, source_target_pairs={{0,1},{1,0},{2,3},{3,2},{4,5},{5,4},{6,7},{7,6},{8,9},{9,8},{10,11... | collective-permute-start | bytes 393224 | tf_op jit(solution)/shard_map/ppermute | solution.py:23
  43.6 3.8 %collective-permute-start.17 = (bf16[256,256]{1,0:T(8,128)(2,1)S(1)}, bf16[256,256]{1,0:T(8,128)(2,1)S(1)}, u32[]{:S(2)}, u32[]{:S(2)}) collective-permute-start(bf16[256,256]{1,0:T(8,128)(2,1)S(1)} %collective-permute-done.15.refs_4_), channel_id=1, source_target_pairs={{0,1},{1,0},{2,3},{3,2},{4,5},{5,4},{6,7},{7,6},{8,9},{9,8},{10,11... | collective-permute-start | bytes 393224 | tf_op jit(solution)/shard_map/ppermute | solution.py:23
  46.1 2.3 %collective-permute-start.18 = (bf16[256,256]{1,0:T(8,128)(2,1)S(1)}, bf16[256,256]{1,0:T(8,128)(2,1)S(1)}, u32[]{:S(2)}, u32[]{:S(2)}) collective-permute-start(bf16[256,256]{1,0:T(8,128)(2,1)S(1)} %collective-permute-done.16.refs_5_), channel_id=1, source_target_pairs={{0,1},{1,0},{2,3},{3,2},{4,5},{5,4},{6,7},{7,6},{8,9},{9,8},{10,11... | collective-permute-start | bytes 393224 | tf_op jit(solution)/shard_map/ppermute | solution.py:23

commit v7 on v6

--- a/solution.py
+++ b/solution.py
@@ -10,7 +10,8 @@
 AXES = ("slab", "sub")
 VMEM = pltpu.VMEM
 SCOPED = 16 << 20
-PARTS = 1
+PARTS = 2
+LAG = 8
 
 
 def permuted(x, slabs, subs, by, flip, ring=False):
@@ -94,7 +95,7 @@
     return dot(jnp.concatenate(lhs, axis=1), jnp.concatenate(rhs, axis=0))
 
 
-def finish(blocks, first, out_idx, sides, cols, val, sol, f_refs, write):
+def solve(inner, blocks, first, out_idx, sides, cols, val, sol, f_refs, write=None):
     rows_out, out_links = out_idx.shape
     size = blocks.shape[1]
     rows_in = val.shape[0] // size
@@ -102,7 +103,13 @@
     last_at = out_at + rows_out * out_links
     some, each = rows_in // PARTS, rows_out // len(f_refs)
     where = out_idx[...]
-    for i in range(rows_in):
+    lag = min(LAG, rows_in)
+    for ahead in range(rows_in + lag):
+        if ahead < rows_in:
+            val[pl.ds(ahead * size, size), :] = inner(ahead).astype(val.dtype)
+        i = ahead - lag
+        if i < 0:
+            continue
         at = pl.ds(i * size, size)
         sol[at, :] = dot(rows_of(blocks, first + i, size), val[at, :]).astype(sol.dtype)
         if write and (i + 1) % some == 0:
@@ -148,49 +155,38 @@
     swap = lax.axis_index("sub") * out_idx.shape[0]
     behind = lax.axis_index("slab") > 0
 
-    def couple():
+    def side(i):
+        return sides[pl.ds(i * size, size), cols]
+
+    def whole():
         for r, ref in enumerate(shares):
             inc[pl.ds(r * part, part), :] = ref[...]
         where = in_idx[...] ^ swap
-        for i in range(rows_in):
-            at = pl.ds(i * size, size)
+
+        def inner(i):
             places = [where[k, i] for k in range(links)]
             coupled = row_sum(blocks, 0, i, inc, places)
-            value = sides[at, cols].astype(jnp.float32) - coupled
-            val[at, :] = value.astype(val.dtype)
-
-    def rest(write=None):
-        finish(
-            blocks, rows_in * links, out_idx, sides, cols, val, sol, f_refs, write
-        )
-
-    if done:
-
-        def whole():
-            couple()
-            write, copies = writer((sol_hbm, fsol_hbm), cols, sems)
-            rest(write)
-            for c in copies:
-                c.wait()
-
-        if group == 0:
-            whole()
-        else:
-            pl.when(behind)(whole)
+            return side(i).astype(jnp.float32) - coupled
+
+        if not done:
+            rest(inner)
+            return
+        write, copies = writer((sol_hbm, fsol_hbm), cols, sems)
+        rest(inner, write)
+        for c in copies:
+            c.wait()
+
+    def rest(inner, write=None):
+        first = rows_in * links
+        solve(inner, blocks, first, out_idx, sides, cols, val, sol, f_refs, write)
+
+    if group == 0:
+        whole()
         return
-    if group == 0:
-        couple()
-    else:
-        pl.when(behind)(couple)
-
-        @pl.when(jnp.logical_not(behind))
-        def _():
-            val[...] = sides[pl.ds(0, rows_in * size), cols]
-
-    rest()
-
-
-def group_of(shares, in_idx, out_idx, blocks, sides, outs, token, group, groups):
+    pl.when(behind)(whole)
+
+
+def group_of(shares, in_idx, out_idx, blocks, sides, given, token, group, groups):
     width = shares[0].shape[1]
     links, rows_in = in_idx.shape
     rows_out, out_links = out_idx.shape
@@ -208,9 +204,16 @@
 
     operands = held([*shares, in_idx, out_idx, blocks, sides])
     in_specs = [vmem] * len(operands)
-    aliases = {len(operands) + n: n for n in range(len(outs))}
-    operands += [*outs] if token is None else [*outs, token]
-    in_specs += [hbm] * (len(operands) - len(in_specs))
+    aliases = {len(operands) + n: n for n in range(len(given))}
+    if done:
+        operands += [*given]
+        in_specs += [hbm] * len(given)
+    else:
+        operands += held(given)
+        in_specs += [vmem] * len(given)
+    if token is not None:
+        operands.append(token)
+        in_specs.append(hbm)
     own = [VMEM((rows, width), dtype)]
     own += [VMEM((front_rows // chunks, width), dtype)] * chunks
     out_shape, out_specs = own, [vmem] * len(own)
@@ -240,35 +243,37 @@
     )(*operands)
 
 
-def flush_kernel(count, column, ahead, *refs):
-    sources = refs[:count]
+def flush_kernel(count, column, groups, *refs):
+    sources, (out_idx, blocks, sides) = refs[:count], refs[count : count + 3]
     width = sources[0].shape[1]
-    if ahead:
-        out_idx, blocks, sides = refs[count : count + 3]
-        *outs, val, sol = refs[-5 - count : -1 - count]
-        *f_refs, more, sems = refs[-1 - count :]
+    last = column + 2 == groups
+    if last:
+        sol_hbm, fsol_hbm, sol, *f_refs, val, more, sems = refs[-5 - count :]
     else:
-        *outs, sems = refs[-3:]
+        sol_hbm, fsol_hbm, sol, *f_refs, val, sems = refs[-4 - count :]
+    outs = (sol_hbm, fsol_hbm)
     write, copies = writer(outs, pl.ds(column * width, width), sems)
     row = 0
     for n, ref in enumerate(sources):
         rows = ref.shape[0]
         write(ref, min(n, 1), row, rows)
         row += rows if n else 0
-    if ahead:
-
-        @pl.when(lax.axis_index("slab") == 0)
-        def _():
-            cols = pl.ds((column + 1) * width, width)
-            to, made = writer(outs, cols, more)
-            val[...] = sides[pl.ds(0, val.shape[0]), cols]
-            size = blocks.shape[1]
-            rows_out, links = out_idx.shape
-            later = val.shape[0] // size + rows_out * (links + 1)
-            first = blocks.shape[0] // size - later
-            finish(blocks, first, out_idx, sides, cols, val, sol, f_refs, to)
-            for c in made:
-                c.wait()
+
+    @pl.when(lax.axis_index("slab") == 0)
+    def _():
+        cols = pl.ds((column + 1) * width, width)
+        to, made = writer(outs, cols, more) if last else (None, [])
+        size = blocks.shape[1]
+        rows_out, links = out_idx.shape
+        later = val.shape[0] // size + rows_out * (links + 1)
+        first = blocks.shape[0] // size - later
+
+        def inner(i):
+            return sides[pl.ds(i * size, size), cols]
+
+        solve(inner, blocks, first, out_idx, sides, cols, val, sol, f_refs, to)
+        for c in made:
+            c.wait()
 
     for c in copies:
         c.wait()
@@ -280,17 +285,22 @@
     rows = (sources[0].shape[0], sum(f.shape[0] for f in sources[1:]))
     hbm = pl.BlockSpec(memory_space=pl.ANY)
     vmem = pl.BlockSpec(memory_space=VMEM)
-    ahead = column + 2 == groups
-    ins = [*sources, out_idx, blocks, sides] if ahead else [*sources]
+    ins = [*sources, out_idx, blocks, sides]
     held = [pltpu.with_memory_space_constraint(a, VMEM) for a in ins]
-    own = [VMEM(sources[0].shape, dtype), *[VMEM(a.shape, dtype) for a in sources]]
-    own.append(pltpu.SemaphoreType.DMA((PARTS + n - 1,)))
-    return pl.pallas_call(
-        functools.partial(flush_kernel, n, column, ahead),
-        out_shape=tuple(pltpu.HBM((r, wide), dtype) for r in rows),
+    own = [VMEM(a.shape, dtype) for a in sources]
+    out_shape = [pltpu.HBM((r, wide), dtype) for r in rows]
+    out_specs = [hbm, hbm]
+    scratch = [VMEM(sources[0].shape, dtype)]
+    if column + 2 == groups:
+        scratch = own + scratch + [pltpu.SemaphoreType.DMA((PARTS + n - 1,))]
+    else:
+        out_shape, out_specs = out_shape + own, out_specs + [vmem] * n
+    made = pl.pallas_call(
+        functools.partial(flush_kernel, n, column, groups),
+        out_shape=tuple(out_shape),
         in_specs=[vmem] * len(ins) + [hbm] * len(outs),
-        out_specs=(hbm, hbm),
-        scratch_shapes=own * ahead + [pltpu.SemaphoreType.DMA((n,))],
+        out_specs=tuple(out_specs),
+        scratch_shapes=scratch + [pltpu.SemaphoreType.DMA((n,))],
         input_output_aliases={len(ins) + k: k for k in range(len(outs))},
         compiler_params=pltpu.CompilerParams(vmem_limit_bytes=SCOPED),
         cost_estimate=pl.CostEstimate(
@@ -300,6 +310,7 @@
         ),
         name=f"flush_{column}",
     )(*held, *outs)
+    return made[:2], made[2:]
 
 
 def shards(
@@ -323,7 +334,7 @@
         [w.reshape(-1, size) for w in weights], [right_sides, front_sides]
     )
     arrived, token = gathered(pending_front, slabs, subs, token)
-    outs = ()
+    outs = early = ()
     for group in range(groups):
         made = group_of(
             arrived,
@@ -331,7 +342,7 @@
             out_idx,
             blocks,
             sides,
-            outs if group + 1 == groups else (),
+            outs if group + 1 == groups else early,
             token if group == 0 else None,
             group,
             groups,
@@ -339,7 +350,7 @@
         if group + 1 < groups:
             ring = True
             hops = [permuted(f, slabs, subs, 1, 0, ring) for f in made[1:]]
-            outs = flushed(made, out_idx, blocks, sides, outs, group, groups)
+            outs, early = flushed(made, out_idx, blocks, sides, outs, group, groups)
             chunks = []
             for n, hop in enumerate(hops):
                 chunk, ahead = gathered(hop, slabs, subs, None if n else outs)

time: 51.9 us -> 51.3 us (0.988)
  no operation moved by 1% of the time
where the time goes in v7:
time: 51.3 us; the launch traced here: 51.1 us
  waiting for transfers between devices  21 us (41%)
  starting transfers between devices  16.3 us (32%)
  Pallas kernels  13 us (25%)
  between operations  0.7 us (1%)
    ppermute x19, waiting for transfers between devices, permuted(): return lax.ppermute(x, AXES, pairs)  21 us
    ppermute x19, starting transfers between devices, permuted(): return lax.ppermute(x, AXES, pairs)  16.3 us
    pallas_call x3, Pallas kernels, group_of(): pl.pallas_call(functools.partial(group_kernel, pieces, group, groups, chu...  7.29 us
    pallas_call x1, Pallas kernels, staged(): pl.pallas_call(functools.partial(stage_kernel, counts), out_shape=(*(VMEM...  3.58 us
    pallas_call x2, Pallas kernels, flushed(): pl.pallas_call(functools.partial(flush_kernel, n, column, groups), out_sh...  2.17 us
  transfers between devices with their start and end apart: 19, of which 11 were waited for; matrix products, arithmetic and copies ran while one was open for 0% of the time, Pallas kernels for 11%

profile of v7, /device:TPU:11, one launch (start us, length us, event | category | flops | bytes accessed | tf_op | source)
XLA Modules:
  0.0 51.1 jit_solution(10362424118867097796)
XLA Ops:
  0.6 0.3 collective-permute-start.1
  1.0 1.0 %collective-permute-start = (bf16[512,256]{1,0:T(8,128)(2,1)}, bf16[512,256]{1,0:T(8,128)(2,1)S(1)}, u32[]{:S(2)}, u32[]{:S(2)}) collective-permute-start(bf16[512,256]{1,0:T(8,128)(2,1)} %refs_0_.1), channel_id=1, source_target_pairs={{0,1},{1,0},{2,3},{3,2},{4,5},{5,4},{6,7},{7,6},{8,9},{9,8},{10,11... | collective-permute-start | bytes 786440 | tf_op jit(solution)/shard_map/ppermute | solution.py:24
  1.9 0.0 copy-start
  1.9 3.6 %stage.1 = (bf16[18944,128]{1,0:T(8,128)(2,1)S(1)}, bf16[2560,768]{1,0:T(8,128)(2,1)S(1)}, f32[8,128]{1,0:T(8,128)S(1)}) custom-call(bf16[12288,128]{1,0:T(8,128)(2,1)} %bitcast.8, bf16[2048,128]{1,0:T(8,128)(2,1)} %bitcast.10, bf16[4096,128]{1,0:T(8,128)(2,1)} %bitcast.9, bf16[512,128]{1,0:T(8,128)(2,1)} %bitcast.11, bf16[2048,768]{1,0:T(8,128)(2,1)} %refs_4_.1, ...), custom_call_target="tpu_custom_call" | custom-call | bytes 17563648 | tf_op jit(solution)/shard_map/stage/pallas_call | solution.py:66
  5.5 2.6 %collective-permute-done.1.refs_2_ = bf16[512,256]{1,0:T(8,128)(2,1)S(1)} collective-permute-done((bf16[512,256]{1,0:T(8,128)(2,1)}, bf16[512,256]{1,0:T(8,128)(2,1)S(1)}, u32[]{:S(2)}, u32[]{:S(2)}) %collective-permute-start.1) | collective-permute-done | bytes 262176 | tf_op jit(solution)/shard_map/ppermute | solution.py:24
  8.1 1.5 %collective-permute-start.2 = (bf16[512,256]{1,0:T(8,128)(2,1)S(1)}, bf16[512,256]{1,0:T(8,128)(2,1)S(1)}, u32[]{:S(2)}, u32[]{:S(2)}) collective-permute-start(bf16[512,256]{1,0:T(8,128)(2,1)S(1)} %collective-permute-done.1.refs_2_), channel_id=1, source_target_pairs={{0,1},{1,0},{2,3},{3,2},{4,5},{5,4},{6,7},{7,6},{8,9},{9,8},{10,11... | collective-permute-start | bytes 786440 | tf_op jit(solution)/shard_map/ppermute | solution.py:24
  9.6 0.0 collective-permute-done.refs_1_
  9.6 1.2 %collective-permute-done.2.refs_3_ = bf16[512,256]{1,0:T(8,128)(2,1)S(1)} collective-permute-done((bf16[512,256]{1,0:T(8,128)(2,1)S(1)}, bf16[512,256]{1,0:T(8,128)(2,1)S(1)}, u32[]{:S(2)}, u32[]{:S(2)}) %collective-permute-start.2) | collective-permute-done | bytes 262176 | tf_op jit(solution)/shard_map/ppermute | solution.py:24
  10.8 0.0 copy-done
  10.8 0.0 copy-done.1
  10.8 0.0 copy-done.2
  10.8 2.2 %group_0.1 = (bf16[2048,256]{1,0:T(8,128)(2,1)S(1)}, bf16[256,256]{1,0:T(8,128)(2,1)S(1)}, bf16[256,256]{1,0:T(8,128)(2,1)S(1)}) custom-call(bf16[512,256]{1,0:T(8,128)(2,1)S(1)} %copy-done, bf16[512,256]{1,0:T(8,128)(2,1)S(1)} %collective-permute-done.refs_1_, bf16[512,256]{1,0:T(8,128)(2,1)S(1)} %collective-permute-done.1.refs_2_, ...), custom_call_target="tpu_custom_call" | custom-call | flops 1241513984 | bytes 6946816 | tf_op jit(solution)/shard_map/group_0/pallas_call | solution.py:229
  13.0 1.3 %collective-permute-start.3 = (bf16[256,256]{1,0:T(8,128)(2,1)S(1)}, bf16[256,256]{1,0:T(8,128)(2,1)S(1)}, u32[]{:S(2)}, u32[]{:S(2)}) collective-permute-start(bf16[256,256]{1,0:T(8,128)(2,1)S(1)} %get-tuple-element.31.refs_1_), channel_id=1, source_target_pairs={{0,4},{1,5},{2,6},{3,7},{4,8},{5,9},{6,10},{7,11},{8,12},{9,13},{1... | collective-permute-start | bytes 393224 | tf_op jit(solution)/shard_map/ppermute | solution.py:24
  14.3 1.2 %collective-permute-start.4 = (bf16[256,256]{1,0:T(8,128)(2,1)S(1)}, bf16[256,256]{1,0:T(8,128)(2,1)S(1)}, u32[]{:S(2)}, u32[]{:S(2)}) collective-permute-start(bf16[256,256]{1,0:T(8,128)(2,1)S(1)} %get-tuple-element.32.refs_2_), channel_id=1, source_target_pairs={{0,4},{1,5},{2,6},{3,7},{4,8},{5,9},{6,10},{7,11},{8,12},{9,13},{1... | collective-permute-start | bytes 393224 | tf_op jit(solution)/shard_map/ppermute | solution.py:24
  15.5 3.1 %collective-permute-done.3.refs_0_ = bf16[256,256]{1,0:T(8,128)(2,1)S(1)} collective-permute-done((bf16[256,256]{1,0:T(8,128)(2,1)S(1)}, bf16[256,256]{1,0:T(8,128)(2,1)S(1)}, u32[]{:S(2)}, u32[]{:S(2)}) %collective-permute-start.3) | collective-permute-done | bytes 131104 | tf_op jit(solution)/shard_map/ppermute | solution.py:24
  18.6 0.3 collective-permute-start.7
  18.9 2.5 %collective-permute-done.4.refs_1_ = bf16[256,256]{1,0:T(8,128)(2,1)S(1)} collective-permute-done((bf16[256,256]{1,0:T(8,128)(2,1)S(1)}, bf16[256,256]{1,0:T(8,128)(2,1)S(1)}, u32[]{:S(2)}, u32[]{:S(2)}) %collective-permute-start.4) | collective-permute-done | bytes 131104 | tf_op jit(solution)/shard_map/ppermute | solution.py:24
  21.5 0.3 collective-permute-start.8
  21.7 1.1 %flush_0.1 = (bf16[2048,768]{1,0:T(8,128)(2,1)}, bf16[512,768]{1,0:T(8,128)(2,1)}, bf16[2048,256]{1,0:T(8,128)(2,1)S(1)}, bf16[256,256]{1,0:T(8,128)(2,1)S(1)}, bf16[256,256]{1,0:T(8,128)(2,1)S(1)}) custom-call(bf16[2048,256]{1,0:T(8,128)(2,1)S(1)} %get-tuple-element.33.refs_0_, bf16[256,256]{1,0:T(8,128)(2,1)S(1)} %get-tuple-element.31.refs_1_, ...), custom_call_target="tpu_custom_call" | custom-call | bytes 2621440 | tf_op jit(solution)/shard_map/flush_0/pallas_call | solution.py:298
  22.8 1.6 %collective-permute-start.5 = (bf16[256,256]{1,0:T(8,128)(2,1)S(1)}, bf16[256,256]{1,0:T(8,128)(2,1)S(1)}, u32[]{:S(2)}, u32[]{:S(2)}) collective-permute-start(bf16[256,256]{1,0:T(8,128)(2,1)S(1)} %collective-permute-done.3.refs_0_), channel_id=1, source_target_pairs={{0,1},{1,0},{2,3},{3,2},{4,5},{5,4},{6,7},{7,6},{8,9},{9,8},{10,11... | collective-permute-start | bytes 393224 | tf_op jit(solution)/shard_map/ppermute | solution.py:24
  24.3 0.1 collective-permute-start.6
  24.4 0.0 collective-permute-done.7.refs_4_
  24.4 2.5 %collective-permute-done.8.refs_5_ = bf16[256,256]{1,0:T(8,128)(2,1)S(1)} collective-permute-done((bf16[256,256]{1,0:T(8,128)(2,1)S(1)}, bf16[256,256]{1,0:T(8,128)(2,1)S(1)}, u32[]{:S(2)}, u32[]{:S(2)}) %collective-permute-start.8) | collective-permute-done | bytes 131104 | tf_op jit(solution)/shard_map/ppermute | solution.py:24
  27.0 1.5 %collective-permute-start.10 = (bf16[256,256]{1,0:T(8,128)(2,1)S(1)}, bf16[256,256]{1,0:T(8,128)(2,1)S(1)}, u32[]{:S(2)}, u32[]{:S(2)}) collective-permute-start(bf16[256,256]{1,0:T(8,128)(2,1)S(1)} %collective-permute-done.8.refs_5_), channel_id=1, source_target_pairs={{0,1},{1,0},{2,3},{3,2},{4,5},{5,4},{6,7},{7,6},{8,9},{9,8},{10,11... | collective-permute-start | bytes 393224 | tf_op jit(solution)/shard_map/ppermute | solution.py:24
  28.4 0.0 collective-permute-start.9
  28.4 0.0 collective-permute-done.5.refs_2_
  28.5 0.0 collective-permute-done.6.refs_3_
  28.5 1.0 %collective-permute-done.10.refs_7_ = bf16[256,256]{1,0:T(8,128)(2,1)S(1)} collective-permute-done((bf16[256,256]{1,0:T(8,128)(2,1)S(1)}, bf16[256,256]{1,0:T(8,128)(2,1)S(1)}, u32[]{:S(2)}, u32[]{:S(2)}) %collective-permute-start.10) | collective-permute-done | bytes 131104 | tf_op jit(solution)/shard_map/ppermute | solution.py:24
  29.4 0.4 collective-permute-done.9.refs_6_
  29.8 2.2 %group_1.1 = (bf16[2048,256]{1,0:T(8,128)(2,1)S(1)}, bf16[256,256]{1,0:T(8,128)(2,1)S(1)}, bf16[256,256]{1,0:T(8,128)(2,1)S(1)}) custom-call(bf16[256,256]{1,0:T(8,128)(2,1)S(1)} %collective-permute-done.3.refs_0_, bf16[256,256]{1,0:T(8,128)(2,1)S(1)} %collective-permute-done.4.refs_1_, ...), custom_call_target="tpu_custom_call", output_to_operand_aliasing={{0}: (12, {}), {1}: (13, {}), {2}: (14, {})} | custom-call | flops 1241513984 | bytes 6946816 | tf_op jit(solution)/shard_map/group_1/pallas_call | solution.py:229
  32.0 0.4 collective-permute-start.11
  32.4 2.1 %collective-permute-start.12 = (bf16[256,256]{1,0:T(8,128)(2,1)S(1)}, bf16[256,256]{1,0:T(8,128)(2,1)S(1)}, u32[]{:S(2)}, u32[]{:S(2)}) collective-permute-start(bf16[256,256]{1,0:T(8,128)(2,1)S(1)} %get-tuple-element.41.refs_2_), channel_id=1, source_target_pairs={{0,4},{1,5},{2,6},{3,7},{4,8},{5,9},{6,10},{7,11},{8,12},{9,13},{1... | collective-permute-start | bytes 393224 | tf_op jit(solution)/shard_map/ppermute | solution.py:24
  34.5 3.3 %collective-permute-done.11.refs_0_ = bf16[256,256]{1,0:T(8,128)(2,1)S(1)} collective-permute-done((bf16[256,256]{1,0:T(8,128)(2,1)S(1)}, bf16[256,256]{1,0:T(8,128)(2,1)S(1)}, u32[]{:S(2)}, u32[]{:S(2)}) %collective-permute-start.11) | collective-permute-done | bytes 131104 | tf_op jit(solution)/shard_map/ppermute | solution.py:24
  37.9 0.2 collective-permute-start.15
  38.1 2.6 %collective-permute-done.12.refs_1_ = bf16[256,256]{1,0:T(8,128)(2,1)S(1)} collective-permute-done((bf16[256,256]{1,0:T(8,128)(2,1)S(1)}, bf16[256,256]{1,0:T(8,128)(2,1)S(1)}, u32[]{:S(2)}, u32[]{:S(2)}) %collective-permute-start.12) | collective-permute-done | bytes 131104 | tf_op jit(solution)/shard_map/ppermute | solution.py:24
  40.7 0.2 collective-permute-start.16
  40.9 1.1 %flush_1.1 = (bf16[2048,768]{1,0:T(8,128)(2,1)}, bf16[512,768]{1,0:T(8,128)(2,1)}) custom-call(bf16[2048,256]{1,0:T(8,128)(2,1)S(1)} %get-tuple-element.42.refs_0_, bf16[256,256]{1,0:T(8,128)(2,1)S(1)} %get-tuple-element.40.refs_1_, bf16[256,256]{1,0:T(8,128)(2,1)S(1)} %get-tuple-element.41.refs_2_, ...), custom_call_target="tpu_custom_call", output_to_operand_aliasing={{0}: (6, {}), {1}: (7, {})} | custom-call | bytes 2621440 | tf_op jit(solution)/shard_map/flush_1/pallas_call | solution.py:298
  42.0 1.3 %collective-permute-start.13 = (bf16[256,256]{1,0:T(8,128)(2,1)S(1)}, bf16[256,256]{1,0:T(8,128)(2,1)S(1)}, u32[]{:S(2)}, u32[]{:S(2)}) collective-permute-start(bf16[256,256]{1,0:T(8,128)(2,1)S(1)} %collective-permute-done.11.refs_0_), channel_id=1, source_target_pairs={{0,1},{1,0},{2,3},{3,2},{4,5},{5,4},{6,7},{7,6},{8,9},{9,8},{10,11... | collective-permute-start | bytes 393224 | tf_op jit(solution)/shard_map/ppermute | solution.py:24
  43.4 0.1 collective-permute-start.14
  43.5 0.0 collective-permute-done.15.refs_4_
  43.5 1.6 %collective-permute-start.17 = (bf16[256,256]{1,0:T(8,128)(2,1)S(1)}, bf16[256,256]{1,0:T(8,128)(2,1)S(1)}, u32[]{:S(2)}, u32[]{:S(2)}) collective-permute-start(bf16[256,256]{1,0:T(8,128)(2,1)S(1)} %collective-permute-done.15.refs_4_), channel_id=1, source_target_pairs={{0,1},{1,0},{2,3},{3,2},{4,5},{5,4},{6,7},{7,6},{8,9},{9,8},{10,11... | collective-permute-start | bytes 393224 | tf_op jit(solution)/shard_map/ppermute | solution.py:24
  45.1 0.9 %collective-permute-done.16.refs_5_ = bf16[256,256]{1,0:T(8,128)(2,1)S(1)} collective-permute-done((bf16[256,256]{1,0:T(8,128)(2,1)S(1)}, bf16[256,256]{1,0:T(8,128)(2,1)S(1)}, u32[]{:S(2)}, u32[]{:S(2)}) %collective-permute-start.16) | collective-permute-done | bytes 131104 | tf_op jit(solution)/shard_map/ppermute | solution.py:24
  46.0 1.3 %collective-permute-start.18 = (bf16[256,256]{1,0:T(8,128)(2,1)S(1)}, bf16[256,256]{1,0:T(8,128)(2,1)S(1)}, u32[]{:S(2)}, u32[]{:S(2)}) collective-permute-start(bf16[256,256]{1,0:T(8,128)(2,1)S(1)} %collective-permute-done.16.refs_5_), channel_id=1, source_target_pairs={{0,1},{1,0},{2,3},{3,2},{4,5},{5,4},{6,7},{7,6},{8,9},{9,8},{10,11... | collective-permute-start | bytes 393224 | tf_op jit(solution)/shard_map/ppermute | solution.py:24
  47.2 0.0 collective-permute-done.13.refs_2_
  47.2 0.0 collective-permute-done.14.refs_3_
  47.2 0.0 collective-permute-done.17.refs_6_
  47.3 1.0 %collective-permute-done.18.refs_7_ = bf16[256,256]{1,0:T(8,128)(2,1)S(1)} collective-permute-done((bf16[256,256]{1,0:T(8,128)(2,1)S(1)}, bf16[256,256]{1,0:T(8,128)(2,1)S(1)}, u32[]{:S(2)}, u32[]{:S(2)}) %collective-permute-start.18) | collective-permute-done | bytes 131104 | tf_op jit(solution)/shard_map/ppermute | solution.py:24
  48.2 2.9 %group_2.1 = (bf16[2048,768]{1,0:T(8,128)(2,1)}, bf16[512,768]{1,0:T(8,128)(2,1)}) custom-call(bf16[256,256]{1,0:T(8,128)(2,1)S(1)} %collective-permute-done.11.refs_0_, bf16[256,256]{1,0:T(8,128)(2,1)S(1)} %collective-permute-done.12.refs_1_, bf16[256,256]{1,0:T(8,128)(2,1)S(1)} %collective-permute-done.13.refs_2_, ...), custom_call_target="tpu_custom_call", output_to_operand_aliasing={{0}: (12, {}), {1}: (13, {})} | custom-call | flops 1241513984 | bytes 6946816 | tf_op jit(solution)/shard_map/group_2/pallas_call | solution.py:229
  (2 shorter events, 0.0 us)
Async XLA Ops:
  0.6 7.5 %collective-permute-start.1 = (bf16[512,256]{1,0:T(8,128)(2,1)}, bf16[512,256]{1,0:T(8,128)(2,1)S(1)}, u32[]{:S(2)}, u32[]{:S(2)}) collective-permute-start(bf16[512,256]{1,0:T(8,128)(2,1)} %refs_0_.1), channel_id=1, source_target_pairs={{0,2},{1,3},{2,0},{3,1},{4,6},{5,7},{6,4},{7,5},{8,10},{9,11},{10,... | collective-permute-start | bytes 786440 | tf_op jit(solution)/shard_map/ppermute | solution.py:24
  1.0 8.7 %collective-permute-start = (bf16[512,256]{1,0:T(8,128)(2,1)}, bf16[512,256]{1,0:T(8,128)(2,1)S(1)}, u32[]{:S(2)}, u32[]{:S(2)}) collective-permute-start(bf16[512,256]{1,0:T(8,128)(2,1)} %refs_0_.1), channel_id=1, source_target_pairs={{0,1},{1,0},{2,3},{3,2},{4,5},{5,4},{6,7},{7,6},{8,9},{9,8},{10,11... | collective-permute-start | bytes 786440 | tf_op jit(solution)/shard_map/ppermute | solution.py:24
  1.9 8.9 %copy-start = (bf16[512,256]{1,0:T(8,128)(2,1)S(1)}, bf16[512,256]{1,0:T(8,128)(2,1)}, u32[]{:S(2)}) copy-start(bf16[512,256]{1,0:T(8,128)(2,1)} %refs_0_.1) | copy-start | bytes 786436
  1.9 8.9 %copy-start.1 = (s32[4,8]{1,0:T(4,128)S(1)}, s32[4,8]{1,0:T(4,128)}, u32[]{:S(2)}) copy-start(s32[4,8]{1,0:T(4,128)} %refs_9_.3) | copy-start | bytes 388
  1.9 8.9 %copy-start.2 = (s32[16,6]{0,1:T(8,128)S(1)}, s32[16,6]{0,1:T(8,128)}, u32[]{:S(2)}) copy-start(s32[16,6]{0,1:T(8,128)} %param.12) | copy-start | bytes 1156
  8.1 2.7 %collective-permute-start.2 = (bf16[512,256]{1,0:T(8,128)(2,1)S(1)}, bf16[512,256]{1,0:T(8,128)(2,1)S(1)}, u32[]{:S(2)}, u32[]{:S(2)}) collective-permute-start(bf16[512,256]{1,0:T(8,128)(2,1)S(1)} %collective-permute-done.1.refs_2_), channel_id=1, source_target_pairs={{0,1},{1,0},{2,3},{3,2},{4,5},{5,4},{6,7},{7,6},{8,9},{9,8},{10,11... | collective-permute-start | bytes 786440 | tf_op jit(solution)/shard_map/ppermute | solution.py:24
  13.0 5.7 %collective-permute-start.3 = (bf16[256,256]{1,0:T(8,128)(2,1)S(1)}, bf16[256,256]{1,0:T(8,128)(2,1)S(1)}, u32[]{:S(2)}, u32[]{:S(2)}) collective-permute-start(bf16[256,256]{1,0:T(8,128)(2,1)S(1)} %get-tuple-element.31.refs_1_), channel_id=1, source_target_pairs={{0,4},{1,5},{2,6},{3,7},{4,8},{5,9},{6,10},{7,11},{8,12},{9,13},{1... | collective-permute-start | bytes 393224 | tf_op jit(solution)/shard_map/ppermute | solution.py:24
  14.3 7.2 %collective-permute-start.4 = (bf16[256,256]{1,0:T(8,128)(2,1)S(1)}, bf16[256,256]{1,0:T(8,128)(2,1)S(1)}, u32[]{:S(2)}, u32[]{:S(2)}) collective-permute-start(bf16[256,256]{1,0:T(8,128)(2,1)S(1)} %get-tuple-element.32.refs_2_), channel_id=1, source_target_pairs={{0,4},{1,5},{2,6},{3,7},{4,8},{5,9},{6,10},{7,11},{8,12},{9,13},{1... | collective-permute-start | bytes 393224 | tf_op jit(solution)/shard_map/ppermute | solution.py:24
  18.6 5.8 %collective-permute-start.7 = (bf16[256,256]{1,0:T(8,128)(2,1)S(1)}, bf16[256,256]{1,0:T(8,128)(2,1)S(1)}, u32[]{:S(2)}, u32[]{:S(2)}) collective-permute-start(bf16[256,256]{1,0:T(8,128)(2,1)S(1)} %collective-permute-done.3.refs_0_), channel_id=1, source_target_pairs={{0,2},{1,3},{2,0},{3,1},{4,6},{5,7},{6,4},{7,5},{8,10},{9,11},{10,... | collective-permute-start | bytes 393224 | tf_op jit(solution)/shard_map/ppermute | solution.py:24
  21.5 5.5 %collective-permute-start.8 = (bf16[256,256]{1,0:T(8,128)(2,1)S(1)}, bf16[256,256]{1,0:T(8,128)(2,1)S(1)}, u32[]{:S(2)}, u32[]{:S(2)}) collective-permute-start(bf16[256,256]{1,0:T(8,128)(2,1)S(1)} %collective-permute-done.4.refs_1_), channel_id=1, source_target_pairs={{0,2},{1,3},{2,0},{3,1},{4,6},{5,7},{6,4},{7,5},{8,10},{9,11},{10,... | collective-permute-start | bytes 393224 | tf_op jit(solution)/shard_map/ppermute | solution.py:24
  22.8 5.7 %collective-permute-start.5 = (bf16[256,256]{1,0:T(8,128)(2,1)S(1)}, bf16[256,256]{1,0:T(8,128)(2,1)S(1)}, u32[]{:S(2)}, u32[]{:S(2)}) collective-permute-start(bf16[256,256]{1,0:T(8,128)(2,1)S(1)} %collective-permute-done.3.refs_0_), channel_id=1, source_target_pairs={{0,1},{1,0},{2,3},{3,2},{4,5},{5,4},{6,7},{7,6},{8,9},{9,8},{10,11... | collective-permute-start | bytes 393224 | tf_op jit(solution)/shard_map/ppermute | solution.py:24
  24.3 4.1 %collective-permute-start.6 = (bf16[256,256]{1,0:T(8,128)(2,1)S(1)}, bf16[256,256]{1,0:T(8,128)(2,1)S(1)}, u32[]{:S(2)}, u32[]{:S(2)}) collective-permute-start(bf16[256,256]{1,0:T(8,128)(2,1)S(1)} %collective-permute-done.4.refs_1_), channel_id=1, source_target_pairs={{0,1},{1,0},{2,3},{3,2},{4,5},{5,4},{6,7},{7,6},{8,9},{9,8},{10,11... | collective-permute-start | bytes 393224 | tf_op jit(solution)/shard_map/ppermute | solution.py:24
  27.0 2.5 %collective-permute-start.10 = (bf16[256,256]{1,0:T(8,128)(2,1)S(1)}, bf16[256,256]{1,0:T(8,128)(2,1)S(1)}, u32[]{:S(2)}, u32[]{:S(2)}) collective-permute-start(bf16[256,256]{1,0:T(8,128)(2,1)S(1)} %collective-permute-done.8.refs_5_), channel_id=1, source_target_pairs={{0,1},{1,0},{2,3},{3,2},{4,5},{5,4},{6,7},{7,6},{8,9},{9,8},{10,11... | collective-permute-start | bytes 393224 | tf_op jit(solution)/shard_map/ppermute | solution.py:24
  28.4 1.3 %collective-permute-start.9 = (bf16[256,256]{1,0:T(8,128)(2,1)S(1)}, bf16[256,256]{1,0:T(8,128)(2,1)S(1)}, u32[]{:S(2)}, u32[]{:S(2)}) collective-permute-start(bf16[256,256]{1,0:T(8,128)(2,1)S(1)} %collective-permute-done.7.refs_4_), channel_id=1, source_target_pairs={{0,1},{1,0},{2,3},{3,2},{4,5},{5,4},{6,7},{7,6},{8,9},{9,8},{10,11... | collective-permute-start | bytes 393224 | tf_op jit(solution)/shard_map/ppermute | solution.py:24
  32.0 5.9 %collective-permute-start.11 = (bf16[256,256]{1,0:T(8,128)(2,1)S(1)}, bf16[256,256]{1,0:T(8,128)(2,1)S(1)}, u32[]{:S(2)}, u32[]{:S(2)}) collective-permute-start(bf16[256,256]{1,0:T(8,128)(2,1)S(1)} %get-tuple-element.40.refs_1_), channel_id=1, source_target_pairs={{0,4},{1,5},{2,6},{3,7},{4,8},{5,9},{6,10},{7,11},{8,12},{9,13},{1... | collective-permute-start | bytes 393224 | tf_op jit(solution)/shard_map/ppermute | solution.py:24
  32.4 8.3 %collective-permute-start.12 = (bf16[256,256]{1,0:T(8,128)(2,1)S(1)}, bf16[256,256]{1,0:T(8,128)(2,1)S(1)}, u32[]{:S(2)}, u32[]{:S(2)}) collective-permute-start(bf16[256,256]{1,0:T(8,128)(2,1)S(1)} %get-tuple-element.41.refs_2_), channel_id=1, source_target_pairs={{0,4},{1,5},{2,6},{3,7},{4,8},{5,9},{6,10},{7,11},{8,12},{9,13},{1... | collective-permute-start | bytes 393224 | tf_op jit(solution)/shard_map/ppermute | solution.py:24
  37.9 5.6 %collective-permute-start.15 = (bf16[256,256]{1,0:T(8,128)(2,1)S(1)}, bf16[256,256]{1,0:T(8,128)(2,1)S(1)}, u32[]{:S(2)}, u32[]{:S(2)}) collective-permute-start(bf16[256,256]{1,0:T(8,128)(2,1)S(1)} %collective-permute-done.11.refs_0_), channel_id=1, source_target_pairs={{0,2},{1,3},{2,0},{3,1},{4,6},{5,7},{6,4},{7,5},{8,10},{9,11},{10,... | collective-permute-start | bytes 393224 | tf_op jit(solution)/shard_map/ppermute | solution.py:24
  40.7 5.3 %collective-permute-start.16 = (bf16[256,256]{1,0:T(8,128)(2,1)S(1)}, bf16[256,256]{1,0:T(8,128)(2,1)S(1)}, u32[]{:S(2)}, u32[]{:S(2)}) collective-permute-start(bf16[256,256]{1,0:T(8,128)(2,1)S(1)} %collective-permute-done.12.refs_1_), channel_id=1, source_target_pairs={{0,2},{1,3},{2,0},{3,1},{4,6},{5,7},{6,4},{7,5},{8,10},{9,11},{10,... | collective-permute-start | bytes 393224 | tf_op jit(solution)/shard_map/ppermute | solution.py:24
  42.0 5.2 %collective-permute-start.13 = (bf16[256,256]{1,0:T(8,128)(2,1)S(1)}, bf16[256,256]{1,0:T(8,128)(2,1)S(1)}, u32[]{:S(2)}, u32[]{:S(2)}) collective-permute-start(bf16[256,256]{1,0:T(8,128)(2,1)S(1)} %collective-permute-done.11.refs_0_), channel_id=1, source_target_pairs={{0,1},{1,0},{2,3},{3,2},{4,5},{5,4},{6,7},{7,6},{8,9},{9,8},{10,11... | collective-permute-start | bytes 393224 | tf_op jit(solution)/shard_map/ppermute | solution.py:24
  43.4 3.9 %collective-permute-start.14 = (bf16[256,256]{1,0:T(8,128)(2,1)S(1)}, bf16[256,256]{1,0:T(8,128)(2,1)S(1)}, u32[]{:S(2)}, u32[]{:S(2)}) collective-permute-start(bf16[256,256]{1,0:T(8,128)(2,1)S(1)} %collective-permute-done.12.refs_1_), channel_id=1, source_target_pairs={{0,1},{1,0},{2,3},{3,2},{4,5},{5,4},{6,7},{7,6},{8,9},{9,8},{10,11... | collective-permute-start | bytes 393224 | tf_op jit(solution)/shard_map/ppermute | solution.py:24
  43.5 3.8 %collective-permute-start.17 = (bf16[256,256]{1,0:T(8,128)(2,1)S(1)}, bf16[256,256]{1,0:T(8,128)(2,1)S(1)}, u32[]{:S(2)}, u32[]{:S(2)}) collective-permute-start(bf16[256,256]{1,0:T(8,128)(2,1)S(1)} %collective-permute-done.15.refs_4_), channel_id=1, source_target_pairs={{0,1},{1,0},{2,3},{3,2},{4,5},{5,4},{6,7},{7,6},{8,9},{9,8},{10,11... | collective-permute-start | bytes 393224 | tf_op jit(solution)/shard_map/ppermute | solution.py:24
  46.0 2.3 %collective-permute-start.18 = (bf16[256,256]{1,0:T(8,128)(2,1)S(1)}, bf16[256,256]{1,0:T(8,128)(2,1)S(1)}, u32[]{:S(2)}, u32[]{:S(2)}) collective-permute-start(bf16[256,256]{1,0:T(8,128)(2,1)S(1)} %collective-permute-done.16.refs_5_), channel_id=1, source_target_pairs={{0,1},{1,0},{2,3},{3,2},{4,5},{5,4},{6,7},{7,6},{8,9},{9,8},{10,11... | collective-permute-start | bytes 393224 | tf_op jit(solution)/shard_map/ppermute | solution.py:24

commit v8 on v7

--- a/solution.py
+++ b/solution.py
@@ -353,8 +353,7 @@
             outs, early = flushed(made, out_idx, blocks, sides, outs, group, groups)
             chunks = []
             for n, hop in enumerate(hops):
-                chunk, ahead = gathered(hop, slabs, subs, None if n else outs)
-                outs = outs if n else ahead
+                chunk, _ = gathered(hop, slabs, subs)
                 chunks.append(chunk)
             arrived = [c[r] for r in range(subs) for c in chunks]
     return tuple(made[:2])

time: 51.3 us -> 51.3 us (level)
  waiting for transfers between devices: 21 us -> 16.4 us
  starting transfers between devices: 16.3 us -> 20.9 us
    ppermute x19, waiting for transfers between devices: 21 us -> 16.4 us  [permuted(): return lax.ppermute(x, AXES, pairs)]
    ppermute x19, starting transfers between devices: 16.3 us -> 20.9 us  [permuted(): return lax.ppermute(x, AXES, pairs)]
  transfers between devices with their start and end apart: 19 -> 19, of which waited for: 11 -> 8; matrix products, arithmetic and copies ran while one was open for 0% -> 0% of each run, Pallas kernels for 11% -> 11%
where the time goes in v8:
time: 51.3 us; the launch traced here: 51.1 us
  starting transfers between devices  20.9 us (41%)
  waiting for transfers between devices  16.4 us (32%)
  Pallas kernels  13.1 us (26%)
  between operations  0.75 us (1%)
    ppermute x19, starting transfers between devices, permuted(): return lax.ppermute(x, AXES, pairs)  20.9 us
    ppermute x19, waiting for transfers between devices, permuted(): return lax.ppermute(x, AXES, pairs)  16.4 us
    pallas_call x3, Pallas kernels, group_of(): pl.pallas_call(functools.partial(group_kernel, pieces, group, groups, chu...  7.33 us
    pallas_call x1, Pallas kernels, staged(): pl.pallas_call(functools.partial(stage_kernel, counts), out_shape=(*(VMEM...  3.58 us
    pallas_call x2, Pallas kernels, flushed(): pl.pallas_call(functools.partial(flush_kernel, n, column, groups), out_sh...  2.17 us
  transfers between devices with their start and end apart: 19, of which 8 were waited for; matrix products, arithmetic and copies ran while one was open for 0% of the time, Pallas kernels for 11%

profile of v8, /device:TPU:11, one launch (start us, length us, event | category | flops | bytes accessed | tf_op | source)
XLA Modules:
  0.0 51.1 jit_solution(8163665357686119403)
XLA Ops:
  0.6 0.3 collective-permute-start.1
  1.0 1.0 %collective-permute-start = (bf16[512,256]{1,0:T(8,128)(2,1)}, bf16[512,256]{1,0:T(8,128)(2,1)S(1)}, u32[]{:S(2)}, u32[]{:S(2)}) collective-permute-start(bf16[512,256]{1,0:T(8,128)(2,1)} %refs_0_.1), channel_id=1, source_target_pairs={{0,1},{1,0},{2,3},{3,2},{4,5},{5,4},{6,7},{7,6},{8,9},{9,8},{10,11... | collective-permute-start | bytes 786440 | tf_op jit(solution)/shard_map/ppermute | solution.py:24
  1.9 0.0 copy-start
  1.9 3.6 %stage.1 = (bf16[18944,128]{1,0:T(8,128)(2,1)S(1)}, bf16[2560,768]{1,0:T(8,128)(2,1)S(1)}, f32[8,128]{1,0:T(8,128)S(1)}) custom-call(bf16[12288,128]{1,0:T(8,128)(2,1)} %bitcast.8, bf16[2048,128]{1,0:T(8,128)(2,1)} %bitcast.10, bf16[4096,128]{1,0:T(8,128)(2,1)} %bitcast.9, bf16[512,128]{1,0:T(8,128)(2,1)} %bitcast.11, bf16[2048,768]{1,0:T(8,128)(2,1)} %refs_4_.1, ...), custom_call_target="tpu_custom_call" | custom-call | bytes 17563648 | tf_op jit(solution)/shard_map/stage/pallas_call | solution.py:66
  5.5 2.6 %collective-permute-done.1.refs_2_ = bf16[512,256]{1,0:T(8,128)(2,1)S(1)} collective-permute-done((bf16[512,256]{1,0:T(8,128)(2,1)}, bf16[512,256]{1,0:T(8,128)(2,1)S(1)}, u32[]{:S(2)}, u32[]{:S(2)}) %collective-permute-start.1) | collective-permute-done | bytes 262176 | tf_op jit(solution)/shard_map/ppermute | solution.py:24
  8.1 1.5 %collective-permute-start.2 = (bf16[512,256]{1,0:T(8,128)(2,1)S(1)}, bf16[512,256]{1,0:T(8,128)(2,1)S(1)}, u32[]{:S(2)}, u32[]{:S(2)}) collective-permute-start(bf16[512,256]{1,0:T(8,128)(2,1)S(1)} %collective-permute-done.1.refs_2_), channel_id=1, source_target_pairs={{0,1},{1,0},{2,3},{3,2},{4,5},{5,4},{6,7},{7,6},{8,9},{9,8},{10,11... | collective-permute-start | bytes 786440 | tf_op jit(solution)/shard_map/ppermute | solution.py:24
  9.6 0.0 collective-permute-done.refs_1_
  9.6 1.2 %collective-permute-done.2.refs_3_ = bf16[512,256]{1,0:T(8,128)(2,1)S(1)} collective-permute-done((bf16[512,256]{1,0:T(8,128)(2,1)S(1)}, bf16[512,256]{1,0:T(8,128)(2,1)S(1)}, u32[]{:S(2)}, u32[]{:S(2)}) %collective-permute-start.2) | collective-permute-done | bytes 262176 | tf_op jit(solution)/shard_map/ppermute | solution.py:24
  10.8 0.0 copy-done
  10.8 0.0 copy-done.1
  10.8 0.0 copy-done.2
  10.8 2.2 %group_0.1 = (bf16[2048,256]{1,0:T(8,128)(2,1)S(1)}, bf16[256,256]{1,0:T(8,128)(2,1)S(1)}, bf16[256,256]{1,0:T(8,128)(2,1)S(1)}) custom-call(bf16[512,256]{1,0:T(8,128)(2,1)S(1)} %copy-done, bf16[512,256]{1,0:T(8,128)(2,1)S(1)} %collective-permute-done.refs_1_, bf16[512,256]{1,0:T(8,128)(2,1)S(1)} %collective-permute-done.1.refs_2_, ...), custom_call_target="tpu_custom_call" | custom-call | flops 1241513984 | bytes 6946816 | tf_op jit(solution)/shard_map/group_0/pallas_call | solution.py:229
  13.0 1.3 %collective-permute-start.3 = (bf16[256,256]{1,0:T(8,128)(2,1)S(1)}, bf16[256,256]{1,0:T(8,128)(2,1)S(1)}, u32[]{:S(2)}, u32[]{:S(2)}) collective-permute-start(bf16[256,256]{1,0:T(8,128)(2,1)S(1)} %get-tuple-element.25.refs_1_), channel_id=1, source_target_pairs={{0,4},{1,5},{2,6},{3,7},{4,8},{5,9},{6,10},{7,11},{8,12},{9,13},{1... | collective-permute-start | bytes 393224 | tf_op jit(solution)/shard_map/ppermute | solution.py:24
  14.3 1.2 %collective-permute-start.4 = (bf16[256,256]{1,0:T(8,128)(2,1)S(1)}, bf16[256,256]{1,0:T(8,128)(2,1)S(1)}, u32[]{:S(2)}, u32[]{:S(2)}) collective-permute-start(bf16[256,256]{1,0:T(8,128)(2,1)S(1)} %get-tuple-element.26.refs_2_), channel_id=1, source_target_pairs={{0,4},{1,5},{2,6},{3,7},{4,8},{5,9},{6,10},{7,11},{8,12},{9,13},{1... | collective-permute-start | bytes 393224 | tf_op jit(solution)/shard_map/ppermute | solution.py:24
  15.5 3.1 %collective-permute-done.3.refs_0_ = bf16[256,256]{1,0:T(8,128)(2,1)S(1)} collective-permute-done((bf16[256,256]{1,0:T(8,128)(2,1)S(1)}, bf16[256,256]{1,0:T(8,128)(2,1)S(1)}, u32[]{:S(2)}, u32[]{:S(2)}) %collective-permute-start.3) | collective-permute-done | bytes 131104 | tf_op jit(solution)/shard_map/ppermute | solution.py:24
  18.6 0.3 collective-permute-start.7
  18.9 2.5 %collective-permute-done.4.refs_1_ = bf16[256,256]{1,0:T(8,128)(2,1)S(1)} collective-permute-done((bf16[256,256]{1,0:T(8,128)(2,1)S(1)}, bf16[256,256]{1,0:T(8,128)(2,1)S(1)}, u32[]{:S(2)}, u32[]{:S(2)}) %collective-permute-start.4) | collective-permute-done | bytes 131104 | tf_op jit(solution)/shard_map/ppermute | solution.py:24
  21.5 0.3 collective-permute-start.8
  21.7 1.5 %collective-permute-start.5 = (bf16[256,256]{1,0:T(8,128)(2,1)S(1)}, bf16[256,256]{1,0:T(8,128)(2,1)S(1)}, u32[]{:S(2)}, u32[]{:S(2)}) collective-permute-start(bf16[256,256]{1,0:T(8,128)(2,1)S(1)} %collective-permute-done.3.refs_0_), channel_id=1, source_target_pairs={{0,1},{1,0},{2,3},{3,2},{4,5},{5,4},{6,7},{7,6},{8,9},{9,8},{10,11... | collective-permute-start | bytes 393224 | tf_op jit(solution)/shard_map/ppermute | solution.py:24
  23.2 0.0 collective-permute-start.6
  23.2 0.0 collective-permute-done.7.refs_4_
  23.2 3.5 %collective-permute-start.9 = (bf16[256,256]{1,0:T(8,128)(2,1)S(1)}, bf16[256,256]{1,0:T(8,128)(2,1)S(1)}, u32[]{:S(2)}, u32[]{:S(2)}) collective-permute-start(bf16[256,256]{1,0:T(8,128)(2,1)S(1)} %collective-permute-done.7.refs_4_), channel_id=1, source_target_pairs={{0,1},{1,0},{2,3},{3,2},{4,5},{5,4},{6,7},{7,6},{8,9},{9,8},{10,11... | collective-permute-start | bytes 393224 | tf_op jit(solution)/shard_map/ppermute | solution.py:24
  26.7 0.3 collective-permute-done.8.refs_5_
  27.0 1.5 %collective-permute-start.10 = (bf16[256,256]{1,0:T(8,128)(2,1)S(1)}, bf16[256,256]{1,0:T(8,128)(2,1)S(1)}, u32[]{:S(2)}, u32[]{:S(2)}) collective-permute-start(bf16[256,256]{1,0:T(8,128)(2,1)S(1)} %collective-permute-done.8.refs_5_), channel_id=1, source_target_pairs={{0,1},{1,0},{2,3},{3,2},{4,5},{5,4},{6,7},{7,6},{8,9},{9,8},{10,11... | collective-permute-start | bytes 393224 | tf_op jit(solution)/shard_map/ppermute | solution.py:24
  28.4 1.1 %flush_0.1 = (bf16[2048,768]{1,0:T(8,128)(2,1)}, bf16[512,768]{1,0:T(8,128)(2,1)}, bf16[2048,256]{1,0:T(8,128)(2,1)S(1)}, bf16[256,256]{1,0:T(8,128)(2,1)S(1)}, bf16[256,256]{1,0:T(8,128)(2,1)S(1)}) custom-call(bf16[2048,256]{1,0:T(8,128)(2,1)S(1)} %get-tuple-element.27.refs_0_, bf16[256,256]{1,0:T(8,128)(2,1)S(1)} %get-tuple-element.25.refs_1_, ...), custom_call_target="tpu_custom_call" | custom-call | bytes 2621440 | tf_op jit(solution)/shard_map/flush_0/pallas_call | solution.py:298
  29.5 0.0 collective-permute-done.5.refs_2_
  29.5 0.0 collective-permute-done.6.refs_3_
  29.5 0.0 collective-permute-done.9.refs_6_
  29.6 0.0 collective-permute-done.10.refs_7_
  29.6 2.2 %group_1.1 = (bf16[2048,256]{1,0:T(8,128)(2,1)S(1)}, bf16[256,256]{1,0:T(8,128)(2,1)S(1)}, bf16[256,256]{1,0:T(8,128)(2,1)S(1)}) custom-call(bf16[256,256]{1,0:T(8,128)(2,1)S(1)} %collective-permute-done.3.refs_0_, bf16[256,256]{1,0:T(8,128)(2,1)S(1)} %collective-permute-done.4.refs_1_, ...), custom_call_target="tpu_custom_call", output_to_operand_aliasing={{0}: (12, {}), {1}: (13, {}), {2}: (14, {})} | custom-call | flops 1241513984 | bytes 6946816 | tf_op jit(solution)/shard_map/group_1/pallas_call | solution.py:229
  31.8 0.4 collective-permute-start.11
  32.2 2.1 %collective-permute-start.12 = (bf16[256,256]{1,0:T(8,128)(2,1)S(1)}, bf16[256,256]{1,0:T(8,128)(2,1)S(1)}, u32[]{:S(2)}, u32[]{:S(2)}) collective-permute-start(bf16[256,256]{1,0:T(8,128)(2,1)S(1)} %get-tuple-element.32.refs_2_), channel_id=1, source_target_pairs={{0,4},{1,5},{2,6},{3,7},{4,8},{5,9},{6,10},{7,11},{8,12},{9,13},{1... | collective-permute-start | bytes 393224 | tf_op jit(solution)/shard_map/ppermute | solution.py:24
  34.3 3.3 %collective-permute-done.11.refs_0_ = bf16[256,256]{1,0:T(8,128)(2,1)S(1)} collective-permute-done((bf16[256,256]{1,0:T(8,128)(2,1)S(1)}, bf16[256,256]{1,0:T(8,128)(2,1)S(1)}, u32[]{:S(2)}, u32[]{:S(2)}) %collective-permute-start.11) | collective-permute-done | bytes 131104 | tf_op jit(solution)/shard_map/ppermute | solution.py:24
  37.6 0.2 collective-permute-start.15
  37.9 2.6 %collective-permute-done.12.refs_1_ = bf16[256,256]{1,0:T(8,128)(2,1)S(1)} collective-permute-done((bf16[256,256]{1,0:T(8,128)(2,1)S(1)}, bf16[256,256]{1,0:T(8,128)(2,1)S(1)}, u32[]{:S(2)}, u32[]{:S(2)}) %collective-permute-start.12) | collective-permute-done | bytes 131104 | tf_op jit(solution)/shard_map/ppermute | solution.py:24
  40.4 0.2 collective-permute-start.16
  40.7 1.3 %collective-permute-start.13 = (bf16[256,256]{1,0:T(8,128)(2,1)S(1)}, bf16[256,256]{1,0:T(8,128)(2,1)S(1)}, u32[]{:S(2)}, u32[]{:S(2)}) collective-permute-start(bf16[256,256]{1,0:T(8,128)(2,1)S(1)} %collective-permute-done.11.refs_0_), channel_id=1, source_target_pairs={{0,1},{1,0},{2,3},{3,2},{4,5},{5,4},{6,7},{7,6},{8,9},{9,8},{10,11... | collective-permute-start | bytes 393224 | tf_op jit(solution)/shard_map/ppermute | solution.py:24
  42.0 0.0 collective-permute-start.14
  42.0 0.0 collective-permute-done.15.refs_4_
  42.0 3.0 %collective-permute-start.17 = (bf16[256,256]{1,0:T(8,128)(2,1)S(1)}, bf16[256,256]{1,0:T(8,128)(2,1)S(1)}, u32[]{:S(2)}, u32[]{:S(2)}) collective-permute-start(bf16[256,256]{1,0:T(8,128)(2,1)S(1)} %collective-permute-done.15.refs_4_), channel_id=1, source_target_pairs={{0,1},{1,0},{2,3},{3,2},{4,5},{5,4},{6,7},{7,6},{8,9},{9,8},{10,11... | collective-permute-start | bytes 393224 | tf_op jit(solution)/shard_map/ppermute | solution.py:24
  45.0 0.8 %collective-permute-done.16.refs_5_ = bf16[256,256]{1,0:T(8,128)(2,1)S(1)} collective-permute-done((bf16[256,256]{1,0:T(8,128)(2,1)S(1)}, bf16[256,256]{1,0:T(8,128)(2,1)S(1)}, u32[]{:S(2)}, u32[]{:S(2)}) %collective-permute-start.16) | collective-permute-done | bytes 131104 | tf_op jit(solution)/shard_map/ppermute | solution.py:24
  45.8 1.3 %collective-permute-start.18 = (bf16[256,256]{1,0:T(8,128)(2,1)S(1)}, bf16[256,256]{1,0:T(8,128)(2,1)S(1)}, u32[]{:S(2)}, u32[]{:S(2)}) collective-permute-start(bf16[256,256]{1,0:T(8,128)(2,1)S(1)} %collective-permute-done.16.refs_5_), channel_id=1, source_target_pairs={{0,1},{1,0},{2,3},{3,2},{4,5},{5,4},{6,7},{7,6},{8,9},{9,8},{10,11... | collective-permute-start | bytes 393224 | tf_op jit(solution)/shard_map/ppermute | solution.py:24
  47.1 1.1 %flush_1.1 = (bf16[2048,768]{1,0:T(8,128)(2,1)}, bf16[512,768]{1,0:T(8,128)(2,1)}) custom-call(bf16[2048,256]{1,0:T(8,128)(2,1)S(1)} %get-tuple-element.33.refs_0_, bf16[256,256]{1,0:T(8,128)(2,1)S(1)} %get-tuple-element.31.refs_1_, bf16[256,256]{1,0:T(8,128)(2,1)S(1)} %get-tuple-element.32.refs_2_, ...), custom_call_target="tpu_custom_call", output_to_operand_aliasing={{0}: (6, {}), {1}: (7, {})} | custom-call | bytes 2621440 | tf_op jit(solution)/shard_map/flush_1/pallas_call | solution.py:298
  48.2 0.0 collective-permute-done.13.refs_2_
  48.2 0.0 collective-permute-done.14.refs_3_
  48.2 0.0 collective-permute-done.17.refs_6_
  48.2 0.0 collective-permute-done.18.refs_7_
  48.2 2.9 %group_2.1 = (bf16[2048,768]{1,0:T(8,128)(2,1)}, bf16[512,768]{1,0:T(8,128)(2,1)}) custom-call(bf16[256,256]{1,0:T(8,128)(2,1)S(1)} %collective-permute-done.11.refs_0_, bf16[256,256]{1,0:T(8,128)(2,1)S(1)} %collective-permute-done.12.refs_1_, bf16[256,256]{1,0:T(8,128)(2,1)S(1)} %collective-permute-done.13.refs_2_, ...), custom_call_target="tpu_custom_call", output_to_operand_aliasing={{0}: (12, {}), {1}: (13, {})} | custom-call | flops 1241513984 | bytes 6946816 | tf_op jit(solution)/shard_map/group_2/pallas_call | solution.py:229
  (2 shorter events, 0.0 us)
Async XLA Ops:
  0.6 7.5 %collective-permute-start.1 = (bf16[512,256]{1,0:T(8,128)(2,1)}, bf16[512,256]{1,0:T(8,128)(2,1)S(1)}, u32[]{:S(2)}, u32[]{:S(2)}) collective-permute-start(bf16[512,256]{1,0:T(8,128)(2,1)} %refs_0_.1), channel_id=1, source_target_pairs={{0,2},{1,3},{2,0},{3,1},{4,6},{5,7},{6,4},{7,5},{8,10},{9,11},{10,... | collective-permute-start | bytes 786440 | tf_op jit(solution)/shard_map/ppermute | solution.py:24
  1.0 8.7 %collective-permute-start = (bf16[512,256]{1,0:T(8,128)(2,1)}, bf16[512,256]{1,0:T(8,128)(2,1)S(1)}, u32[]{:S(2)}, u32[]{:S(2)}) collective-permute-start(bf16[512,256]{1,0:T(8,128)(2,1)} %refs_0_.1), channel_id=1, source_target_pairs={{0,1},{1,0},{2,3},{3,2},{4,5},{5,4},{6,7},{7,6},{8,9},{9,8},{10,11... | collective-permute-start | bytes 786440 | tf_op jit(solution)/shard_map/ppermute | solution.py:24
  1.9 8.9 %copy-start = (bf16[512,256]{1,0:T(8,128)(2,1)S(1)}, bf16[512,256]{1,0:T(8,128)(2,1)}, u32[]{:S(2)}) copy-start(bf16[512,256]{1,0:T(8,128)(2,1)} %refs_0_.1) | copy-start | bytes 786436
  1.9 8.9 %copy-start.1 = (s32[4,8]{1,0:T(4,128)S(1)}, s32[4,8]{1,0:T(4,128)}, u32[]{:S(2)}) copy-start(s32[4,8]{1,0:T(4,128)} %refs_9_.3) | copy-start | bytes 388
  1.9 8.9 %copy-start.2 = (s32[16,6]{0,1:T(8,128)S(1)}, s32[16,6]{0,1:T(8,128)}, u32[]{:S(2)}) copy-start(s32[16,6]{0,1:T(8,128)} %param.12) | copy-start | bytes 1156
  8.1 2.7 %collective-permute-start.2 = (bf16[512,256]{1,0:T(8,128)(2,1)S(1)}, bf16[512,256]{1,0:T(8,128)(2,1)S(1)}, u32[]{:S(2)}, u32[]{:S(2)}) collective-permute-start(bf16[512,256]{1,0:T(8,128)(2,1)S(1)} %collective-permute-done.1.refs_2_), channel_id=1, source_target_pairs={{0,1},{1,0},{2,3},{3,2},{4,5},{5,4},{6,7},{7,6},{8,9},{9,8},{10,11... | collective-permute-start | bytes 786440 | tf_op jit(solution)/shard_map/ppermute | solution.py:24
  13.0 5.7 %collective-permute-start.3 = (bf16[256,256]{1,0:T(8,128)(2,1)S(1)}, bf16[256,256]{1,0:T(8,128)(2,1)S(1)}, u32[]{:S(2)}, u32[]{:S(2)}) collective-permute-start(bf16[256,256]{1,0:T(8,128)(2,1)S(1)} %get-tuple-element.25.refs_1_), channel_id=1, source_target_pairs={{0,4},{1,5},{2,6},{3,7},{4,8},{5,9},{6,10},{7,11},{8,12},{9,13},{1... | collective-permute-start | bytes 393224 | tf_op jit(solution)/shard_map/ppermute | solution.py:24
  14.3 7.2 %collective-permute-start.4 = (bf16[256,256]{1,0:T(8,128)(2,1)S(1)}, bf16[256,256]{1,0:T(8,128)(2,1)S(1)}, u32[]{:S(2)}, u32[]{:S(2)}) collective-permute-start(bf16[256,256]{1,0:T(8,128)(2,1)S(1)} %get-tuple-element.26.refs_2_), channel_id=1, source_target_pairs={{0,4},{1,5},{2,6},{3,7},{4,8},{5,9},{6,10},{7,11},{8,12},{9,13},{1... | collective-permute-start | bytes 393224 | tf_op jit(solution)/shard_map/ppermute | solution.py:24
  18.6 4.6 %collective-permute-start.7 = (bf16[256,256]{1,0:T(8,128)(2,1)S(1)}, bf16[256,256]{1,0:T(8,128)(2,1)S(1)}, u32[]{:S(2)}, u32[]{:S(2)}) collective-permute-start(bf16[256,256]{1,0:T(8,128)(2,1)S(1)} %collective-permute-done.3.refs_0_), channel_id=1, source_target_pairs={{0,2},{1,3},{2,0},{3,1},{4,6},{5,7},{6,4},{7,5},{8,10},{9,11},{10,... | collective-permute-start | bytes 393224 | tf_op jit(solution)/shard_map/ppermute | solution.py:24
  21.5 5.5 %collective-permute-start.8 = (bf16[256,256]{1,0:T(8,128)(2,1)S(1)}, bf16[256,256]{1,0:T(8,128)(2,1)S(1)}, u32[]{:S(2)}, u32[]{:S(2)}) collective-permute-start(bf16[256,256]{1,0:T(8,128)(2,1)S(1)} %collective-permute-done.4.refs_1_), channel_id=1, source_target_pairs={{0,2},{1,3},{2,0},{3,1},{4,6},{5,7},{6,4},{7,5},{8,10},{9,11},{10,... | collective-permute-start | bytes 393224 | tf_op jit(solution)/shard_map/ppermute | solution.py:24
  21.7 7.8 %collective-permute-start.5 = (bf16[256,256]{1,0:T(8,128)(2,1)S(1)}, bf16[256,256]{1,0:T(8,128)(2,1)S(1)}, u32[]{:S(2)}, u32[]{:S(2)}) collective-permute-start(bf16[256,256]{1,0:T(8,128)(2,1)S(1)} %collective-permute-done.3.refs_0_), channel_id=1, source_target_pairs={{0,1},{1,0},{2,3},{3,2},{4,5},{5,4},{6,7},{7,6},{8,9},{9,8},{10,11... | collective-permute-start | bytes 393224 | tf_op jit(solution)/shard_map/ppermute | solution.py:24
  23.2 6.3 %collective-permute-start.6 = (bf16[256,256]{1,0:T(8,128)(2,1)S(1)}, bf16[256,256]{1,0:T(8,128)(2,1)S(1)}, u32[]{:S(2)}, u32[]{:S(2)}) collective-permute-start(bf16[256,256]{1,0:T(8,128)(2,1)S(1)} %collective-permute-done.4.refs_1_), channel_id=1, source_target_pairs={{0,1},{1,0},{2,3},{3,2},{4,5},{5,4},{6,7},{7,6},{8,9},{9,8},{10,11... | collective-permute-start | bytes 393224 | tf_op jit(solution)/shard_map/ppermute | solution.py:24
  23.2 6.3 %collective-permute-start.9 = (bf16[256,256]{1,0:T(8,128)(2,1)S(1)}, bf16[256,256]{1,0:T(8,128)(2,1)S(1)}, u32[]{:S(2)}, u32[]{:S(2)}) collective-permute-start(bf16[256,256]{1,0:T(8,128)(2,1)S(1)} %collective-permute-done.7.refs_4_), channel_id=1, source_target_pairs={{0,1},{1,0},{2,3},{3,2},{4,5},{5,4},{6,7},{7,6},{8,9},{9,8},{10,11... | collective-permute-start | bytes 393224 | tf_op jit(solution)/shard_map/ppermute | solution.py:24
  27.0 2.6 %collective-permute-start.10 = (bf16[256,256]{1,0:T(8,128)(2,1)S(1)}, bf16[256,256]{1,0:T(8,128)(2,1)S(1)}, u32[]{:S(2)}, u32[]{:S(2)}) collective-permute-start(bf16[256,256]{1,0:T(8,128)(2,1)S(1)} %collective-permute-done.8.refs_5_), channel_id=1, source_target_pairs={{0,1},{1,0},{2,3},{3,2},{4,5},{5,4},{6,7},{7,6},{8,9},{9,8},{10,11... | collective-permute-start | bytes 393224 | tf_op jit(solution)/shard_map/ppermute | solution.py:24
  31.8 5.8 %collective-permute-start.11 = (bf16[256,256]{1,0:T(8,128)(2,1)S(1)}, bf16[256,256]{1,0:T(8,128)(2,1)S(1)}, u32[]{:S(2)}, u32[]{:S(2)}) collective-permute-start(bf16[256,256]{1,0:T(8,128)(2,1)S(1)} %get-tuple-element.31.refs_1_), channel_id=1, source_target_pairs={{0,4},{1,5},{2,6},{3,7},{4,8},{5,9},{6,10},{7,11},{8,12},{9,13},{1... | collective-permute-start | bytes 393224 | tf_op jit(solution)/shard_map/ppermute | solution.py:24
  32.2 8.3 %collective-permute-start.12 = (bf16[256,256]{1,0:T(8,128)(2,1)S(1)}, bf16[256,256]{1,0:T(8,128)(2,1)S(1)}, u32[]{:S(2)}, u32[]{:S(2)}) collective-permute-start(bf16[256,256]{1,0:T(8,128)(2,1)S(1)} %get-tuple-element.32.refs_2_), channel_id=1, source_target_pairs={{0,4},{1,5},{2,6},{3,7},{4,8},{5,9},{6,10},{7,11},{8,12},{9,13},{1... | collective-permute-start | bytes 393224 | tf_op jit(solution)/shard_map/ppermute | solution.py:24
  37.6 4.4 %collective-permute-start.15 = (bf16[256,256]{1,0:T(8,128)(2,1)S(1)}, bf16[256,256]{1,0:T(8,128)(2,1)S(1)}, u32[]{:S(2)}, u32[]{:S(2)}) collective-permute-start(bf16[256,256]{1,0:T(8,128)(2,1)S(1)} %collective-permute-done.11.refs_0_), channel_id=1, source_target_pairs={{0,2},{1,3},{2,0},{3,1},{4,6},{5,7},{6,4},{7,5},{8,10},{9,11},{10,... | collective-permute-start | bytes 393224 | tf_op jit(solution)/shard_map/ppermute | solution.py:24
  40.4 5.4 %collective-permute-start.16 = (bf16[256,256]{1,0:T(8,128)(2,1)S(1)}, bf16[256,256]{1,0:T(8,128)(2,1)S(1)}, u32[]{:S(2)}, u32[]{:S(2)}) collective-permute-start(bf16[256,256]{1,0:T(8,128)(2,1)S(1)} %collective-permute-done.12.refs_1_), channel_id=1, source_target_pairs={{0,2},{1,3},{2,0},{3,1},{4,6},{5,7},{6,4},{7,5},{8,10},{9,11},{10,... | collective-permute-start | bytes 393224 | tf_op jit(solution)/shard_map/ppermute | solution.py:24
  40.7 7.5 %collective-permute-start.13 = (bf16[256,256]{1,0:T(8,128)(2,1)S(1)}, bf16[256,256]{1,0:T(8,128)(2,1)S(1)}, u32[]{:S(2)}, u32[]{:S(2)}) collective-permute-start(bf16[256,256]{1,0:T(8,128)(2,1)S(1)} %collective-permute-done.11.refs_0_), channel_id=1, source_target_pairs={{0,1},{1,0},{2,3},{3,2},{4,5},{5,4},{6,7},{7,6},{8,9},{9,8},{10,11... | collective-permute-start | bytes 393224 | tf_op jit(solution)/shard_map/ppermute | solution.py:24
  42.0 6.2 %collective-permute-start.14 = (bf16[256,256]{1,0:T(8,128)(2,1)S(1)}, bf16[256,256]{1,0:T(8,128)(2,1)S(1)}, u32[]{:S(2)}, u32[]{:S(2)}) collective-permute-start(bf16[256,256]{1,0:T(8,128)(2,1)S(1)} %collective-permute-done.12.refs_1_), channel_id=1, source_target_pairs={{0,1},{1,0},{2,3},{3,2},{4,5},{5,4},{6,7},{7,6},{8,9},{9,8},{10,11... | collective-permute-start | bytes 393224 | tf_op jit(solution)/shard_map/ppermute | solution.py:24
  42.0 6.2 %collective-permute-start.17 = (bf16[256,256]{1,0:T(8,128)(2,1)S(1)}, bf16[256,256]{1,0:T(8,128)(2,1)S(1)}, u32[]{:S(2)}, u32[]{:S(2)}) collective-permute-start(bf16[256,256]{1,0:T(8,128)(2,1)S(1)} %collective-permute-done.15.refs_4_), channel_id=1, source_target_pairs={{0,1},{1,0},{2,3},{3,2},{4,5},{5,4},{6,7},{7,6},{8,9},{9,8},{10,11... | collective-permute-start | bytes 393224 | tf_op jit(solution)/shard_map/ppermute | solution.py:24
  45.8 2.4 %collective-permute-start.18 = (bf16[256,256]{1,0:T(8,128)(2,1)S(1)}, bf16[256,256]{1,0:T(8,128)(2,1)S(1)}, u32[]{:S(2)}, u32[]{:S(2)}) collective-permute-start(bf16[256,256]{1,0:T(8,128)(2,1)S(1)} %collective-permute-done.16.refs_5_), channel_id=1, source_target_pairs={{0,1},{1,0},{2,3},{3,2},{4,5},{5,4},{6,7},{7,6},{8,9},{9,8},{10,11... | collective-permute-start | bytes 393224 | tf_op jit(solution)/shard_map/ppermute | solution.py:24
